TPU v7x, 32 devices: a whole 2x2x4 slice. The times are simulated.
32 devices in a mesh: tm: 4 (over y, x), cells: 8 (over z, core).
Axes of the slice: x: 2, y: 2, z: 4, core: 2. Of those that a mesh axis runs over, the one named last changes fastest.
Arguments:
- footprint: float32 [4, 4, 768, 8192], P('tm', None, None, 'cells'), may hold values from -0.03125 to 0.03125
- flux: float32 [4, 8192, 2048], P('tm', 'cells'), may hold values from -6 to 6
- obs_weight: float32 [4, 768], P('tm'), may hold values from 0.2 to 5
- obs_count: int32 [4], P('tm'), may hold values from 1 to 768, 2304 in all
Outputs:
- normal_image: float32 [4, 8192, 2048], P('tm', 'cells')
Inputs may be any that keep to these rules, and one draw needn't show every extreme that they name: `obs_count`: each block has at least one valid slot; one block has all 768 slots valid.
All inputs are finite; a program needn't handle non-finite values.
Results may differ from a plain program's by a relative error of at most 0.0001.
Values sent between devices are 32-bit elements; how exact they have to be, the bound alone decides.
No kernel may reach another device: no remote copies, remote signals or barrier semaphores. Data moves between devices by JAX's collectives and lax.ppermute only.
A program may use at most 128 MiB of HBM per device.

v0:
```python
import functools

import jax
import jax.numpy as jnp
from jax import lax
from jax.experimental import pallas as pl
from jax.experimental.pallas import tpu as pltpu
from jax.sharding import Mesh, PartitionSpec as P

CHUNKS = 4
TILE = 256
WIDE = 512
LIGHT = pl.CostEstimate(flops=1, bytes_accessed=1, transcendentals=0)
IN_PLACE = pl.BlockSpec(memory_space=pl.ANY)
VMEM_LIMIT = 60 * 1024 * 1024


def shifted(value, by):
    devices = lax.axis_size("tm")
    pairs = [(i, i + by) for i in range(devices) if 0 <= i + by < devices]
    return lax.ppermute(value, "tm", pairs)


def cycled(value, by):
    devices = lax.axis_size("tm")
    return lax.ppermute(value, "tm", [(i, (i - by) % devices) for i in range(devices)])


def swapped(value):
    return lax.ppermute(value, "core", [(0, 1), (1, 0)])


def together(first, second):
    return lax.optimization_barrier((first, second))


def halves(value):
    high = value.astype(jnp.bfloat16)
    low = (value - high.astype(jnp.float32)).astype(jnp.bfloat16)
    return high, low


def times(left, right, dims):
    return lax.dot_general(left, right, (dims, ((), ())), preferred_element_type=jnp.float32)


def split_kernel(core_ref, own, other, high_ref, low_ref):
    cells = other.shape[0]
    for at, value in ((0, own[0]), (cells, other[...])):
        high, low = halves(value)
        high_ref[pl.ds(at, cells), :] = high
        low_ref[pl.ds(at, cells), :] = low


def split(flux, flux_other, core):
    cells, half = flux_other.shape
    tile = min(TILE, half)
    steps = half // tile
    block = pl.BlockSpec((2 * cells, tile), lambda j, c: (0, j))
    return list(pl.pallas_call(
        split_kernel,
        grid_spec=pltpu.PrefetchScalarGridSpec(
            num_scalar_prefetch=1,
            grid=(steps,),
            in_specs=[
                pl.BlockSpec((1, cells, tile), lambda j, c: (0, 0, c[0] * steps + j)),
                pl.BlockSpec((cells, tile), lambda j, c: (0, j)),
            ],
            out_specs=[block, block],
        ),
        out_shape=[jax.ShapeDtypeStruct((2 * cells, half), jnp.bfloat16)] * 2,
        name="split",
        cost_estimate=LIGHT,
    )(core, flux, flux_other))


def forward_kernel(count, *refs):
    foot_own, foot_other = refs[:count], refs[count:2 * count]
    flux_high, flux_low = refs[2 * count:2 * count + 2]
    outs = refs[2 * count + 2:3 * count + 2]
    parts_ref = refs[-1]
    rows, cells = foot_own[0].shape[-2:]
    depth = count * rows

    @pl.when(pl.program_id(0) == 0)
    def _():
        for i in range(count):
            for side, source in ((0, foot_own[i]), (1, foot_other[i])):
                high, low = halves(source[...].reshape(rows, cells))
                columns = pl.ds(side * cells, cells)
                parts_ref[pl.ds(i * rows, rows), columns] = high
                parts_ref[pl.ds(depth + i * rows, rows), columns] = low

    dims = ((1,), (0,))
    both = times(parts_ref[...], flux_high[...], dims)
    total = both[:depth] + both[depth:] + times(parts_ref[pl.ds(0, depth), :], flux_low[...], dims)
    for i in range(count):
        outs[i][...] = total[i * rows:(i + 1) * rows]


def forward(foot_own, own_specs, foot_other, other_specs, rows, flux_parts):
    count = len(foot_own)
    depth, half = flux_parts[0].shape
    tile = min(WIDE, half)
    outs = pl.pallas_call(
        functools.partial(forward_kernel, count),
        grid=(half // tile,),
        in_specs=[
            *own_specs,
            *other_specs,
            *[pl.BlockSpec((depth, tile), lambda j: (0, j))] * 2,
        ],
        out_specs=[pl.BlockSpec((rows, tile), lambda j: (0, j))] * count,
        scratch_shapes=[pltpu.VMEM((2 * count * rows, depth), jnp.bfloat16)],
        out_shape=[jax.ShapeDtypeStruct((rows, half), jnp.float32)] * count,
        compiler_params=pltpu.CompilerParams(vmem_limit_bytes=VMEM_LIMIT),
        name="forward",
        cost_estimate=LIGHT,
    )(*foot_own, *foot_other, *flux_parts)
    return list(outs)


def adjoint_kernel(count, sides, first, place_ref, *refs):
    weighted, refs = refs[:count], refs[count:]
    foot, refs = refs[:sides * count], refs[sides * count:]
    before, refs = (None, refs) if first else (refs[:sides], refs[sides:])
    outs, (high_ref, low_ref) = refs[:sides], refs[sides:]
    rows, tile = foot[0].shape[-2:]

    @pl.when(pl.program_id(0) == 0)
    def _():
        for i in range(count):
            value = jnp.where(place_ref[1] + i < place_ref[2], weighted[i][...], 0.0)
            high, low = halves(value)
            high_ref[pl.ds(i * rows, rows), :] = high
            low_ref[pl.ds(i * rows, rows), :] = low

    dims = ((1,), (0,))
    for side in range(sides):
        mine = foot[side * count:(side + 1) * count]
        slab = jnp.concatenate([ref[...].reshape(rows, tile) for ref in mine], axis=0)
        high, low = halves(slab.T)
        both = times(jnp.concatenate([high, low], axis=0), high_ref[...], dims)
        total = both[:tile] + both[tile:] + times(high, low_ref[...], dims)
        if not first:
            total = total + before[side][...]
        outs[side][...] = total


def adjoint(weighted, sides, core, cells):
    count = len(weighted)
    rows, half = weighted[0].shape
    tile = min(WIDE, cells)
    first = sides[0][2] is None
    out_specs = []
    for side in sides:
        if side[4]:
            out_specs.append(pl.BlockSpec((tile, half), lambda j, c: (j, c[0])))
        else:
            out_specs.append(pl.BlockSpec((tile, half), lambda j, c: (j, 0)))
    foot = [array for side in sides for array in side[0]]
    earlier = [] if first else [side[2] for side in sides]
    at = 1 + count + len(foot)
    return pl.pallas_call(
        functools.partial(adjoint_kernel, count, len(sides), first),
        grid_spec=pltpu.PrefetchScalarGridSpec(
            num_scalar_prefetch=1,
            grid=(cells // tile,),
            in_specs=[
                *[pl.BlockSpec((rows, half), lambda j, c: (0, 0))] * count,
                *[spec(tile) for side in sides for spec in side[1]],
                *([] if first else out_specs),
            ],
            out_specs=out_specs,
            scratch_shapes=[pltpu.VMEM((count * rows, half), jnp.bfloat16)] * 2,
        ),
        out_shape=[jax.ShapeDtypeStruct((cells, side[3]), jnp.float32) for side in sides],
        input_output_aliases={} if first else {at + i: i for i in range(len(sides))},
        compiler_params=pltpu.CompilerParams(vmem_limit_bytes=VMEM_LIMIT),
        name="adjoint",
        cost_estimate=LIGHT,
    )(core, *weighted, *foot, *earlier)


def run(copies):
    for copy in copies:
        copy.start()
    for copy in copies:
        copy.wait()


def cut_kernel(lags, r, footprint, *refs):
    outs, sems = refs[:-1], refs[-1]
    rows = outs[0].shape[0]
    run([
        pltpu.make_async_copy(footprint.at[0, lag, pl.ds(r * rows, rows), :], out, sems.at[i])
        for i, (lag, out) in enumerate(zip(lags, outs))
    ])


def cut(footprint, lags, rows, r):
    return list(pl.pallas_call(
        functools.partial(cut_kernel, lags, r),
        in_specs=[IN_PLACE],
        out_specs=[IN_PLACE] * len(lags),
        scratch_shapes=[pltpu.SemaphoreType.DMA((len(lags),))],
        out_shape=[jax.ShapeDtypeStruct((rows, footprint.shape[3]), jnp.float32)] * len(lags),
        name="cut",
        cost_estimate=LIGHT,
    )(footprint))


def stack_kernel(*refs):
    pieces, out, sems = refs[:-2], refs[-2], refs[-1]
    rows = pieces[0].shape[0]
    run([
        pltpu.make_async_copy(piece, out.at[pl.ds(i * rows, rows), :], sems.at[i])
        for i, piece in enumerate(pieces)
    ])


def stack(pieces):
    rows, cells = pieces[0].shape
    return pl.pallas_call(
        stack_kernel,
        in_specs=[IN_PLACE] * len(pieces),
        out_specs=IN_PLACE,
        scratch_shapes=[pltpu.SemaphoreType.DMA((len(pieces),))],
        out_shape=jax.ShapeDtypeStruct((rows * len(pieces), cells), jnp.float32),
        name="stack",
        cost_estimate=LIGHT,
    )(*pieces)


def side_kernel(core_ref, flux, out):
    out[...] = flux[0]


def side_of(flux, core):
    _, cells, width = flux.shape
    tile = min(TILE, width // 2)
    steps = width // 2 // tile
    return pl.pallas_call(
        side_kernel,
        grid_spec=pltpu.PrefetchScalarGridSpec(
            num_scalar_prefetch=1,
            grid=(steps,),
            in_specs=[pl.BlockSpec((1, cells, tile), lambda j, c: (0, 0, (1 - c[0]) * steps + j))],
            out_specs=pl.BlockSpec((cells, tile), lambda j, c: (0, j)),
        ),
        out_shape=jax.ShapeDtypeStruct((cells, width // 2), jnp.float32),
        name="side",
        cost_estimate=LIGHT,
    )(core, flux)


def combine_kernel(place_ref, scale, same, *refs):
    total = same[...]
    for lag, ref in enumerate(refs[:-1], 1):
        total = total + jnp.where(place_ref[1] >= lag, ref[...], 0.0)
    refs[-1][...] = scale[...] * total


def combine(scale, same, arrived, r, place):
    rows, half = same.shape
    tile = min(WIDE, half)
    block = pl.BlockSpec((rows, tile), lambda j, c: (0, j))
    return pl.pallas_call(
        combine_kernel,
        grid_spec=pltpu.PrefetchScalarGridSpec(
            num_scalar_prefetch=1,
            grid=(half // tile,),
            in_specs=[
                pl.BlockSpec((rows, 1), lambda j, c: (r, 0)),
                block,
                *[block] * len(arrived),
            ],
            out_specs=block,
        ),
        out_shape=jax.ShapeDtypeStruct((rows, half), jnp.float32),
        name="combine",
        cost_estimate=LIGHT,
    )(place, scale, same, *arrived)


def choose_kernel(r, place_ref, source, *refs):
    count = len(refs) // 2
    ups, outs, sems = refs[:count], refs[count:2 * count], refs[-1]
    rows = outs[0].shape[0]
    choices = []
    for i, (up, out) in enumerate(zip(ups, outs)):
        down = source if r is None else source.at[0, i + 1, pl.ds(r * rows, rows), :]
        below = place_ref[1] > i
        choices.append((below, pltpu.make_async_copy(down, out, sems.at[i])))
        choices.append((jnp.logical_not(below), pltpu.make_async_copy(up, out, sems.at[i])))
    for taken, copy in choices:
        pl.when(taken)(copy.start)
    for taken, copy in choices:
        pl.when(taken)(copy.wait)


def choose(place, source, r, up):
    rows, width = up[0].shape
    return list(pl.pallas_call(
        functools.partial(choose_kernel, r),
        in_specs=[pl.BlockSpec(memory_space=pltpu.SMEM)] + [IN_PLACE] * (1 + len(up)),
        out_specs=[IN_PLACE] * len(up),
        scratch_shapes=[pltpu.SemaphoreType.DMA((len(up),))],
        out_shape=[jax.ShapeDtypeStruct((rows, width), jnp.float32)] * len(up),
        name="choose",
        cost_estimate=LIGHT,
    )(place, source, *up))


def paste_kernel(parts, place_ref, arrived, before, out, sems):
    cells, half = arrived.shape
    rows = cells // parts
    left = pl.multiple_of((1 - place_ref[0]) * half, 128)
    copies = []
    for i in range(parts):
        at = pl.ds(i * rows, rows)
        copies.append(pltpu.make_async_copy(
            arrived.at[at, :], out.at[at, pl.ds(left, half)], sems.at[i]
        ))
    run(copies)


def paste(arrived, whole, place):
    parts = 4
    return pl.pallas_call(
        functools.partial(paste_kernel, parts),
        in_specs=[
            pl.BlockSpec(memory_space=pltpu.SMEM),
            IN_PLACE,
            IN_PLACE,
        ],
        out_specs=IN_PLACE,
        scratch_shapes=[pltpu.SemaphoreType.DMA((parts,))],
        out_shape=jax.ShapeDtypeStruct(whole.shape, jnp.float32),
        input_output_aliases={2: 0},
        name="paste",
        cost_estimate=LIGHT,
    )(place, arrived, whole)


def on_device(footprint, flux, obs_weight, obs_count):
    _, lags, slots, cells = footprint.shape
    half = flux.shape[2] // 2
    rows = slots // CHUNKS
    chunks = range(CHUNKS)
    devices = lax.axis_size("tm")
    place = jnp.stack(
        [lax.axis_index("core"), lax.axis_index("tm"), jnp.int32(devices)]
    ).astype(jnp.int32)
    valid = (jnp.arange(slots, dtype=jnp.int32) < obs_count[0]).astype(jnp.float32)
    row_scale = (valid * obs_weight[0])[:, None]
    later = range(1, lags)
    paired = devices == lags and cells == half

    own, terms, weighted = [], [], []
    specs = [pl.BlockSpec((rows, cells), lambda j: (0, 0))] * len(later)
    other_specs = [pl.BlockSpec((rows, cells), lambda j, i=i: (i, 0)) for i in range(len(later))]

    def row_block(r, lag):
        return lambda tile: pl.BlockSpec((1, 1, rows, tile), lambda j, c: (0, lag, r, j))

    def column(r):
        return lambda tile: pl.BlockSpec((rows, tile), lambda j, c: (r, j))

    def payload(k):
        h, p, w = k, k - 2, k - 4
        up = terms[p] if 0 <= p < CHUNKS else []
        down = []
        if h < CHUNKS:
            if up and paired:
                return "one", choose(place, footprint, h, up[::-1])
            down = cut(footprint, later, rows, h)
        elif w >= 0:
            value = weighted[w]
            if w > 1:
                value, done[0] = together(value, done[0])
            if up and paired:
                return "one", choose(place, value, None, up[::-1])
            down = [value] * len(later)
        return ("down" if not up else "both" if down else "up"), [*down, *up]

    def exchange(kind, sent):
        lags_of = {"down": [-1], "up": [1], "both": [-1, 1]}.get(kind)
        if kind == "one":
            return [cycled(value, lag) for value, lag in zip(sent, later)]
        ways = [way * lag for way in lags_of for lag in later]
        return [shifted(value, by) for value, by in zip(sent, ways)]

    def sorted_out(kind, arrived):
        count = len(later)
        if kind == "one":
            return arrived, arrived[::-1]
        low = arrived[:count] if kind != "up" else None
        return low, arrived[-count:] if kind != "down" else None

    def my_side(r, before):
        return [footprint, *own[r]], [row_block(r, 0)] + [column(0)] * len(later), before, 2 * half, True

    def their_side(r, before):
        foot = [foot_other] + [other[r]] * len(later)
        return foot, [column(r)] + [column(i) for i in range(len(later))], before, half, False

    other, done = [], [None, None]
    kind, sent = payload(0)
    flux, sent[0] = together(flux, sent[0])
    flux_parts = split(flux, swapped(side_of(flux, place)), place)
    foot_other = swapped(cut(footprint, [0], slots, 0)[0])
    same = forward(
        [footprint] * CHUNKS,
        [pl.BlockSpec((1, 1, rows, cells), lambda j, r=r: (0, 0, r, 0)) for r in chunks],
        [foot_other] * CHUNKS,
        [pl.BlockSpec((rows, cells), lambda j, r=r: (r, 0)) for r in chunks],
        rows, flux_parts,
    )
    for k in range(CHUNKS + 4):
        h, p, w = k, k - 2, k - 4
        arrived, sort = exchange(kind, sent), kind
        if k == 0:
            arrived[0], flux_parts[0] = together(arrived[0], flux_parts[0])
        if k == 2:
            arrived[0], same[0] = together(arrived[0], same[0])
        if k + 1 < CHUNKS + 4:
            kind, sent = payload(k + 1)
            for i in range(min(len(sent), len(arrived))):
                arrived[i], sent[i] = together(arrived[i], sent[i])
        low, high = sorted_out(sort, arrived)
        if h < CHUNKS:
            own.append(low)
            other.append(swapped(stack(low)))
            terms.append(forward(low, specs, [other[h]] * len(later), other_specs, rows, flux_parts))
        if 0 <= p < CHUNKS:
            total = combine(row_scale, same[p], high, p, place)
            if p > 0:
                total, weighted[p - 1] = together(total, weighted[p - 1])
            weighted.append(lax.psum(total, "z"))
        if w >= 0:
            here = [weighted[w], *low]
            if w + 1 < CHUNKS:
                done[:] = adjoint(here, [my_side(w, done[0]), their_side(w, done[1])], place, cells)
    (theirs,) = adjoint(here, [their_side(w, done[1])], place, cells)
    (mine,) = adjoint(here, [my_side(w, done[0])], place, cells)
    return paste(swapped(theirs), mine, place)[None]


def solution(mesh):
    devices = mesh.devices
    split = Mesh(devices.reshape(devices.shape[0], devices.shape[1] // 2, 2), ("tm", "z", "core"))
    cells = ("z", "core")
    placed = (P("tm", None, None, cells), P("tm", cells, None), P("tm", None), P("tm"))
    return jax.shard_map(
        on_device, mesh=split, in_specs=placed, out_specs=P("tm", cells, None), check_vma=False
    )
```

profile of v0, /device:TPU:3, one launch (start us, length us, event | category | flops | bytes accessed | tf_op | source)
XLA Modules:
  0.0 1300.5 jit_solution(2389064168538710894)
XLA Ops:
  6.5 72.6 %cut.4 = (f32[192,1024]{1,0:T(8,128)}, f32[192,1024]{1,0:T(8,128)}, f32[192,1024]{1,0:T(8,128)}) custom-call(f32[1,4,768,1024]{3,2,1,0:T(8,128)} %refs_4_.7), custom_call_target="tpu_custom_call" | custom-call | flops 1 | bytes 1 | tf_op jit(solution)/shard_map/cut/pallas_call | solution.py:202
  79.8 5.5 side.1
  88.0 1.9 collective-permute-start.4
  89.9 72.6 %cut.5 = (f32[192,1024]{1,0:T(8,128)}, f32[192,1024]{1,0:T(8,128)}, f32[192,1024]{1,0:T(8,128)}) custom-call(f32[1,4,768,1024]{3,2,1,0:T(8,128)} %refs_4_.7), custom_call_target="tpu_custom_call" | custom-call | flops 1 | bytes 1 | tf_op jit(solution)/shard_map/cut/pallas_call | solution.py:202
  162.6 7.9 split.1
  171.3 72.6 %stack.16 = f32[576,1024]{1,0:T(8,128)} custom-call(f32[192,1024]{1,0:T(8,128)} %copy-done.6, f32[192,1024]{1,0:T(8,128)} %copy-done.5, f32[192,1024]{1,0:T(8,128)} %copy-done.4), custom_call_target="tpu_custom_call" | custom-call | flops 1 | bytes 1 | tf_op jit(solution)/shard_map/stack/pallas_call | solution.py:224
  244.1 1.6 collective-permute-start.3
  245.7 1.9 collective-permute-start.8
  248.9 96.4 %cut.3 = f32[768,1024]{1,0:T(8,128)} custom-call(f32[1,4,768,1024]{3,2,1,0:T(8,128)} %refs_4_.7), custom_call_target="tpu_custom_call" | custom-call | flops 1 | bytes 1 | tf_op jit(solution)/shard_map/cut/pallas_call | solution.py:202
  345.8 12.9 forward.6
  358.7 73.3 %choose.4 = (f32[192,1024]{1,0:T(8,128)}, f32[192,1024]{1,0:T(8,128)}, f32[192,1024]{1,0:T(8,128)}) custom-call(s32[3]{0:T(128)} %pad_add_fusion.core_ref.place_ref, f32[1,4,768,1024]{3,2,1,0:T(8,128)} %refs_4_.7, f32[192,1024]{1,0:T(8,128)} %get-tuple-element.122.refs_0_, f32[192,1024]{1,0:T(8,128)} %get-tuple-element.123.refs_1_, ...), custom_call_target="tpu_custom_call" | custom-call | flops 1 | bytes 1 | tf_op jit(solution)/shard_map/choose/pallas_call | solution.py:304
  432.0 72.6 %stack.17 = f32[576,1024]{1,0:T(8,128)} custom-call(f32[192,1024]{1,0:T(8,128)} %collective-permute-done.8.refs_0_.refs_5_, f32[192,1024]{1,0:T(8,128)} %collective-permute-done.9.refs_1_.refs_6_, f32[192,1024]{1,0:T(8,128)} %collective-permute-done.3.refs_2_.refs_7_), custom_call_target="tpu_custom_call" | custom-call | flops 1 | bytes 1 | tf_op jit(solution)/shard_map/stack/pallas_call | solution.py:224
  504.8 3.5 collective-permute-start.7
  508.3 3.5 collective-permute-start.13
  511.8 1.7 copy-done
  513.5 16.0 %forward.5 = (f32[192,1024]{1,0:T(8,128)}, f32[192,1024]{1,0:T(8,128)}, f32[192,1024]{1,0:T(8,128)}, f32[192,1024]{1,0:T(8,128)}) custom-call(f32[1,4,768,1024]{3,2,1,0:T(8,128)} %refs_4_.7, f32[1,4,768,1024]{3,2,1,0:T(8,128)} %refs_4_.7, f32[1,4,768,1024]{3,2,1,0:T(8,128)} %refs_4_.7, f32[1,4,768,1024]{3,2,1,0:T(8,128)} %refs_4_.7, f32[768,1024]{1,0:T(8,128)} %copy-done, ...), custom_call_target="tpu_custom_call" | custom-call | flops 1 | bytes 1 | tf_op jit(solution)/shard_map/forward/pallas_call | solution.py:105
  529.5 12.9 forward.7
  542.3 73.3 %choose.5 = (f32[192,1024]{1,0:T(8,128)}, f32[192,1024]{1,0:T(8,128)}, f32[192,1024]{1,0:T(8,128)}) custom-call(s32[3]{0:T(128)} %pad_add_fusion.core_ref.place_ref, f32[1,4,768,1024]{3,2,1,0:T(8,128)} %refs_4_.7, f32[192,1024]{1,0:T(8,128)} %get-tuple-element.134.refs_0_, f32[192,1024]{1,0:T(8,128)} %get-tuple-element.135.refs_1_, ...), custom_call_target="tpu_custom_call" | custom-call | flops 1 | bytes 1 | tf_op jit(solution)/shard_map/choose/pallas_call | solution.py:304
  615.6 72.6 %stack.18 = f32[576,1024]{1,0:T(8,128)} custom-call(f32[192,1024]{1,0:T(8,128)} %collective-permute-done.12.refs_2_.refs_0_.refs_5_, f32[192,1024]{1,0:T(8,128)} %collective-permute-done.13.refs_1_.refs_6_, f32[192,1024]{1,0:T(8,128)} %collective-permute-done.7.refs_0_.refs_2_.refs_7_), custom_call_target="tpu_custom_call" | custom-call | flops 1 | bytes 1 | tf_op jit(solution)/shard_map/stack/pallas_call | solution.py:224
  688.2 1.4 collective-permute-start.14
  691.2 3.5 combine.4
  695.7 1.6 collective-permute-start.17
  697.3 1.4 copy-done.2
  698.7 12.9 forward.8
  711.6 27.4 %all-reduce.5.cloned.1.call-done.source.refs_0_ = f32[192,1024]{1,0:T(8,128)} async-done(((f32[192,1024]{1,0:T(8,128)}), f32[192,1024]{1,0:T(8,128)}) %all-reduce.5.cloned.1.call-update) | async-done | bytes 786448 | tf_op jit(solution)/shard_map/psum | solution.py:440
  739.0 73.3 %choose.6 = (f32[192,1024]{1,0:T(8,128)}, f32[192,1024]{1,0:T(8,128)}, f32[192,1024]{1,0:T(8,128)}) custom-call(s32[3]{0:T(128)} %pad_add_fusion.core_ref.place_ref, f32[192,1024]{1,0:T(8,128)} %all-reduce.5.cloned.1.call-done.source.refs_0_, f32[192,1024]{1,0:T(8,128)} %get-tuple-element.149.refs_0_, f32[192,1024]{1,0:T(8,128)} %get-tuple-element.150.refs_1_, ...), custom_call_target="tpu_custom_call" | custom-call | flops 1 | bytes 1 | tf_op jit(solution)/shard_map/choose/pallas_call | solution.py:304
  813.2 72.6 %stack.19 = f32[576,1024]{1,0:T(8,128)} custom-call(f32[192,1024]{1,0:T(8,128)} %collective-permute-done.17.refs_2_.refs_0_.refs_5_, f32[192,1024]{1,0:T(8,128)} %collective-permute-done.16.refs_1_.refs_6_, f32[192,1024]{1,0:T(8,128)} %copy-done.3), custom_call_target="tpu_custom_call" | custom-call | flops 1 | bytes 1 | tf_op jit(solution)/shard_map/stack/pallas_call | solution.py:224
  886.6 3.5 combine.5
  892.9 1.4 copy-done.1
  894.3 13.0 %forward.9 = (f32[192,1024]{1,0:T(8,128)}, f32[192,1024]{1,0:T(8,128)}, f32[192,1024]{1,0:T(8,128)}) custom-call(f32[192,1024]{1,0:T(8,128)} %collective-permute-done.17.refs_2_.refs_0_.refs_5_, f32[192,1024]{1,0:T(8,128)} %collective-permute-done.16.refs_1_.refs_6_, f32[192,1024]{1,0:T(8,128)} %copy-done.3, f32[576,1024]{1,0:T(8,128)} %copy-done.1, ...), custom_call_target="tpu_custom_call" | custom-call | flops 1 | bytes 1 | tf_op jit(solution)/shard_map/forward/pallas_call | solution.py:105
  907.3 25.3 %all-reduce.7.cloned.1.call-done.source.refs_0_ = f32[192,1024]{1,0:T(8,128)} async-done(((f32[192,1024]{1,0:T(8,128)}), f32[192,1024]{1,0:T(8,128)}) %all-reduce.7.cloned.1.call-update) | async-done | bytes 786448 | tf_op jit(solution)/shard_map/psum | solution.py:440
  932.7 73.3 %choose.7 = (f32[192,1024]{1,0:T(8,128)}, f32[192,1024]{1,0:T(8,128)}, f32[192,1024]{1,0:T(8,128)}) custom-call(s32[3]{0:T(128)} %pad_add_fusion.core_ref.place_ref, f32[192,1024]{1,0:T(8,128)} %all-reduce.7.cloned.1.call-done.source.refs_0_, f32[192,1024]{1,0:T(8,128)} %get-tuple-element.163.refs_0_, f32[192,1024]{1,0:T(8,128)} %get-tuple-element.164.refs_1_, ...), custom_call_target="tpu_custom_call" | custom-call | flops 1 | bytes 1 | tf_op jit(solution)/shard_map/choose/pallas_call | solution.py:304
  1006.8 3.4 combine.6
  1011.9 2.1 collective-permute-start.19
  1014.0 16.1 %adjoint.5 = (f32[1024,2048]{1,0:T(8,128)}, f32[1024,1024]{1,0:T(8,128)}) custom-call(s32[3]{0:T(128)} %pad_add_fusion.core_ref.place_ref, f32[192,1024]{1,0:T(8,128)} %all-reduce.5.cloned.1.call-done.source.refs_0_, f32[192,1024]{1,0:T(8,128)} %collective-permute-done.21.refs_2_.refs_1_, f32[192,1024]{1,0:T(8,128)} %collective-permute-done.20.refs_1_.refs_2_, ...), custom_call_target="tpu_custom_call" | custom-call | flops 1 | bytes 1 | tf_op jit(solution)/shard_map/adjoint/pallas_call | solution.py:164
  1030.0 23.4 %all-reduce.9.cloned.1.call-done.refs_0_ = f32[192,1024]{1,0:T(8,128)} async-done(((f32[192,1024]{1,0:T(8,128)}), f32[192,1024]{1,0:T(8,128)}) %all-reduce.9.cloned.1.call-update) | async-done | bytes 786448 | tf_op jit(solution)/shard_map/psum | solution.py:440
  1054.9 3.5 combine.7
  1058.3 1.6 collective-permute-start.28
  1061.2 12.3 collective-permute-start.24
  1073.5 17.3 %adjoint.6 = (f32[1024,2048]{1,0:T(8,128)}, f32[1024,1024]{1,0:T(8,128)}) custom-call(s32[3]{0:T(128)} %pad_add_fusion.core_ref.place_ref, f32[192,1024]{1,0:T(8,128)} %all-reduce.7.cloned.1.call-done.source.refs_0_, f32[192,1024]{1,0:T(8,128)} %copy-done.11, f32[192,1024]{1,0:T(8,128)} %copy-done.12, ...), custom_call_target="tpu_custom_call", output_to_operand_aliasing={{0}: (13, {}), {1}: (14, {})} | custom-call | flops 1 | bytes 1 | tf_op jit(solution)/shard_map/adjoint/pallas_call | solution.py:164
  1090.8 10.3 all-reduce.11.cloned.1.call-done.refs_0_
  1103.1 3.2 collective-permute-start.25
  1106.3 17.2 %adjoint.7 = (f32[1024,2048]{1,0:T(8,128)}, f32[1024,1024]{1,0:T(8,128)}) custom-call(s32[3]{0:T(128)} %pad_add_fusion.core_ref.place_ref, f32[192,1024]{1,0:T(8,128)} %all-reduce.9.cloned.1.call-done.refs_0_, f32[192,1024]{1,0:T(8,128)} %collective-permute-done.24.refs_1_, ...), custom_call_target="tpu_custom_call", output_to_operand_aliasing={{0}: (13, {}), {1}: (14, {})} | custom-call | flops 1 | bytes 1 | tf_op jit(solution)/shard_map/adjoint/pallas_call | solution.py:164
  1123.6 16.5 %collective-permute-done.27.refs_2_ = f32[192,1024]{1,0:T(8,128)S(1)} collective-permute-done((f32[192,1024]{1,0:T(8,128)}, f32[192,1024]{1,0:T(8,128)S(1)}, u32[]{:S(2)}, u32[]{:S(2)}) %collective-permute-start.27) | collective-permute-done | bytes 786464 | tf_op jit(solution)/shard_map/ppermute | solution.py:21
  1141.2 11.0 adjoint.8
  1152.3 1.6 collective-permute-start.30
  1153.9 11.0 adjoint.9.before
  1164.9 128.9 %paste.1 = f32[1024,2048]{1,0:T(8,128)} custom-call(s32[3]{0:T(128)} %pad_add_fusion.core_ref.place_ref, f32[1024,1024]{1,0:T(8,128)} %collective-permute-done.30.arrived, f32[1024,2048]{1,0:T(8,128)} %adjoint.9.before), custom_call_target="tpu_custom_call", output_to_operand_aliasing={{}: (2, {})} | custom-call | flops 1 | bytes 1 | tf_op jit(solution)/shard_map/paste/pallas_call | solution.py:330
  (91 shorter events, 21.0 us)
Async XLA Ops:
  6.5 732.5 %all-reduce.5.cloned.1.call-start = ((), (), s32[]{:S(2)}) async-start(), calls=%async_computation | async-start | bytes 1572864 | tf_op jit(solution)/shard_map/psum | solution.py:440
  79.8 8.2 copy-start.16
  85.3 77.3 %collective-permute-start.1 = (f32[1024,1024]{1,0:T(8,128)}, f32[1024,1024]{1,0:T(8,128)}, u32[]{:S(2)}, u32[]{:S(2)}) collective-permute-start(f32[1024,1024]{1,0:T(8,128)} %side.1), channel_id=1, source_target_pairs={{0,1},{1,0},{2,3},{3,2},{4,5},{5,4},{6,7},{7,6},{8,9},{9,8},{10,11... | collective-permute-start | bytes 12582920 | tf_op jit(solution)/shard_map/ppermute | solution.py:30
  86.0 76.6 %collective-permute-start.2 = (f32[192,1024]{1,0:T(8,128)}, f32[192,1024]{1,0:T(8,128)S(1)}, u32[]{:S(2)}, u32[]{:S(2)}) collective-permute-start(f32[192,1024]{1,0:T(8,128)} %get-tuple-element.110), channel_id=1, source_target_pairs={{24,0},{25,1},{26,2},{27,3},{28,4},{29,5},{30,6},{31,7}} | collective-permute-start | bytes 2359304 | tf_op jit(solution)/shard_map/ppermute | solution.py:21
  86.7 75.9 %collective-permute-start.5 = (f32[192,1024]{1,0:T(8,128)}, f32[192,1024]{1,0:T(8,128)S(1)}, u32[]{:S(2)}, u32[]{:S(2)}) collective-permute-start(f32[192,1024]{1,0:T(8,128)} %get-tuple-element.117), channel_id=1, source_target_pairs={{16,0},{24,8},{17,1},{25,9},{18,2},{26,10},{19,3},{27,11},{20,4},{... | collective-permute-start | bytes 2359304 | tf_op jit(solution)/shard_map/ppermute | solution.py:21
  88.0 82.5 %collective-permute-start.4 = (f32[192,1024]{1,0:T(8,128)S(1)}, f32[192,1024]{1,0:T(8,128)S(1)}, u32[]{:S(2)}, u32[]{:S(2)}) collective-permute-start(f32[192,1024]{1,0:T(8,128)S(1)} %copy-done.16), channel_id=1, source_target_pairs={{8,0},{16,8},{24,16},{9,1},{17,9},{25,17},{10,2},{18,10},{26,18},{... | collective-permute-start | bytes 2359304 | tf_op jit(solution)/shard_map/ppermute | solution.py:21
  162.5 7.9 copy-start.4
  162.6 7.9 copy-start.5
  243.9 101.8 %collective-permute-start.6 = (f32[576,1024]{1,0:T(8,128)}, f32[576,1024]{1,0:T(8,128)}, u32[]{:S(2)}, u32[]{:S(2)}) collective-permute-start(f32[576,1024]{1,0:T(8,128)} %stack.16), channel_id=1, source_target_pairs={{0,1},{1,0},{2,3},{3,2},{4,5},{5,4},{6,7},{7,6},{8,9},{9,8},{10,11... | collective-permute-start | bytes 7077896 | tf_op jit(solution)/shard_map/ppermute | solution.py:30
  244.1 187.9 %collective-permute-start.3 = (f32[192,1024]{1,0:T(8,128)}, f32[192,1024]{1,0:T(8,128)}, u32[]{:S(2)}, u32[]{:S(2)}) collective-permute-start(f32[192,1024]{1,0:T(8,128)} %get-tuple-element.112), channel_id=1, source_target_pairs={{24,0},{25,1},{26,2},{27,3},{28,4},{29,5},{30,6},{31,7}} | collective-permute-start | bytes 2359304 | tf_op jit(solution)/shard_map/ppermute | solution.py:21
  245.7 186.3 %collective-permute-start.8 = (f32[192,1024]{1,0:T(8,128)}, f32[192,1024]{1,0:T(8,128)}, u32[]{:S(2)}, u32[]{:S(2)}) collective-permute-start(f32[192,1024]{1,0:T(8,128)} %get-tuple-element.127), channel_id=1, source_target_pairs={{8,0},{16,8},{24,16},{9,1},{17,9},{25,17},{10,2},{18,10},{26,18},{... | collective-permute-start | bytes 2359304 | tf_op jit(solution)/shard_map/ppermute | solution.py:21
  247.6 184.4 %collective-permute-start.9 = (f32[192,1024]{1,0:T(8,128)}, f32[192,1024]{1,0:T(8,128)}, u32[]{:S(2)}, u32[]{:S(2)}) collective-permute-start(f32[192,1024]{1,0:T(8,128)} %get-tuple-element.130), channel_id=1, source_target_pairs={{16,0},{24,8},{17,1},{25,9},{18,2},{26,10},{19,3},{27,11},{20,4},{... | collective-permute-start | bytes 2359304 | tf_op jit(solution)/shard_map/ppermute | solution.py:21
  345.3 166.5 %collective-permute-start = (f32[768,1024]{1,0:T(8,128)}, f32[768,1024]{1,0:T(8,128)S(1)}, u32[]{:S(2)}, u32[]{:S(2)}) collective-permute-start(f32[768,1024]{1,0:T(8,128)} %cut.3), channel_id=1, source_target_pairs={{0,1},{1,0},{2,3},{3,2},{4,5},{5,4},{6,7},{7,6},{8,9},{9,8},{10,11... | collective-permute-start | bytes 9437192 | tf_op jit(solution)/shard_map/ppermute | solution.py:30
  504.6 24.8 %collective-permute-start.10 = (f32[576,1024]{1,0:T(8,128)}, f32[576,1024]{1,0:T(8,128)}, u32[]{:S(2)}, u32[]{:S(2)}) collective-permute-start(f32[576,1024]{1,0:T(8,128)} %stack.17), channel_id=1, source_target_pairs={{0,1},{1,0},{2,3},{3,2},{4,5},{5,4},{6,7},{7,6},{8,9},{9,8},{10,11... | collective-permute-start | bytes 7077896 | tf_op jit(solution)/shard_map/ppermute | solution.py:30
  504.8 24.7 %collective-permute-start.12 = (f32[192,1024]{1,0:T(8,128)}, f32[192,1024]{1,0:T(8,128)}, u32[]{:S(2)}, u32[]{:S(2)}) collective-permute-start(f32[192,1024]{1,0:T(8,128)} %get-tuple-element.139), channel_id=1, source_target_pairs={{0,24},{8,0},{16,8},{24,16},{1,25},{9,1},{17,9},{25,17},{2,26},{10... | collective-permute-start | bytes 2359304 | tf_op jit(solution)/shard_map/ppermute | solution.py:26
  504.8 110.8 %collective-permute-start.7 = (f32[192,1024]{1,0:T(8,128)}, f32[192,1024]{1,0:T(8,128)}, u32[]{:S(2)}, u32[]{:S(2)}) collective-permute-start(f32[192,1024]{1,0:T(8,128)} %get-tuple-element.126), channel_id=1, source_target_pairs={{0,8},{8,16},{16,24},{24,0},{1,9},{9,17},{17,25},{25,1},{2,10},{10... | collective-permute-start | bytes 2359304 | tf_op jit(solution)/shard_map/ppermute | solution.py:26
  508.3 107.3 %collective-permute-start.13 = (f32[192,1024]{1,0:T(8,128)}, f32[192,1024]{1,0:T(8,128)}, u32[]{:S(2)}, u32[]{:S(2)}) collective-permute-start(f32[192,1024]{1,0:T(8,128)} %get-tuple-element.143), channel_id=1, source_target_pairs={{0,16},{8,24},{16,0},{24,8},{1,17},{9,25},{17,1},{25,9},{2,18},{10... | collective-permute-start | bytes 2359304 | tf_op jit(solution)/shard_map/ppermute | solution.py:26
  511.8 1.7 copy-start
  615.6 74.7 %copy-start.15 = (f32[1,768]{1,0:T(1,128)S(1)}, f32[1,768]{1,0:T(1,128)}, u32[]{:S(2)}) copy-start(f32[1,768]{1,0:T(1,128)} %param.6) | copy-start | bytes 9220
  688.2 9.1 collective-permute-start.14
  694.8 237.9 %all-reduce.7.cloned.1.call-start = ((), (), s32[]{:S(2)}) async-start(), calls=%async_computation.1 | async-start | bytes 1572864 | tf_op jit(solution)/shard_map/psum | solution.py:440
  694.8 117.5 %collective-permute-start.11 = (f32[192,1024]{1,0:T(8,128)}, f32[192,1024]{1,0:T(8,128)S(1)}, u32[]{:S(2)}, u32[]{:S(2)}) collective-permute-start(f32[192,1024]{1,0:T(8,128)} %get-tuple-element.138), channel_id=1, source_target_pairs={{0,8},{8,16},{16,24},{24,0},{1,9},{9,17},{17,25},{25,1},{2,10},{10... | collective-permute-start | bytes 2359304 | tf_op jit(solution)/shard_map/ppermute | solution.py:26
  694.9 117.4 %collective-permute-start.16 = (f32[192,1024]{1,0:T(8,128)}, f32[192,1024]{1,0:T(8,128)}, u32[]{:S(2)}, u32[]{:S(2)}) collective-permute-start(f32[192,1024]{1,0:T(8,128)} %get-tuple-element.156), channel_id=1, source_target_pairs={{0,16},{8,24},{16,0},{24,8},{1,17},{9,25},{17,1},{25,9},{2,18},{10... | collective-permute-start | bytes 2359304 | tf_op jit(solution)/shard_map/ppermute | solution.py:26
  695.7 116.6 %collective-permute-start.17 = (f32[192,1024]{1,0:T(8,128)}, f32[192,1024]{1,0:T(8,128)}, u32[]{:S(2)}, u32[]{:S(2)}) collective-permute-start(f32[192,1024]{1,0:T(8,128)} %get-tuple-element.159), channel_id=1, source_target_pairs={{0,24},{8,0},{16,8},{24,16},{1,25},{9,1},{17,9},{25,17},{2,26},{10... | collective-permute-start | bytes 2359304 | tf_op jit(solution)/shard_map/ppermute | solution.py:26
  697.3 1.4 copy-start.2
  885.8 7.1 collective-permute-start.18
  890.1 163.3 %all-reduce.9.cloned.1.call-start = ((), (), s32[]{:S(2)}) async-start(), calls=%async_computation.2 | async-start | bytes 1572864 | tf_op jit(solution)/shard_map/psum | solution.py:440
  890.2 115.8 %collective-permute-start.15 = (f32[192,1024]{1,0:T(8,128)}, f32[192,1024]{1,0:T(8,128)S(1)}, u32[]{:S(2)}, u32[]{:S(2)}) collective-permute-start(f32[192,1024]{1,0:T(8,128)} %get-tuple-element.153), channel_id=1, source_target_pairs={{0,8},{8,16},{16,24},{24,0},{1,9},{9,17},{17,25},{25,1},{2,10},{10... | collective-permute-start | bytes 2359304 | tf_op jit(solution)/shard_map/ppermute | solution.py:26
  891.4 114.5 %collective-permute-start.20 = (f32[192,1024]{1,0:T(8,128)}, f32[192,1024]{1,0:T(8,128)}, u32[]{:S(2)}, u32[]{:S(2)}) collective-permute-start(f32[192,1024]{1,0:T(8,128)} %get-tuple-element.170), channel_id=1, source_target_pairs={{0,16},{8,24},{16,0},{24,8},{1,17},{9,25},{17,1},{25,9},{2,18},{10... | collective-permute-start | bytes 2359304 | tf_op jit(solution)/shard_map/ppermute | solution.py:26
  891.7 114.3 %collective-permute-start.21 = (f32[192,1024]{1,0:T(8,128)}, f32[192,1024]{1,0:T(8,128)}, u32[]{:S(2)}, u32[]{:S(2)}) collective-permute-start(f32[192,1024]{1,0:T(8,128)} %get-tuple-element.173), channel_id=1, source_target_pairs={{0,24},{8,0},{16,8},{24,16},{1,25},{9,1},{17,9},{25,17},{2,26},{10... | collective-permute-start | bytes 2359304 | tf_op jit(solution)/shard_map/ppermute | solution.py:26
  892.9 1.4 copy-start.1
  1010.3 90.8 %all-reduce.11.cloned.1.call-start = ((), (), s32[]{:S(2)}) async-start(), calls=%async_computation.3 | async-start | bytes 1572864 | tf_op jit(solution)/shard_map/psum | solution.py:440
  1010.4 43.1 %collective-permute-start.23 = (f32[192,1024]{1,0:T(8,128)}, f32[192,1024]{1,0:T(8,128)S(1)}, u32[]{:S(2)}, u32[]{:S(2)}) collective-permute-start(f32[192,1024]{1,0:T(8,128)} %get-tuple-element.183), channel_id=1, source_target_pairs={{0,24},{8,0},{16,8},{24,16},{1,25},{9,1},{17,9},{25,17},{2,26},{10... | collective-permute-start | bytes 2359304 | tf_op jit(solution)/shard_map/ppermute | solution.py:26
  1010.7 42.8 %collective-permute-start.22 = (f32[192,1024]{1,0:T(8,128)}, f32[192,1024]{1,0:T(8,128)S(1)}, u32[]{:S(2)}, u32[]{:S(2)}) collective-permute-start(f32[192,1024]{1,0:T(8,128)} %get-tuple-element.181), channel_id=1, source_target_pairs={{0,16},{8,24},{16,0},{24,8},{1,17},{9,25},{17,1},{25,9},{2,18},{10... | collective-permute-start | bytes 2359304 | tf_op jit(solution)/shard_map/ppermute | solution.py:26
  1011.9 41.6 %collective-permute-start.19 = (f32[192,1024]{1,0:T(8,128)}, f32[192,1024]{1,0:T(8,128)S(1)}, u32[]{:S(2)}, u32[]{:S(2)}) collective-permute-start(f32[192,1024]{1,0:T(8,128)} %get-tuple-element.167), channel_id=1, source_target_pairs={{0,8},{8,16},{16,24},{24,0},{1,9},{9,17},{17,25},{25,1},{2,10},{10... | collective-permute-start | bytes 2359304 | tf_op jit(solution)/shard_map/ppermute | solution.py:26
  1053.5 4.9 copy-start.14
  1053.5 1.2 copy-start.12
  1053.5 1.4 copy-start.13
  1058.3 42.8 %collective-permute-start.28 = (f32[192,1024]{1,0:T(8,128)S(1)}, f32[192,1024]{1,0:T(8,128)}, u32[]{:S(2)}, u32[]{:S(2)}) collective-permute-start(f32[192,1024]{1,0:T(8,128)S(1)} %copy-done.14), channel_id=1, source_target_pairs={{24,0},{25,1},{26,2},{27,3},{28,4},{29,5},{30,6},{31,7}} | collective-permute-start | bytes 2359304 | tf_op jit(solution)/shard_map/ppermute | solution.py:21
  1059.9 41.9 %collective-permute-start.26 = (f32[192,1024]{1,0:T(8,128)S(1)}, f32[192,1024]{1,0:T(8,128)}, u32[]{:S(2)}, u32[]{:S(2)}) collective-permute-start(f32[192,1024]{1,0:T(8,128)S(1)} %copy-done.14), channel_id=1, source_target_pairs={{16,0},{24,8},{17,1},{25,9},{18,2},{26,10},{19,3},{27,11},{20,4},{... | collective-permute-start | bytes 2359304 | tf_op jit(solution)/shard_map/ppermute | solution.py:21
  1061.2 41.9 %collective-permute-start.24 = (f32[192,1024]{1,0:T(8,128)S(1)}, f32[192,1024]{1,0:T(8,128)}, u32[]{:S(2)}, u32[]{:S(2)}) collective-permute-start(f32[192,1024]{1,0:T(8,128)S(1)} %copy-done.14), channel_id=1, source_target_pairs={{8,0},{16,8},{24,16},{9,1},{17,9},{25,17},{10,2},{18,10},{26,18},{... | collective-permute-start | bytes 2359304 | tf_op jit(solution)/shard_map/ppermute | solution.py:21
  1101.1 22.4 %collective-permute-start.29 = (f32[192,1024]{1,0:T(8,128)}, f32[192,1024]{1,0:T(8,128)S(1)}, u32[]{:S(2)}, u32[]{:S(2)}) collective-permute-start(f32[192,1024]{1,0:T(8,128)} %all-reduce.11.cloned.1.call-done.refs_0_), channel_id=1, source_target_pairs={{24,0},{25,1},{26,2},{27,3},{28,4},{29,5},{30,6},{31,7}} | collective-permute-start | bytes 2359304 | tf_op jit(solution)/shard_map/ppermute | solution.py:21
  1101.8 38.3 %collective-permute-start.27 = (f32[192,1024]{1,0:T(8,128)}, f32[192,1024]{1,0:T(8,128)S(1)}, u32[]{:S(2)}, u32[]{:S(2)}) collective-permute-start(f32[192,1024]{1,0:T(8,128)} %all-reduce.11.cloned.1.call-done.refs_0_), channel_id=1, source_target_pairs={{16,0},{24,8},{17,1},{25,9},{18,2},{26,10},{19,3},{27,11},{20,4},{... | collective-permute-start | bytes 2359304 | tf_op jit(solution)/shard_map/ppermute | solution.py:21
  1103.1 37.0 %collective-permute-start.25 = (f32[192,1024]{1,0:T(8,128)}, f32[192,1024]{1,0:T(8,128)S(1)}, u32[]{:S(2)}, u32[]{:S(2)}) collective-permute-start(f32[192,1024]{1,0:T(8,128)} %all-reduce.11.cloned.1.call-done.refs_0_), channel_id=1, source_target_pairs={{8,0},{16,8},{24,16},{9,1},{17,9},{25,17},{10,2},{18,10},{26,18},{... | collective-permute-start | bytes 2359304 | tf_op jit(solution)/shard_map/ppermute | solution.py:21
  1123.5 16.6 %copy-start.7 = (f32[192,1024]{1,0:T(8,128)}, f32[192,1024]{1,0:T(8,128)S(1)}, u32[]{:S(2)}) copy-start(f32[192,1024]{1,0:T(8,128)S(1)} %collective-permute-done.29.refs_3_) | copy-start | bytes 2359300
  1140.1 0.9 copy-start.8
  1140.1 1.1 copy-start.9
  1152.3 12.6 collective-permute-start.30
  (4 other events, 3.5 us)
Sparse Core Ops, SparseCore 0:
  694.9 44.0 all-reduce.4
  890.2 42.3 all-reduce.6
  1010.4 42.9 all-reduce.8
  1058.5 42.5 all-reduce.10
where the time goes:
time: 1310 us; the launch traced here: 1300 us
  Pallas kernels  1120 us (85%)
  waiting for transfers between devices  103 us (8%)
  starting transfers between devices  50.2 us (4%)
  between operations  14.5 us (1%)
    pallas_call x4, Pallas kernels, choose(): pl.pallas_call(functools.partial(choose_kernel, r), in_specs=[pl.BlockSpe...  293 us
    pallas_call x4, Pallas kernels, stack(): pl.pallas_call(stack_kernel, in_specs=[IN_PLACE] * len(pieces), out_specs...  290 us
    pallas_call x3, Pallas kernels, cut(): pl.pallas_call(functools.partial(cut_kernel, lags, r), in_specs=[IN_PLACE...  242 us
    pallas_call x1, Pallas kernels, paste(): pl.pallas_call(functools.partial(paste_kernel, parts), in_specs=[pl.Block...  129 us
    psum x4, waiting for transfers between devices, on_device(): weighted.append(lax.psum(total, 'z'))  86.4 us
    pallas_call x5, Pallas kernels, adjoint(): pl.pallas_call(functools.partial(adjoint_kernel, count, len(sides), first...  72.6 us
    pallas_call x5, Pallas kernels, forward(): pl.pallas_call(functools.partial(forward_kernel, count), grid=(half // ti...  67.8 us
    ppermute x12, starting transfers between devices, shifted(): return lax.ppermute(value, 'tm', pairs)  29 us
  transfers between devices with their start and end apart: 35, of which 5 were waited for; matrix products, arithmetic and copies ran while one was open for 0% of the time, Pallas kernels for 52%

commit v1 on v0

--- a/solution.py
+++ b/solution.py
@@ -8,6 +8,7 @@
 from jax.sharding import Mesh, PartitionSpec as P
 
 CHUNKS = 4
+PARTS = 8
 TILE = 256
 WIDE = 512
 LIGHT = pl.CostEstimate(flops=1, bytes_accessed=1, transcendentals=0)
@@ -44,20 +45,19 @@
     return lax.dot_general(left, right, (dims, ((), ())), preferred_element_type=jnp.float32)
 
 
-def split_kernel(core_ref, own, other, high_ref, low_ref):
+def split_kernel(core_ref, own, other, out):
     cells = other.shape[0]
     for at, value in ((0, own[0]), (cells, other[...])):
         high, low = halves(value)
-        high_ref[pl.ds(at, cells), :] = high
-        low_ref[pl.ds(at, cells), :] = low
+        for block, part in enumerate((high, high, low)):
+            out[pl.ds(block * 2 * cells + at, cells), :] = part
 
 
 def split(flux, flux_other, core):
     cells, half = flux_other.shape
     tile = min(TILE, half)
     steps = half // tile
-    block = pl.BlockSpec((2 * cells, tile), lambda j, c: (0, j))
-    return list(pl.pallas_call(
+    return pl.pallas_call(
         split_kernel,
         grid_spec=pltpu.PrefetchScalarGridSpec(
             num_scalar_prefetch=1,
@@ -66,57 +66,53 @@
                 pl.BlockSpec((1, cells, tile), lambda j, c: (0, 0, c[0] * steps + j)),
                 pl.BlockSpec((cells, tile), lambda j, c: (0, j)),
             ],
-            out_specs=[block, block],
+            out_specs=pl.BlockSpec((6 * cells, tile), lambda j, c: (0, j)),
         ),
-        out_shape=[jax.ShapeDtypeStruct((2 * cells, half), jnp.bfloat16)] * 2,
+        out_shape=jax.ShapeDtypeStruct((6 * cells, half), jnp.bfloat16),
+        compiler_params=pltpu.CompilerParams(vmem_limit_bytes=VMEM_LIMIT),
         name="split",
         cost_estimate=LIGHT,
-    )(core, flux, flux_other))
+    )(core, flux, flux_other)
 
 
 def forward_kernel(count, *refs):
     foot_own, foot_other = refs[:count], refs[count:2 * count]
-    flux_high, flux_low = refs[2 * count:2 * count + 2]
-    outs = refs[2 * count + 2:3 * count + 2]
-    parts_ref = refs[-1]
+    flux_parts, outs, parts_ref = refs[2 * count], refs[2 * count + 1:-1], refs[-1]
     rows, cells = foot_own[0].shape[-2:]
-    depth = count * rows
 
     @pl.when(pl.program_id(0) == 0)
     def _():
         for i in range(count):
             for side, source in ((0, foot_own[i]), (1, foot_other[i])):
                 high, low = halves(source[...].reshape(rows, cells))
-                columns = pl.ds(side * cells, cells)
-                parts_ref[pl.ds(i * rows, rows), columns] = high
-                parts_ref[pl.ds(depth + i * rows, rows), columns] = low
-
-    dims = ((1,), (0,))
-    both = times(parts_ref[...], flux_high[...], dims)
-    total = both[:depth] + both[depth:] + times(parts_ref[pl.ds(0, depth), :], flux_low[...], dims)
+                for block, part in enumerate((high, low, high)):
+                    columns = pl.ds((2 * block + side) * cells, cells)
+                    parts_ref[pl.ds(i * rows, rows), columns] = part
+
+    total = times(parts_ref[...], flux_parts[...], ((1,), (0,)))
     for i in range(count):
         outs[i][...] = total[i * rows:(i + 1) * rows]
 
 
 def forward(foot_own, own_specs, foot_other, other_specs, rows, flux_parts):
     count = len(foot_own)
-    depth, half = flux_parts[0].shape
-    tile = min(WIDE, half)
+    depth, half = flux_parts.shape
+    tile = min(TILE, half)
     outs = pl.pallas_call(
         functools.partial(forward_kernel, count),
         grid=(half // tile,),
         in_specs=[
             *own_specs,
             *other_specs,
-            *[pl.BlockSpec((depth, tile), lambda j: (0, j))] * 2,
+            pl.BlockSpec((depth, tile), lambda j: (0, j)),
         ],
         out_specs=[pl.BlockSpec((rows, tile), lambda j: (0, j))] * count,
-        scratch_shapes=[pltpu.VMEM((2 * count * rows, depth), jnp.bfloat16)],
+        scratch_shapes=[pltpu.VMEM((count * rows, depth), jnp.bfloat16)],
         out_shape=[jax.ShapeDtypeStruct((rows, half), jnp.float32)] * count,
         compiler_params=pltpu.CompilerParams(vmem_limit_bytes=VMEM_LIMIT),
         name="forward",
         cost_estimate=LIGHT,
-    )(*foot_own, *foot_other, *flux_parts)
+    )(*foot_own, *foot_other, flux_parts)
     return list(outs)
 
 
@@ -124,24 +120,23 @@
     weighted, refs = refs[:count], refs[count:]
     foot, refs = refs[:sides * count], refs[sides * count:]
     before, refs = (None, refs) if first else (refs[:sides], refs[sides:])
-    outs, (high_ref, low_ref) = refs[:sides], refs[sides:]
+    outs, parts_ref = refs[:sides], refs[sides]
     rows, tile = foot[0].shape[-2:]
+    depth = count * rows
 
     @pl.when(pl.program_id(0) == 0)
     def _():
         for i in range(count):
             value = jnp.where(place_ref[1] + i < place_ref[2], weighted[i][...], 0.0)
             high, low = halves(value)
-            high_ref[pl.ds(i * rows, rows), :] = high
-            low_ref[pl.ds(i * rows, rows), :] = low
-
-    dims = ((1,), (0,))
+            for block, part in enumerate((high, high, low)):
+                parts_ref[pl.ds(block * depth + i * rows, rows), :] = part
+
     for side in range(sides):
         mine = foot[side * count:(side + 1) * count]
         slab = jnp.concatenate([ref[...].reshape(rows, tile) for ref in mine], axis=0)
         high, low = halves(slab.T)
-        both = times(jnp.concatenate([high, low], axis=0), high_ref[...], dims)
-        total = both[:tile] + both[tile:] + times(high, low_ref[...], dims)
+        total = times(jnp.concatenate([high, low, high], axis=1), parts_ref[...], ((1,), (0,)))
         if not first:
             total = total + before[side][...]
         outs[side][...] = total
@@ -172,7 +167,7 @@
                 *([] if first else out_specs),
             ],
             out_specs=out_specs,
-            scratch_shapes=[pltpu.VMEM((count * rows, half), jnp.bfloat16)] * 2,
+            scratch_shapes=[pltpu.VMEM((3 * count * rows, half), jnp.bfloat16)],
         ),
         out_shape=[jax.ShapeDtypeStruct((cells, side[3]), jnp.float32) for side in sides],
         input_output_aliases={} if first else {at + i: i for i in range(len(sides))},
@@ -182,19 +177,27 @@
     )(core, *weighted, *foot, *earlier)
 
 
-def run(copies):
-    for copy in copies:
-        copy.start()
-    for copy in copies:
-        copy.wait()
+def through(buffer, sems, moves):
+    loads = [pltpu.make_async_copy(a, buffer.at[i], sems.at[0, i]) for i, (a, _) in enumerate(moves)]
+    stores = [pltpu.make_async_copy(buffer.at[i], b, sems.at[1, i]) for i, (_, b) in enumerate(moves)]
+    for load in loads:
+        load.start()
+    for load, store in zip(loads, stores):
+        load.wait()
+        store.start()
+    for store in stores:
+        store.wait()
+
+
+def passage(count, rows, columns):
+    return [pltpu.VMEM((count, rows, columns), jnp.float32), pltpu.SemaphoreType.DMA((2, count))]
 
 
 def cut_kernel(lags, r, footprint, *refs):
-    outs, sems = refs[:-1], refs[-1]
+    outs, buffer, sems = refs[:-2], refs[-2], refs[-1]
     rows = outs[0].shape[0]
-    run([
-        pltpu.make_async_copy(footprint.at[0, lag, pl.ds(r * rows, rows), :], out, sems.at[i])
-        for i, (lag, out) in enumerate(zip(lags, outs))
+    through(buffer, sems, [
+        (footprint.at[0, lag, pl.ds(r * rows, rows), :], out) for lag, out in zip(lags, outs)
     ])
 
 
@@ -203,7 +206,7 @@
         functools.partial(cut_kernel, lags, r),
         in_specs=[IN_PLACE],
         out_specs=[IN_PLACE] * len(lags),
-        scratch_shapes=[pltpu.SemaphoreType.DMA((len(lags),))],
+        scratch_shapes=passage(len(lags), rows, footprint.shape[3]),
         out_shape=[jax.ShapeDtypeStruct((rows, footprint.shape[3]), jnp.float32)] * len(lags),
         name="cut",
         cost_estimate=LIGHT,
@@ -211,12 +214,9 @@
 
 
 def stack_kernel(*refs):
-    pieces, out, sems = refs[:-2], refs[-2], refs[-1]
+    pieces, out, buffer, sems = refs[:-3], refs[-3], refs[-2], refs[-1]
     rows = pieces[0].shape[0]
-    run([
-        pltpu.make_async_copy(piece, out.at[pl.ds(i * rows, rows), :], sems.at[i])
-        for i, piece in enumerate(pieces)
-    ])
+    through(buffer, sems, [(piece, out.at[pl.ds(i * rows, rows), :]) for i, piece in enumerate(pieces)])
 
 
 def stack(pieces):
@@ -225,33 +225,32 @@
         stack_kernel,
         in_specs=[IN_PLACE] * len(pieces),
         out_specs=IN_PLACE,
-        scratch_shapes=[pltpu.SemaphoreType.DMA((len(pieces),))],
+        scratch_shapes=passage(len(pieces), rows, cells),
         out_shape=jax.ShapeDtypeStruct((rows * len(pieces), cells), jnp.float32),
         name="stack",
         cost_estimate=LIGHT,
     )(*pieces)
 
 
-def side_kernel(core_ref, flux, out):
-    out[...] = flux[0]
-
-
-def side_of(flux, core):
+def side_kernel(parts, place_ref, flux, out, buffer, sems):
+    cells, half = out.shape
+    rows = cells // parts
+    left = pl.multiple_of((1 - place_ref[0]) * half, 128)
+    bands = [pl.ds(i * rows, rows) for i in range(parts)]
+    through(buffer, sems, [(flux.at[0, at, pl.ds(left, half)], out.at[at, :]) for at in bands])
+
+
+def side_of(flux, place):
     _, cells, width = flux.shape
-    tile = min(TILE, width // 2)
-    steps = width // 2 // tile
-    return pl.pallas_call(
-        side_kernel,
-        grid_spec=pltpu.PrefetchScalarGridSpec(
-            num_scalar_prefetch=1,
-            grid=(steps,),
-            in_specs=[pl.BlockSpec((1, cells, tile), lambda j, c: (0, 0, (1 - c[0]) * steps + j))],
-            out_specs=pl.BlockSpec((cells, tile), lambda j, c: (0, j)),
-        ),
+    return pl.pallas_call(
+        functools.partial(side_kernel, PARTS),
+        in_specs=[pl.BlockSpec(memory_space=pltpu.SMEM), IN_PLACE],
+        out_specs=IN_PLACE,
+        scratch_shapes=passage(PARTS, cells // PARTS, width // 2),
         out_shape=jax.ShapeDtypeStruct((cells, width // 2), jnp.float32),
         name="side",
         cost_estimate=LIGHT,
-    )(core, flux)
+    )(place, flux)
 
 
 def combine_kernel(place_ref, scale, same, *refs):
@@ -284,19 +283,27 @@
 
 
 def choose_kernel(r, place_ref, source, *refs):
-    count = len(refs) // 2
-    ups, outs, sems = refs[:count], refs[count:2 * count], refs[-1]
+    count = len(refs) // 2 - 1
+    ups, outs, buffer, sems = refs[:count], refs[count:2 * count], refs[-2], refs[-1]
     rows = outs[0].shape[0]
-    choices = []
+    loads, stores = [], []
     for i, (up, out) in enumerate(zip(ups, outs)):
         down = source if r is None else source.at[0, i + 1, pl.ds(r * rows, rows), :]
         below = place_ref[1] > i
-        choices.append((below, pltpu.make_async_copy(down, out, sems.at[i])))
-        choices.append((jnp.logical_not(below), pltpu.make_async_copy(up, out, sems.at[i])))
-    for taken, copy in choices:
-        pl.when(taken)(copy.start)
-    for taken, copy in choices:
-        pl.when(taken)(copy.wait)
+        loads.append([
+            (below, pltpu.make_async_copy(down, buffer.at[i], sems.at[0, i])),
+            (jnp.logical_not(below), pltpu.make_async_copy(up, buffer.at[i], sems.at[0, i])),
+        ])
+        stores.append(pltpu.make_async_copy(buffer.at[i], out, sems.at[1, i]))
+    for pair in loads:
+        for taken, load in pair:
+            pl.when(taken)(load.start)
+    for pair, store in zip(loads, stores):
+        for taken, load in pair:
+            pl.when(taken)(load.wait)
+        store.start()
+    for store in stores:
+        store.wait()
 
 
 def choose(place, source, r, up):
@@ -305,37 +312,28 @@
         functools.partial(choose_kernel, r),
         in_specs=[pl.BlockSpec(memory_space=pltpu.SMEM)] + [IN_PLACE] * (1 + len(up)),
         out_specs=[IN_PLACE] * len(up),
-        scratch_shapes=[pltpu.SemaphoreType.DMA((len(up),))],
+        scratch_shapes=passage(len(up), rows, width),
         out_shape=[jax.ShapeDtypeStruct((rows, width), jnp.float32)] * len(up),
         name="choose",
         cost_estimate=LIGHT,
     )(place, source, *up))
 
 
-def paste_kernel(parts, place_ref, arrived, before, out, sems):
+def paste_kernel(parts, place_ref, arrived, before, out, buffer, sems):
     cells, half = arrived.shape
     rows = cells // parts
     left = pl.multiple_of((1 - place_ref[0]) * half, 128)
-    copies = []
-    for i in range(parts):
-        at = pl.ds(i * rows, rows)
-        copies.append(pltpu.make_async_copy(
-            arrived.at[at, :], out.at[at, pl.ds(left, half)], sems.at[i]
-        ))
-    run(copies)
+    bands = [pl.ds(i * rows, rows) for i in range(parts)]
+    through(buffer, sems, [(arrived.at[at, :], out.at[at, pl.ds(left, half)]) for at in bands])
 
 
 def paste(arrived, whole, place):
-    parts = 4
-    return pl.pallas_call(
-        functools.partial(paste_kernel, parts),
-        in_specs=[
-            pl.BlockSpec(memory_space=pltpu.SMEM),
-            IN_PLACE,
-            IN_PLACE,
-        ],
+    cells, half = arrived.shape
+    return pl.pallas_call(
+        functools.partial(paste_kernel, PARTS),
+        in_specs=[pl.BlockSpec(memory_space=pltpu.SMEM), IN_PLACE, IN_PLACE],
         out_specs=IN_PLACE,
-        scratch_shapes=[pltpu.SemaphoreType.DMA((parts,))],
+        scratch_shapes=passage(PARTS, cells // PARTS, half),
         out_shape=jax.ShapeDtypeStruct(whole.shape, jnp.float32),
         input_output_aliases={2: 0},
         name="paste",
@@ -421,7 +419,7 @@
         h, p, w = k, k - 2, k - 4
         arrived, sort = exchange(kind, sent), kind
         if k == 0:
-            arrived[0], flux_parts[0] = together(arrived[0], flux_parts[0])
+            arrived[0], flux_parts = together(arrived[0], flux_parts)
         if k == 2:
             arrived[0], same[0] = together(arrived[0], same[0])
         if k + 1 < CHUNKS + 4:

time: 1310 us -> 431 us (0.33)
  Pallas kernels: 1120 us -> 204 us
  waiting for transfers between devices: 103 us -> 164 us
  starting transfers between devices: 50.2 us -> 35.6 us
    pallas_call x4, Pallas kernels: 290 us -> 10.4 us  [stack(): pl.pallas_call(stack_kernel, in_specs=[IN_PLACE] * len(pieces), out_specs...]
    pallas_call x4, Pallas kernels: 293 us -> 13.1 us  [choose(): pl.pallas_call(functools.partial(choose_kernel, r), in_specs=[pl.BlockSpe...]
    pallas_call x3, Pallas kernels: 242 us -> 8.83 us  [cut(): pl.pallas_call(functools.partial(cut_kernel, lags, r), in_specs=[IN_PLACE...]
    pallas_call x2, Pallas kernels: 134 us -> 8.62 us  [the longest x1 4.37 us: side_of(): pl.pallas_call(functools.partial(side_kernel, PARTS), in_specs=[pl.BlockS...]
    ppermute x12, waiting for transfers between devices: 16.6 us -> 65.2 us  [shifted(): return lax.ppermute(value, 'tm', pairs)]
  transfers between devices with their start and end apart: 35 -> 35, of which waited for: 5 -> 9; matrix products, arithmetic and copies ran while one was open for 0% -> 0% of each run, Pallas kernels for 52% -> 39%
where the time goes in v1:
time: 431 us; the launch traced here: 430 us
  Pallas kernels  204 us (47%)
  waiting for transfers between devices  164 us (38%)
  starting transfers between devices  35.6 us (8%)
  between operations  14.2 us (3%)
  local copies, waits for them, and re-layouts  9.94 us (2%)
    psum x4, waiting for transfers between devices, on_device(): weighted.append(lax.psum(total, 'z'))  97.6 us
    pallas_call x5, Pallas kernels, adjoint(): pl.pallas_call(functools.partial(adjoint_kernel, count, len(sides), first...  72.6 us
    pallas_call x5, Pallas kernels, forward(): pl.pallas_call(functools.partial(forward_kernel, count), grid=(half // ti...  67.5 us
    ppermute x12, waiting for transfers between devices, shifted(): return lax.ppermute(value, 'tm', pairs)  65.2 us
    ppermute x12, starting transfers between devices, shifted(): return lax.ppermute(value, 'tm', pairs)  18.4 us
    pallas_call x4, Pallas kernels, combine(): pl.pallas_call(combine_kernel, grid_spec=pltpu.PrefetchScalarGridSpec(num...  13.8 us
    pallas_call x4, Pallas kernels, choose(): pl.pallas_call(functools.partial(choose_kernel, r), in_specs=[pl.BlockSpe...  13.1 us
    ppermute x12, starting transfers between devices, cycled(): lax.ppermute(value, 'tm', [(i, (i - by) % devices) for i in range(devices)])  11.8 us
  transfers between devices with their start and end apart: 35, of which 9 were waited for; matrix products, arithmetic and copies ran while one was open for 0% of the time, Pallas kernels for 39%

profile of v1, /device:TPU:3, one launch (start us, length us, event | category | flops | bytes accessed | tf_op | source)
XLA Modules:
  0.0 429.5 jit_solution(9361699230455342150)
XLA Ops:
  6.5 2.7 cut.4
  9.8 4.4 %side.1 = f32[1024,1024]{1,0:T(8,128)} custom-call(s32[3]{0:T(128)} %pad_add_fusion.place_ref.core_ref, f32[1,1024,2048]{2,1,0:T(8,128)} %own), custom_call_target="tpu_custom_call" | custom-call | flops 1 | bytes 1 | tf_op jit(solution)/shard_map/side/pallas_call | solution.py:245
  17.0 1.9 collective-permute-start.4
  18.9 2.6 cut.5
  21.5 32.2 %collective-permute-done.5.refs_1_.refs_6_ = f32[192,1024]{1,0:T(8,128)S(1)} collective-permute-done((f32[192,1024]{1,0:T(8,128)}, f32[192,1024]{1,0:T(8,128)S(1)}, u32[]{:S(2)}, u32[]{:S(2)}) %collective-permute-start.5) | collective-permute-done | bytes 786464 | tf_op jit(solution)/shard_map/ppermute | solution.py:22
  53.8 9.2 %split.1.refs_8_.refs_6_ = bf16[6144,1024]{1,0:T(8,128)(2,1)} custom-call(s32[3]{0:T(128)} %pad_add_fusion.place_ref.core_ref, f32[1,1024,2048]{2,1,0:T(8,128)} %own, f32[1024,1024]{1,0:T(8,128)} %collective-permute-done.1.other), custom_call_target="tpu_custom_call" | custom-call | flops 1 | bytes 1 | tf_op jit(solution)/shard_map/split/pallas_call | solution.py:60
  63.9 2.6 stack.16
  67.4 1.6 collective-permute-start.3
  68.9 1.9 collective-permute-start.8
  72.2 3.6 cut.3
  75.8 12.9 %forward.6 = (f32[192,1024]{1,0:T(8,128)}, f32[192,1024]{1,0:T(8,128)}, f32[192,1024]{1,0:T(8,128)}) custom-call(f32[192,1024]{1,0:T(8,128)} %copy-done.6, f32[192,1024]{1,0:T(8,128)} %copy-done.5, f32[192,1024]{1,0:T(8,128)} %copy-done.4, f32[576,1024]{1,0:T(8,128)} %collective-permute-done.6.refs_3_.refs_4_.refs_5_.refs_9_.refs_10_.refs_11_, ...), custom_call_target="tpu_custom_call" | custom-call | flops 1 | bytes 1 | tf_op jit(solution)/shard_map/forward/pallas_call | solution.py:101
  88.7 3.2 choose.4
  92.0 16.4 %collective-permute-done.9.refs_1_.refs_6_ = f32[192,1024]{1,0:T(8,128)} collective-permute-done((f32[192,1024]{1,0:T(8,128)}, f32[192,1024]{1,0:T(8,128)}, u32[]{:S(2)}, u32[]{:S(2)}) %collective-permute-start.9) | collective-permute-done | bytes 786464 | tf_op jit(solution)/shard_map/ppermute | solution.py:22
  108.4 2.6 stack.17
  111.6 2.4 collective-permute-start.7
  113.9 1.6 copy-done
  115.6 16.0 %forward.5 = (f32[192,1024]{1,0:T(8,128)}, f32[192,1024]{1,0:T(8,128)}, f32[192,1024]{1,0:T(8,128)}, f32[192,1024]{1,0:T(8,128)}) custom-call(f32[1,4,768,1024]{3,2,1,0:T(8,128)} %refs_4_.7, f32[1,4,768,1024]{3,2,1,0:T(8,128)} %refs_4_.7, f32[1,4,768,1024]{3,2,1,0:T(8,128)} %refs_4_.7, f32[1,4,768,1024]{3,2,1,0:T(8,128)} %refs_4_.7, f32[768,1024]{1,0:T(8,128)} %copy-done, ...), custom_call_target="tpu_custom_call" | custom-call | flops 1 | bytes 1 | tf_op jit(solution)/shard_map/forward/pallas_call | solution.py:101
  131.9 12.8 %forward.7 = (f32[192,1024]{1,0:T(8,128)}, f32[192,1024]{1,0:T(8,128)}, f32[192,1024]{1,0:T(8,128)}) custom-call(f32[192,1024]{1,0:T(8,128)} %collective-permute-done.8.refs_0_.refs_5_, f32[192,1024]{1,0:T(8,128)} %collective-permute-done.9.refs_1_.refs_6_, f32[192,1024]{1,0:T(8,128)} %collective-permute-done.3.refs_2_.refs_7_, ...), custom_call_target="tpu_custom_call" | custom-call | flops 1 | bytes 1 | tf_op jit(solution)/shard_map/forward/pallas_call | solution.py:101
  144.8 3.3 choose.5
  149.1 2.6 stack.18
  153.9 3.5 combine.4
  157.4 1.5 collective-permute-start.11
  161.1 12.8 %forward.8 = (f32[192,1024]{1,0:T(8,128)}, f32[192,1024]{1,0:T(8,128)}, f32[192,1024]{1,0:T(8,128)}) custom-call(f32[192,1024]{1,0:T(8,128)} %collective-permute-done.12.refs_2_.refs_0_.refs_5_, f32[192,1024]{1,0:T(8,128)} %collective-permute-done.13.refs_1_.refs_6_, f32[192,1024]{1,0:T(8,128)} %collective-permute-done.7.refs_0_.refs_2_.refs_7_, ...), custom_call_target="tpu_custom_call" | custom-call | flops 1 | bytes 1 | tf_op jit(solution)/shard_map/forward/pallas_call | solution.py:101
  173.9 28.0 %all-reduce.5.cloned.1.call-done.source.refs_0_ = f32[192,1024]{1,0:T(8,128)} async-done(((f32[192,1024]{1,0:T(8,128)}), f32[192,1024]{1,0:T(8,128)}) %all-reduce.5.cloned.1.call-update) | async-done | bytes 786448 | tf_op jit(solution)/shard_map/psum | solution.py:438
  201.8 3.3 choose.6
  206.0 2.6 stack.19
  209.5 3.4 combine.5
  213.0 1.6 collective-permute-start.15
  217.6 13.0 %forward.9 = (f32[192,1024]{1,0:T(8,128)}, f32[192,1024]{1,0:T(8,128)}, f32[192,1024]{1,0:T(8,128)}) custom-call(f32[192,1024]{1,0:T(8,128)} %collective-permute-done.17.refs_2_.refs_0_.refs_5_, f32[192,1024]{1,0:T(8,128)} %collective-permute-done.16.refs_1_.refs_6_, f32[192,1024]{1,0:T(8,128)} %copy-done.3, f32[576,1024]{1,0:T(8,128)} %copy-done.1, ...), custom_call_target="tpu_custom_call" | custom-call | flops 1 | bytes 1 | tf_op jit(solution)/shard_map/forward/pallas_call | solution.py:101
  230.6 25.3 %all-reduce.7.cloned.1.call-done.source.refs_0_ = f32[192,1024]{1,0:T(8,128)} async-done(((f32[192,1024]{1,0:T(8,128)}), f32[192,1024]{1,0:T(8,128)}) %all-reduce.7.cloned.1.call-update) | async-done | bytes 786448 | tf_op jit(solution)/shard_map/psum | solution.py:438
  255.9 3.3 choose.7
  260.1 3.5 combine.6
  264.0 1.5 collective-permute-start.22
  265.5 2.2 collective-permute-start.19
  267.7 16.1 %adjoint.5 = (f32[1024,2048]{1,0:T(8,128)}, f32[1024,1024]{1,0:T(8,128)}) custom-call(s32[3]{0:T(128)} %pad_add_fusion.place_ref.core_ref, f32[192,1024]{1,0:T(8,128)} %all-reduce.5.cloned.1.call-done.source.refs_0_, f32[192,1024]{1,0:T(8,128)} %collective-permute-done.21.refs_2_.refs_1_, f32[192,1024]{1,0:T(8,128)} %collective-permute-done.20.refs_1_.refs_2_, ...), custom_call_target="tpu_custom_call" | custom-call | flops 1 | bytes 1 | tf_op jit(solution)/shard_map/adjoint/pallas_call | solution.py:159
  283.8 23.4 %all-reduce.9.cloned.1.call-done.refs_0_ = f32[192,1024]{1,0:T(8,128)} async-done(((f32[192,1024]{1,0:T(8,128)}), f32[192,1024]{1,0:T(8,128)}) %all-reduce.9.cloned.1.call-update) | async-done | bytes 786448 | tf_op jit(solution)/shard_map/psum | solution.py:438
  308.6 3.5 combine.7
  312.1 1.6 collective-permute-start.28
  314.9 2.2 collective-permute-start.24
  317.1 17.3 %adjoint.6 = (f32[1024,2048]{1,0:T(8,128)}, f32[1024,1024]{1,0:T(8,128)}) custom-call(s32[3]{0:T(128)} %pad_add_fusion.place_ref.core_ref, f32[192,1024]{1,0:T(8,128)} %all-reduce.7.cloned.1.call-done.source.refs_0_, f32[192,1024]{1,0:T(8,128)} %copy-done.11, f32[192,1024]{1,0:T(8,128)} %copy-done.12, ...), custom_call_target="tpu_custom_call", output_to_operand_aliasing={{0}: (13, {}), {1}: (14, {})} | custom-call | flops 1 | bytes 1 | tf_op jit(solution)/shard_map/adjoint/pallas_call | solution.py:159
  334.4 20.8 %all-reduce.11.cloned.1.call-done.refs_0_ = f32[192,1024]{1,0:T(8,128)} async-done(((f32[192,1024]{1,0:T(8,128)}), f32[192,1024]{1,0:T(8,128)}) %all-reduce.11.cloned.1.call-update) | async-done | bytes 786448 | tf_op jit(solution)/shard_map/psum | solution.py:438
  357.3 2.8 collective-permute-start.25
  360.1 17.2 %adjoint.7 = (f32[1024,2048]{1,0:T(8,128)}, f32[1024,1024]{1,0:T(8,128)}) custom-call(s32[3]{0:T(128)} %pad_add_fusion.place_ref.core_ref, f32[192,1024]{1,0:T(8,128)} %all-reduce.9.cloned.1.call-done.refs_0_, f32[192,1024]{1,0:T(8,128)} %collective-permute-done.24.refs_1_, ...), custom_call_target="tpu_custom_call", output_to_operand_aliasing={{0}: (13, {}), {1}: (14, {})} | custom-call | flops 1 | bytes 1 | tf_op jit(solution)/shard_map/adjoint/pallas_call | solution.py:159
  377.3 16.5 %collective-permute-done.27.refs_2_ = f32[192,1024]{1,0:T(8,128)S(1)} collective-permute-done((f32[192,1024]{1,0:T(8,128)}, f32[192,1024]{1,0:T(8,128)S(1)}, u32[]{:S(2)}, u32[]{:S(2)}) %collective-permute-start.27) | collective-permute-done | bytes 786464 | tf_op jit(solution)/shard_map/ppermute | solution.py:22
  395.0 11.0 %adjoint.8 = f32[1024,1024]{1,0:T(8,128)} custom-call(s32[3]{0:T(128)} %pad_add_fusion.place_ref.core_ref, f32[192,1024]{1,0:T(8,128)} %all-reduce.11.cloned.1.call-done.refs_0_, f32[192,1024]{1,0:T(8,128)} %copy-done.9, f32[192,1024]{1,0:T(8,128)} %copy-done.8, f32[192,1024]{1,0:T(8,128)} %copy-done.7, ...), custom_call_target="tpu_custom_call", output_to_operand_aliasing={{}: (9, {})} | custom-call | flops 1 | bytes 1 | tf_op jit(solution)/shard_map/adjoint/pallas_call | solution.py:159
  406.1 1.6 collective-permute-start.30
  407.7 11.0 %adjoint.9.before = f32[1024,2048]{1,0:T(8,128)} custom-call(s32[3]{0:T(128)} %pad_add_fusion.place_ref.core_ref, f32[192,1024]{1,0:T(8,128)} %all-reduce.11.cloned.1.call-done.refs_0_, f32[192,1024]{1,0:T(8,128)} %copy-done.9, f32[192,1024]{1,0:T(8,128)} %copy-done.8, f32[192,1024]{1,0:T(8,128)} %copy-done.7, ...), custom_call_target="tpu_custom_call", output_to_operand_aliasing={{}: (9, {})} | custom-call | flops 1 | bytes 1 | tf_op jit(solution)/shard_map/adjoint/pallas_call | solution.py:159
  418.7 4.2 paste.1
  (91 shorter events, 23.9 us)
Async XLA Ops:
  6.5 195.3 %all-reduce.5.cloned.1.call-start = ((), (), s32[]{:S(2)}) async-start(), calls=%async_computation | async-start | bytes 1572864 | tf_op jit(solution)/shard_map/psum | solution.py:438
  9.8 7.1 %copy-start.16 = (f32[192,1024]{1,0:T(8,128)S(1)}, f32[192,1024]{1,0:T(8,128)}, u32[]{:S(2)}) copy-start(f32[192,1024]{1,0:T(8,128)} %get-tuple-element.109) | copy-start | bytes 2359300
  14.2 39.6 %collective-permute-start.1 = (f32[1024,1024]{1,0:T(8,128)}, f32[1024,1024]{1,0:T(8,128)}, u32[]{:S(2)}, u32[]{:S(2)}) collective-permute-start(f32[1024,1024]{1,0:T(8,128)} %side.1), channel_id=1, source_target_pairs={{0,1},{1,0},{2,3},{3,2},{4,5},{5,4},{6,7},{7,6},{8,9},{9,8},{10,11... | collective-permute-start | bytes 12582920 | tf_op jit(solution)/shard_map/ppermute | solution.py:31
  15.0 6.6 %collective-permute-start.2 = (f32[192,1024]{1,0:T(8,128)}, f32[192,1024]{1,0:T(8,128)S(1)}, u32[]{:S(2)}, u32[]{:S(2)}) collective-permute-start(f32[192,1024]{1,0:T(8,128)} %get-tuple-element.106), channel_id=1, source_target_pairs={{24,0},{25,1},{26,2},{27,3},{28,4},{29,5},{30,6},{31,7}} | collective-permute-start | bytes 2359304 | tf_op jit(solution)/shard_map/ppermute | solution.py:22
  15.7 38.1 %collective-permute-start.5 = (f32[192,1024]{1,0:T(8,128)}, f32[192,1024]{1,0:T(8,128)S(1)}, u32[]{:S(2)}, u32[]{:S(2)}) collective-permute-start(f32[192,1024]{1,0:T(8,128)} %get-tuple-element.113), channel_id=1, source_target_pairs={{16,0},{24,8},{17,1},{25,9},{18,2},{26,10},{19,3},{27,11},{20,4},{... | collective-permute-start | bytes 2359304 | tf_op jit(solution)/shard_map/ppermute | solution.py:22
  17.0 46.0 %collective-permute-start.4 = (f32[192,1024]{1,0:T(8,128)S(1)}, f32[192,1024]{1,0:T(8,128)S(1)}, u32[]{:S(2)}, u32[]{:S(2)}) collective-permute-start(f32[192,1024]{1,0:T(8,128)S(1)} %copy-done.16), channel_id=1, source_target_pairs={{8,0},{16,8},{24,16},{9,1},{17,9},{25,17},{10,2},{18,10},{26,18},{... | collective-permute-start | bytes 2359304 | tf_op jit(solution)/shard_map/ppermute | solution.py:22
  21.5 41.5 %copy-start.4 = (f32[192,1024]{1,0:T(8,128)}, f32[192,1024]{1,0:T(8,128)S(1)}, u32[]{:S(2)}) copy-start(f32[192,1024]{1,0:T(8,128)S(1)} %collective-permute-done.2.refs_2_.refs_7_) | copy-start | bytes 2359300
  53.8 9.2 %copy-start.5 = (f32[192,1024]{1,0:T(8,128)}, f32[192,1024]{1,0:T(8,128)S(1)}, u32[]{:S(2)}) copy-start(f32[192,1024]{1,0:T(8,128)S(1)} %collective-permute-done.5.refs_1_.refs_6_) | copy-start | bytes 2359300
  63.0 0.9 copy-start.6
  66.5 9.3 %collective-permute-start.6 = (f32[576,1024]{1,0:T(8,128)}, f32[576,1024]{1,0:T(8,128)}, u32[]{:S(2)}, u32[]{:S(2)}) collective-permute-start(f32[576,1024]{1,0:T(8,128)} %stack.16), channel_id=1, source_target_pairs={{0,1},{1,0},{2,3},{3,2},{4,5},{5,4},{6,7},{7,6},{8,9},{9,8},{10,11... | collective-permute-start | bytes 7077896 | tf_op jit(solution)/shard_map/ppermute | solution.py:31
  67.4 24.6 %collective-permute-start.3 = (f32[192,1024]{1,0:T(8,128)}, f32[192,1024]{1,0:T(8,128)}, u32[]{:S(2)}, u32[]{:S(2)}) collective-permute-start(f32[192,1024]{1,0:T(8,128)} %get-tuple-element.108), channel_id=1, source_target_pairs={{24,0},{25,1},{26,2},{27,3},{28,4},{29,5},{30,6},{31,7}} | collective-permute-start | bytes 2359304 | tf_op jit(solution)/shard_map/ppermute | solution.py:22
  68.9 23.1 %collective-permute-start.8 = (f32[192,1024]{1,0:T(8,128)}, f32[192,1024]{1,0:T(8,128)}, u32[]{:S(2)}, u32[]{:S(2)}) collective-permute-start(f32[192,1024]{1,0:T(8,128)} %get-tuple-element.123), channel_id=1, source_target_pairs={{8,0},{16,8},{24,16},{9,1},{17,9},{25,17},{10,2},{18,10},{26,18},{... | collective-permute-start | bytes 2359304 | tf_op jit(solution)/shard_map/ppermute | solution.py:22
  70.9 37.6 %collective-permute-start.9 = (f32[192,1024]{1,0:T(8,128)}, f32[192,1024]{1,0:T(8,128)}, u32[]{:S(2)}, u32[]{:S(2)}) collective-permute-start(f32[192,1024]{1,0:T(8,128)} %get-tuple-element.126), channel_id=1, source_target_pairs={{16,0},{24,8},{17,1},{25,9},{18,2},{26,10},{19,3},{27,11},{20,4},{... | collective-permute-start | bytes 2359304 | tf_op jit(solution)/shard_map/ppermute | solution.py:22
  75.7 38.2 %collective-permute-start = (f32[768,1024]{1,0:T(8,128)}, f32[768,1024]{1,0:T(8,128)S(1)}, u32[]{:S(2)}, u32[]{:S(2)}) collective-permute-start(f32[768,1024]{1,0:T(8,128)} %cut.3), channel_id=1, source_target_pairs={{0,1},{1,0},{2,3},{3,2},{4,5},{5,4},{6,7},{7,6},{8,9},{9,8},{10,11... | collective-permute-start | bytes 9437192 | tf_op jit(solution)/shard_map/ppermute | solution.py:31
  111.1 20.9 %collective-permute-start.10 = (f32[576,1024]{1,0:T(8,128)}, f32[576,1024]{1,0:T(8,128)}, u32[]{:S(2)}, u32[]{:S(2)}) collective-permute-start(f32[576,1024]{1,0:T(8,128)} %stack.17), channel_id=1, source_target_pairs={{0,1},{1,0},{2,3},{3,2},{4,5},{5,4},{6,7},{7,6},{8,9},{9,8},{10,11... | collective-permute-start | bytes 7077896 | tf_op jit(solution)/shard_map/ppermute | solution.py:31
  111.6 20.4 %collective-permute-start.12 = (f32[192,1024]{1,0:T(8,128)}, f32[192,1024]{1,0:T(8,128)}, u32[]{:S(2)}, u32[]{:S(2)}) collective-permute-start(f32[192,1024]{1,0:T(8,128)} %get-tuple-element.135), channel_id=1, source_target_pairs={{0,24},{8,0},{16,8},{24,16},{1,25},{9,1},{17,9},{25,17},{2,26},{10... | collective-permute-start | bytes 2359304 | tf_op jit(solution)/shard_map/ppermute | solution.py:27
  111.6 36.5 %collective-permute-start.7 = (f32[192,1024]{1,0:T(8,128)}, f32[192,1024]{1,0:T(8,128)}, u32[]{:S(2)}, u32[]{:S(2)}) collective-permute-start(f32[192,1024]{1,0:T(8,128)} %get-tuple-element.122), channel_id=1, source_target_pairs={{0,8},{8,16},{16,24},{24,0},{1,9},{9,17},{17,25},{25,1},{2,10},{10... | collective-permute-start | bytes 2359304 | tf_op jit(solution)/shard_map/ppermute | solution.py:27
  113.9 35.2 %collective-permute-start.13 = (f32[192,1024]{1,0:T(8,128)}, f32[192,1024]{1,0:T(8,128)}, u32[]{:S(2)}, u32[]{:S(2)}) collective-permute-start(f32[192,1024]{1,0:T(8,128)} %get-tuple-element.139), channel_id=1, source_target_pairs={{0,16},{8,24},{16,0},{24,8},{1,17},{9,25},{17,1},{25,9},{2,18},{10... | collective-permute-start | bytes 2359304 | tf_op jit(solution)/shard_map/ppermute | solution.py:27
  113.9 1.7 copy-start
  148.1 4.8 %copy-start.15 = (f32[1,768]{1,0:T(1,128)S(1)}, f32[1,768]{1,0:T(1,128)}, u32[]{:S(2)}) copy-start(f32[1,768]{1,0:T(1,128)} %param.6) | copy-start | bytes 9220
  151.7 7.9 %collective-permute-start.14 = (f32[576,1024]{1,0:T(8,128)}, f32[576,1024]{1,0:T(8,128)S(1)}, u32[]{:S(2)}, u32[]{:S(2)}) collective-permute-start(f32[576,1024]{1,0:T(8,128)} %stack.18), channel_id=1, source_target_pairs={{0,1},{1,0},{2,3},{3,2},{4,5},{5,4},{6,7},{7,6},{8,9},{9,8},{10,11... | collective-permute-start | bytes 7077896 | tf_op jit(solution)/shard_map/ppermute | solution.py:31
  157.4 98.5 %all-reduce.7.cloned.1.call-start = ((), (), s32[]{:S(2)}) async-start(), calls=%async_computation.1 | async-start | bytes 1572864 | tf_op jit(solution)/shard_map/psum | solution.py:438
  157.4 47.7 %collective-permute-start.11 = (f32[192,1024]{1,0:T(8,128)}, f32[192,1024]{1,0:T(8,128)S(1)}, u32[]{:S(2)}, u32[]{:S(2)}) collective-permute-start(f32[192,1024]{1,0:T(8,128)} %get-tuple-element.134), channel_id=1, source_target_pairs={{0,8},{8,16},{16,24},{24,0},{1,9},{9,17},{17,25},{25,1},{2,10},{10... | collective-permute-start | bytes 2359304 | tf_op jit(solution)/shard_map/ppermute | solution.py:27
  159.0 46.2 %collective-permute-start.16 = (f32[192,1024]{1,0:T(8,128)}, f32[192,1024]{1,0:T(8,128)}, u32[]{:S(2)}, u32[]{:S(2)}) collective-permute-start(f32[192,1024]{1,0:T(8,128)} %get-tuple-element.152), channel_id=1, source_target_pairs={{0,16},{8,24},{16,0},{24,8},{1,17},{9,25},{17,1},{25,9},{2,18},{10... | collective-permute-start | bytes 2359304 | tf_op jit(solution)/shard_map/ppermute | solution.py:27
  159.2 45.9 %collective-permute-start.17 = (f32[192,1024]{1,0:T(8,128)}, f32[192,1024]{1,0:T(8,128)}, u32[]{:S(2)}, u32[]{:S(2)}) collective-permute-start(f32[192,1024]{1,0:T(8,128)} %get-tuple-element.155), channel_id=1, source_target_pairs={{0,24},{8,0},{16,8},{24,16},{1,25},{9,1},{17,9},{25,17},{2,26},{10... | collective-permute-start | bytes 2359304 | tf_op jit(solution)/shard_map/ppermute | solution.py:27
  159.6 1.4 copy-start.2
  208.6 7.5 %collective-permute-start.18 = (f32[576,1024]{1,0:T(8,128)}, f32[576,1024]{1,0:T(8,128)S(1)}, u32[]{:S(2)}, u32[]{:S(2)}) collective-permute-start(f32[576,1024]{1,0:T(8,128)} %stack.19), channel_id=1, source_target_pairs={{0,1},{1,0},{2,3},{3,2},{4,5},{5,4},{6,7},{7,6},{8,9},{9,8},{10,11... | collective-permute-start | bytes 7077896 | tf_op jit(solution)/shard_map/ppermute | solution.py:31
  212.9 94.3 %all-reduce.9.cloned.1.call-start = ((), (), s32[]{:S(2)}) async-start(), calls=%async_computation.2 | async-start | bytes 1572864 | tf_op jit(solution)/shard_map/psum | solution.py:438
  213.0 46.2 %collective-permute-start.15 = (f32[192,1024]{1,0:T(8,128)}, f32[192,1024]{1,0:T(8,128)S(1)}, u32[]{:S(2)}, u32[]{:S(2)}) collective-permute-start(f32[192,1024]{1,0:T(8,128)} %get-tuple-element.149), channel_id=1, source_target_pairs={{0,8},{8,16},{16,24},{24,0},{1,9},{9,17},{17,25},{25,1},{2,10},{10... | collective-permute-start | bytes 2359304 | tf_op jit(solution)/shard_map/ppermute | solution.py:27
  214.6 44.7 %collective-permute-start.20 = (f32[192,1024]{1,0:T(8,128)}, f32[192,1024]{1,0:T(8,128)}, u32[]{:S(2)}, u32[]{:S(2)}) collective-permute-start(f32[192,1024]{1,0:T(8,128)} %get-tuple-element.166), channel_id=1, source_target_pairs={{0,16},{8,24},{16,0},{24,8},{1,17},{9,25},{17,1},{25,9},{2,18},{10... | collective-permute-start | bytes 2359304 | tf_op jit(solution)/shard_map/ppermute | solution.py:27
  214.7 44.5 %collective-permute-start.21 = (f32[192,1024]{1,0:T(8,128)}, f32[192,1024]{1,0:T(8,128)}, u32[]{:S(2)}, u32[]{:S(2)}) collective-permute-start(f32[192,1024]{1,0:T(8,128)} %get-tuple-element.169), channel_id=1, source_target_pairs={{0,24},{8,0},{16,8},{24,16},{1,25},{9,1},{17,9},{25,17},{2,26},{10... | collective-permute-start | bytes 2359304 | tf_op jit(solution)/shard_map/ppermute | solution.py:27
  216.1 1.5 copy-start.1
  263.6 91.7 %all-reduce.11.cloned.1.call-start = ((), (), s32[]{:S(2)}) async-start(), calls=%async_computation.3 | async-start | bytes 1572864 | tf_op jit(solution)/shard_map/psum | solution.py:438
  263.6 43.6 %collective-permute-start.23 = (f32[192,1024]{1,0:T(8,128)}, f32[192,1024]{1,0:T(8,128)S(1)}, u32[]{:S(2)}, u32[]{:S(2)}) collective-permute-start(f32[192,1024]{1,0:T(8,128)} %get-tuple-element.179), channel_id=1, source_target_pairs={{0,24},{8,0},{16,8},{24,16},{1,25},{9,1},{17,9},{25,17},{2,26},{10... | collective-permute-start | bytes 2359304 | tf_op jit(solution)/shard_map/ppermute | solution.py:27
  264.0 43.3 %collective-permute-start.22 = (f32[192,1024]{1,0:T(8,128)}, f32[192,1024]{1,0:T(8,128)S(1)}, u32[]{:S(2)}, u32[]{:S(2)}) collective-permute-start(f32[192,1024]{1,0:T(8,128)} %get-tuple-element.177), channel_id=1, source_target_pairs={{0,16},{8,24},{16,0},{24,8},{1,17},{9,25},{17,1},{25,9},{2,18},{10... | collective-permute-start | bytes 2359304 | tf_op jit(solution)/shard_map/ppermute | solution.py:27
  265.5 41.7 %collective-permute-start.19 = (f32[192,1024]{1,0:T(8,128)}, f32[192,1024]{1,0:T(8,128)S(1)}, u32[]{:S(2)}, u32[]{:S(2)}) collective-permute-start(f32[192,1024]{1,0:T(8,128)} %get-tuple-element.163), channel_id=1, source_target_pairs={{0,8},{8,16},{16,24},{24,0},{1,9},{9,17},{17,25},{25,1},{2,10},{10... | collective-permute-start | bytes 2359304 | tf_op jit(solution)/shard_map/ppermute | solution.py:27
  307.2 4.9 %copy-start.14 = (f32[192,1024]{1,0:T(8,128)S(1)}, f32[192,1024]{1,0:T(8,128)}, u32[]{:S(2)}) copy-start(f32[192,1024]{1,0:T(8,128)} %all-reduce.9.cloned.1.call-done.refs_0_) | copy-start | bytes 2359300
  307.2 1.2 copy-start.12
  307.2 1.4 copy-start.13
  312.1 43.1 %collective-permute-start.28 = (f32[192,1024]{1,0:T(8,128)S(1)}, f32[192,1024]{1,0:T(8,128)}, u32[]{:S(2)}, u32[]{:S(2)}) collective-permute-start(f32[192,1024]{1,0:T(8,128)S(1)} %copy-done.14), channel_id=1, source_target_pairs={{24,0},{25,1},{26,2},{27,3},{28,4},{29,5},{30,6},{31,7}} | collective-permute-start | bytes 2359304 | tf_op jit(solution)/shard_map/ppermute | solution.py:22
  313.7 42.3 %collective-permute-start.26 = (f32[192,1024]{1,0:T(8,128)S(1)}, f32[192,1024]{1,0:T(8,128)}, u32[]{:S(2)}, u32[]{:S(2)}) collective-permute-start(f32[192,1024]{1,0:T(8,128)S(1)} %copy-done.14), channel_id=1, source_target_pairs={{16,0},{24,8},{17,1},{25,9},{18,2},{26,10},{19,3},{27,11},{20,4},{... | collective-permute-start | bytes 2359304 | tf_op jit(solution)/shard_map/ppermute | solution.py:22
  314.9 42.3 %collective-permute-start.24 = (f32[192,1024]{1,0:T(8,128)S(1)}, f32[192,1024]{1,0:T(8,128)}, u32[]{:S(2)}, u32[]{:S(2)}) collective-permute-start(f32[192,1024]{1,0:T(8,128)S(1)} %copy-done.14), channel_id=1, source_target_pairs={{8,0},{16,8},{24,16},{9,1},{17,9},{25,17},{10,2},{18,10},{26,18},{... | collective-permute-start | bytes 2359304 | tf_op jit(solution)/shard_map/ppermute | solution.py:22
  355.3 22.1 %collective-permute-start.29 = (f32[192,1024]{1,0:T(8,128)}, f32[192,1024]{1,0:T(8,128)S(1)}, u32[]{:S(2)}, u32[]{:S(2)}) collective-permute-start(f32[192,1024]{1,0:T(8,128)} %all-reduce.11.cloned.1.call-done.refs_0_), channel_id=1, source_target_pairs={{24,0},{25,1},{26,2},{27,3},{28,4},{29,5},{30,6},{31,7}} | collective-permute-start | bytes 2359304 | tf_op jit(solution)/shard_map/ppermute | solution.py:22
  356.0 37.9 %collective-permute-start.27 = (f32[192,1024]{1,0:T(8,128)}, f32[192,1024]{1,0:T(8,128)S(1)}, u32[]{:S(2)}, u32[]{:S(2)}) collective-permute-start(f32[192,1024]{1,0:T(8,128)} %all-reduce.11.cloned.1.call-done.refs_0_), channel_id=1, source_target_pairs={{16,0},{24,8},{17,1},{25,9},{18,2},{26,10},{19,3},{27,11},{20,4},{... | collective-permute-start | bytes 2359304 | tf_op jit(solution)/shard_map/ppermute | solution.py:22
  357.3 36.6 %collective-permute-start.25 = (f32[192,1024]{1,0:T(8,128)}, f32[192,1024]{1,0:T(8,128)S(1)}, u32[]{:S(2)}, u32[]{:S(2)}) collective-permute-start(f32[192,1024]{1,0:T(8,128)} %all-reduce.11.cloned.1.call-done.refs_0_), channel_id=1, source_target_pairs={{8,0},{16,8},{24,16},{9,1},{17,9},{25,17},{10,2},{18,10},{26,18},{... | collective-permute-start | bytes 2359304 | tf_op jit(solution)/shard_map/ppermute | solution.py:22
  377.3 16.6 %copy-start.7 = (f32[192,1024]{1,0:T(8,128)}, f32[192,1024]{1,0:T(8,128)S(1)}, u32[]{:S(2)}) copy-start(f32[192,1024]{1,0:T(8,128)S(1)} %collective-permute-done.29.refs_3_) | copy-start | bytes 2359300
  393.9 1.2 copy-start.9
  406.1 12.6 %collective-permute-start.30 = (f32[1024,1024]{1,0:T(8,128)}, f32[1024,1024]{1,0:T(8,128)}, u32[]{:S(2)}, u32[]{:S(2)}) collective-permute-start(f32[1024,1024]{1,0:T(8,128)} %adjoint.8), channel_id=1, source_target_pairs={{0,1},{1,0},{2,3},{3,2},{4,5},{5,4},{6,7},{7,6},{8,9},{9,8},{10,11... | collective-permute-start | bytes 12582920 | tf_op jit(solution)/shard_map/ppermute | solution.py:31
  (4 other events, 3.6 us)
Sparse Core Ops, SparseCore 0:
  157.5 44.2 all-reduce.4
  213.0 42.8 all-reduce.6
  263.7 43.4 all-reduce.8
  312.2 42.9 all-reduce.10

commit v2 on v1

--- a/solution.py
+++ b/solution.py
@@ -116,65 +116,89 @@
     return list(outs)
 
 
-def adjoint_kernel(count, sides, first, place_ref, *refs):
+def adjoint_kernel(count, sides, first, start, place_ref, counts_ref, *refs):
     weighted, refs = refs[:count], refs[count:]
     foot, refs = refs[:sides * count], refs[sides * count:]
     before, refs = (None, refs) if first else (refs[:sides], refs[sides:])
-    outs, parts_ref = refs[:sides], refs[sides]
+    outs, (high_ref, low_ref, foot_high, foot_low) = refs[:sides], refs[sides:]
     rows, tile = foot[0].shape[-2:]
-    depth = count * rows
-
-    @pl.when(pl.program_id(0) == 0)
-    def _():
+
+    taken, spots, filled = [], [], jnp.int32(0)
+    for i in range(count):
+        block = place_ref[1] + i
+        number = counts_ref[jnp.minimum(block, place_ref[2] - 1)]
+        taken.append(jnp.logical_and(block < place_ref[2], number > start))
+        spots.append(pl.multiple_of(filled * rows, rows))
+        filled = filled + taken[-1].astype(jnp.int32)
+
+    for i in range(count):
+        @pl.when(jnp.logical_and(taken[i], pl.program_id(0) == 0))
+        def _(i=i):
+            high, low = halves(weighted[i][...])
+            high_ref[pl.ds(spots[i], rows), :] = high
+            low_ref[pl.ds(spots[i], rows), :] = low
+
+    dims = ((0,), (0,))
+    for side in range(sides):
         for i in range(count):
-            value = jnp.where(place_ref[1] + i < place_ref[2], weighted[i][...], 0.0)
-            high, low = halves(value)
-            for block, part in enumerate((high, high, low)):
-                parts_ref[pl.ds(block * depth + i * rows, rows), :] = part
-
-    for side in range(sides):
-        mine = foot[side * count:(side + 1) * count]
-        slab = jnp.concatenate([ref[...].reshape(rows, tile) for ref in mine], axis=0)
-        high, low = halves(slab.T)
-        total = times(jnp.concatenate([high, low, high], axis=1), parts_ref[...], ((1,), (0,)))
-        if not first:
-            total = total + before[side][...]
-        outs[side][...] = total
-
-
-def adjoint(weighted, sides, core, cells):
+            @pl.when(taken[i])
+            def _(i=i):
+                high, low = halves(foot[side * count + i][...].reshape(rows, tile))
+                foot_high[side, pl.ds(spots[i], rows), :] = high
+                foot_low[side, pl.ds(spots[i], rows), :] = low
+
+    for number in range(count + 1):
+        @pl.when(filled == number)
+        def _(number=number):
+            at = pl.ds(0, number * rows)
+            for side in range(sides):
+                if number == 0:
+                    total = jnp.zeros(outs[side].shape, jnp.float32)
+                else:
+                    total = times(foot_high[side, at, :], high_ref[at, :], dims)
+                    total = total + times(foot_low[side, at, :], high_ref[at, :], dims)
+                    total = total + times(foot_high[side, at, :], low_ref[at, :], dims)
+                if not first:
+                    total = total + before[side][...]
+                outs[side][...] = total
+
+
+def adjoint(weighted, sides, start, place, counts, cells):
     count = len(weighted)
     rows, half = weighted[0].shape
-    tile = min(WIDE, cells)
+    tile = min(TILE, cells)
     first = sides[0][2] is None
     out_specs = []
     for side in sides:
         if side[4]:
-            out_specs.append(pl.BlockSpec((tile, half), lambda j, c: (j, c[0])))
+            out_specs.append(pl.BlockSpec((tile, half), lambda j, *c: (j, c[0][0])))
         else:
-            out_specs.append(pl.BlockSpec((tile, half), lambda j, c: (j, 0)))
+            out_specs.append(pl.BlockSpec((tile, half), lambda j, *c: (j, 0)))
     foot = [array for side in sides for array in side[0]]
     earlier = [] if first else [side[2] for side in sides]
-    at = 1 + count + len(foot)
-    return pl.pallas_call(
-        functools.partial(adjoint_kernel, count, len(sides), first),
+    at = 2 + count + len(foot)
+    return pl.pallas_call(
+        functools.partial(adjoint_kernel, count, len(sides), first, start),
         grid_spec=pltpu.PrefetchScalarGridSpec(
-            num_scalar_prefetch=1,
+            num_scalar_prefetch=2,
             grid=(cells // tile,),
             in_specs=[
-                *[pl.BlockSpec((rows, half), lambda j, c: (0, 0))] * count,
+                *[pl.BlockSpec((rows, half), lambda j, *c: (0, 0))] * count,
                 *[spec(tile) for side in sides for spec in side[1]],
                 *([] if first else out_specs),
             ],
             out_specs=out_specs,
-            scratch_shapes=[pltpu.VMEM((3 * count * rows, half), jnp.bfloat16)],
+            scratch_shapes=[
+                *[pltpu.VMEM((count * rows, half), jnp.bfloat16)] * 2,
+                *[pltpu.VMEM((len(sides), count * rows, tile), jnp.bfloat16)] * 2,
+            ],
         ),
         out_shape=[jax.ShapeDtypeStruct((cells, side[3]), jnp.float32) for side in sides],
         input_output_aliases={} if first else {at + i: i for i in range(len(sides))},
         compiler_params=pltpu.CompilerParams(vmem_limit_bytes=VMEM_LIMIT),
         name="adjoint",
         cost_estimate=LIGHT,
-    )(core, *weighted, *foot, *earlier)
+    )(place, counts, *weighted, *foot, *earlier)
 
 
 def through(buffer, sems, moves):
@@ -353,6 +377,7 @@
     valid = (jnp.arange(slots, dtype=jnp.int32) < obs_count[0]).astype(jnp.float32)
     row_scale = (valid * obs_weight[0])[:, None]
     later = range(1, lags)
+    counts = lax.all_gather(obs_count, "tm", tiled=True)
     paired = devices == lags and cells == half
 
     own, terms, weighted = [], [], []
@@ -360,10 +385,10 @@
     other_specs = [pl.BlockSpec((rows, cells), lambda j, i=i: (i, 0)) for i in range(len(later))]
 
     def row_block(r, lag):
-        return lambda tile: pl.BlockSpec((1, 1, rows, tile), lambda j, c: (0, lag, r, j))
+        return lambda tile: pl.BlockSpec((1, 1, rows, tile), lambda j, *c: (0, lag, r, j))
 
     def column(r):
-        return lambda tile: pl.BlockSpec((rows, tile), lambda j, c: (r, j))
+        return lambda tile: pl.BlockSpec((rows, tile), lambda j, *c: (r, j))
 
     def payload(k):
         h, p, w = k, k - 2, k - 4
@@ -406,20 +431,22 @@
     other, done = [], [None, None]
     kind, sent = payload(0)
     flux, sent[0] = together(flux, sent[0])
-    flux_parts = split(flux, swapped(side_of(flux, place)), place)
+    flux_other = swapped(side_of(flux, place))
     foot_other = swapped(cut(footprint, [0], slots, 0)[0])
-    same = forward(
-        [footprint] * CHUNKS,
-        [pl.BlockSpec((1, 1, rows, cells), lambda j, r=r: (0, 0, r, 0)) for r in chunks],
-        [foot_other] * CHUNKS,
-        [pl.BlockSpec((rows, cells), lambda j, r=r: (r, 0)) for r in chunks],
-        rows, flux_parts,
-    )
     for k in range(CHUNKS + 4):
         h, p, w = k, k - 2, k - 4
         arrived, sort = exchange(kind, sent), kind
         if k == 0:
-            arrived[0], flux_parts = together(arrived[0], flux_parts)
+            arrived[0], counts = together(arrived[0], counts)
+            arrived[1], flux_other = together(arrived[1], flux_other)
+            flux_parts = split(flux, flux_other, place)
+            same = forward(
+                [footprint] * CHUNKS,
+                [pl.BlockSpec((1, 1, rows, cells), lambda j, r=r: (0, 0, r, 0)) for r in chunks],
+                [foot_other] * CHUNKS,
+                [pl.BlockSpec((rows, cells), lambda j, r=r: (r, 0)) for r in chunks],
+                rows, flux_parts,
+            )
         if k == 2:
             arrived[0], same[0] = together(arrived[0], same[0])
         if k + 1 < CHUNKS + 4:
@@ -439,9 +466,9 @@
         if w >= 0:
             here = [weighted[w], *low]
             if w + 1 < CHUNKS:
-                done[:] = adjoint(here, [my_side(w, done[0]), their_side(w, done[1])], place, cells)
-    (theirs,) = adjoint(here, [their_side(w, done[1])], place, cells)
-    (mine,) = adjoint(here, [my_side(w, done[0])], place, cells)
+                done[:] = adjoint(here, [my_side(w, done[0]), their_side(w, done[1])], w * rows, place, counts, cells)
+    (theirs,) = adjoint(here, [their_side(w, done[1])], w * rows, place, counts, cells)
+    (mine,) = adjoint(here, [my_side(w, done[0])], w * rows, place, counts, cells)
     return paste(swapped(theirs), mine, place)[None]
 
 

time: 431 us -> 427 us (level); the launches traced: 430 us -> 419 us
  waiting for transfers between devices: 164 us -> 117 us
  blocking collectives: 0 us -> 31.3 us
    ppermute x12, waiting for transfers between devices: 65.2 us -> 20.8 us  [shifted(): return lax.ppermute(value, 'tm', pairs)]
    optimization_barrier x0 -> x1, blocking collectives: none -> 31.3 us  [together(): return lax.optimization_barrier((first, second))]
    unnamed x34 -> x39, local copies, waits for them, and re-layouts: 9.76 us -> 11.7 us
  transfers between devices with their start and end apart: 35 -> 35, of which waited for: 9 -> 8; matrix products, arithmetic and copies ran while one was open for 0% -> 1% of each run, Pallas kernels for 39% -> 40%
where the time goes in v2:
time: 427 us; the launch traced here: 419 us
  Pallas kernels  204 us (48%)
  waiting for transfers between devices  117 us (27%)
  starting transfers between devices  39.4 us (9%)
  blocking collectives  31.3 us (7%)
  between operations  14.5 us (3%)
  local copies, waits for them, and re-layouts  11.9 us (3%)
    psum x4, waiting for transfers between devices, on_device(): weighted.append(lax.psum(total, 'z'))  94.5 us
    pallas_call x5, Pallas kernels, adjoint(): pl.pallas_call(functools.partial(adjoint_kernel, count, len(sides), first...  72 us
    pallas_call x5, Pallas kernels, forward(): pl.pallas_call(functools.partial(forward_kernel, count), grid=(half // ti...  67.7 us
    optimization_barrier x1, blocking collectives, together(): return lax.optimization_barrier((first, second))  31.3 us
    ppermute x12, starting transfers between devices, shifted(): return lax.ppermute(value, 'tm', pairs)  21.1 us
    ppermute x12, waiting for transfers between devices, shifted(): return lax.ppermute(value, 'tm', pairs)  20.8 us
    pallas_call x4, Pallas kernels, combine(): pl.pallas_call(combine_kernel, grid_spec=pltpu.PrefetchScalarGridSpec(num...  13.8 us
    pallas_call x4, Pallas kernels, choose(): pl.pallas_call(functools.partial(choose_kernel, r), in_specs=[pl.BlockSpe...  13.1 us
  transfers between devices with their start and end apart: 35, of which 8 were waited for; matrix products, arithmetic and copies ran while one was open for 1% of the time, Pallas kernels for 40%

profile of v2, /device:TPU:3, one launch (start us, length us, event | category | flops | bytes accessed | tf_op | source)
XLA Modules:
  0.0 418.8 jit_solution(744127118097582738)
XLA Ops:
  6.5 2.6 cut.3
  9.7 4.4 %side.1 = f32[1024,1024]{1,0:T(8,128)} custom-call(s32[3]{0:T(128)} %pad_add_fusion.place_ref.core_ref, f32[1,1024,2048]{2,1,0:T(8,128)} %own), custom_call_target="tpu_custom_call" | custom-call | flops 1 | bytes 1 | tf_op jit(solution)/shard_map/side/pallas_call | solution.py:269
  14.9 1.9 collective-permute-start
  20.9 2.6 cut.5
  23.6 31.3 %all-reduce.counts_ref = s32[4]{0:T(128)} all-reduce(s32[4]{0:T(128)S(1)} %dynamic-update-slice), channel_id=1, replica_groups=mesh['tm'=4,'z'=4,'core'=2] {'tm'}, use_global_device_ids=true, to_apply=%add | all-reduce | flops 4 | bytes 32 | tf_op jit(solution)/shard_map/optimization_barrier | solution.py:35
  56.2 2.6 stack.16
  59.4 1.6 collective-permute-start.5
  61.0 4.2 collective-permute-start.8
  66.4 3.6 cut.4
  70.4 9.2 %split.1.refs_8_.refs_6_ = bf16[6144,1024]{1,0:T(8,128)(2,1)} custom-call(s32[3]{0:T(128)} %pad_add_fusion.place_ref.core_ref, f32[1,1024,2048]{2,1,0:T(8,128)} %own, f32[1024,1024]{1,0:T(8,128)} %collective-permute-done.3.other), custom_call_target="tpu_custom_call" | custom-call | flops 1 | bytes 1 | tf_op jit(solution)/shard_map/split/pallas_call | solution.py:60
  79.6 12.8 %forward.6 = (f32[192,1024]{1,0:T(8,128)}, f32[192,1024]{1,0:T(8,128)}, f32[192,1024]{1,0:T(8,128)}) custom-call(f32[192,1024]{1,0:T(8,128)} %copy-done.4, f32[192,1024]{1,0:T(8,128)} %copy-done.6, f32[192,1024]{1,0:T(8,128)} %copy-done.5, f32[576,1024]{1,0:T(8,128)} %collective-permute-done.6.refs_3_.refs_4_.refs_5_.refs_9_.refs_10_.refs_11_, ...), custom_call_target="tpu_custom_call" | custom-call | flops 1 | bytes 1 | tf_op jit(solution)/shard_map/forward/pallas_call | solution.py:101
  92.4 3.3 choose.4
  95.7 4.7 %collective-permute-done.9.refs_1_.refs_6_ = f32[192,1024]{1,0:T(8,128)} collective-permute-done((f32[192,1024]{1,0:T(8,128)}, f32[192,1024]{1,0:T(8,128)}, u32[]{:S(2)}, u32[]{:S(2)}) %collective-permute-start.9) | collective-permute-done | bytes 786464 | tf_op jit(solution)/shard_map/ppermute | solution.py:22
  100.4 2.6 stack.17
  106.0 1.7 copy-done
  107.6 16.0 %forward.5 = (f32[192,1024]{1,0:T(8,128)}, f32[192,1024]{1,0:T(8,128)}, f32[192,1024]{1,0:T(8,128)}, f32[192,1024]{1,0:T(8,128)}) custom-call(f32[1,4,768,1024]{3,2,1,0:T(8,128)} %refs_4_.7, f32[1,4,768,1024]{3,2,1,0:T(8,128)} %refs_4_.7, f32[1,4,768,1024]{3,2,1,0:T(8,128)} %refs_4_.7, f32[1,4,768,1024]{3,2,1,0:T(8,128)} %refs_4_.7, f32[768,1024]{1,0:T(8,128)} %copy-done, ...), custom_call_target="tpu_custom_call" | custom-call | flops 1 | bytes 1 | tf_op jit(solution)/shard_map/forward/pallas_call | solution.py:101
  123.9 12.9 %forward.7 = (f32[192,1024]{1,0:T(8,128)}, f32[192,1024]{1,0:T(8,128)}, f32[192,1024]{1,0:T(8,128)}) custom-call(f32[192,1024]{1,0:T(8,128)} %collective-permute-done.8.refs_0_.refs_5_, f32[192,1024]{1,0:T(8,128)} %collective-permute-done.9.refs_1_.refs_6_, f32[192,1024]{1,0:T(8,128)} %collective-permute-done.5.refs_2_.refs_7_, ...), custom_call_target="tpu_custom_call" | custom-call | flops 1 | bytes 1 | tf_op jit(solution)/shard_map/forward/pallas_call | solution.py:101
  136.8 3.3 choose.5
  141.1 2.6 stack.18
  145.2 3.5 combine.4
  148.8 1.6 collective-permute-start.11
  151.8 1.4 copy-done.1
  153.2 13.0 %forward.8 = (f32[192,1024]{1,0:T(8,128)}, f32[192,1024]{1,0:T(8,128)}, f32[192,1024]{1,0:T(8,128)}) custom-call(f32[192,1024]{1,0:T(8,128)} %collective-permute-done.12.refs_2_.refs_0_.refs_5_, f32[192,1024]{1,0:T(8,128)} %collective-permute-done.13.refs_1_.refs_6_, f32[192,1024]{1,0:T(8,128)} %collective-permute-done.7.refs_0_.refs_2_.refs_7_, ...), custom_call_target="tpu_custom_call" | custom-call | flops 1 | bytes 1 | tf_op jit(solution)/shard_map/forward/pallas_call | solution.py:101
  166.2 26.4 %all-reduce.6.cloned.1.call-done.source.refs_0_ = f32[192,1024]{1,0:T(8,128)} async-done(((f32[192,1024]{1,0:T(8,128)}), f32[192,1024]{1,0:T(8,128)}) %all-reduce.6.cloned.1.call-update) | async-done | bytes 786448 | tf_op jit(solution)/shard_map/psum | solution.py:465
  192.6 3.3 choose.6
  196.8 2.6 stack.19
  200.2 3.4 combine.5
  203.7 1.7 collective-permute-start.15
  208.5 13.0 %forward.9 = (f32[192,1024]{1,0:T(8,128)}, f32[192,1024]{1,0:T(8,128)}, f32[192,1024]{1,0:T(8,128)}) custom-call(f32[192,1024]{1,0:T(8,128)} %collective-permute-done.17.refs_2_.refs_0_.refs_5_, f32[192,1024]{1,0:T(8,128)} %collective-permute-done.16.refs_1_.refs_6_, f32[192,1024]{1,0:T(8,128)} %copy-done.3, f32[576,1024]{1,0:T(8,128)} %copy-done.2, ...), custom_call_target="tpu_custom_call" | custom-call | flops 1 | bytes 1 | tf_op jit(solution)/shard_map/forward/pallas_call | solution.py:101
  221.4 25.4 %all-reduce.8.cloned.1.call-done.source.refs_0_ = f32[192,1024]{1,0:T(8,128)} async-done(((f32[192,1024]{1,0:T(8,128)}), f32[192,1024]{1,0:T(8,128)}) %all-reduce.8.cloned.1.call-update) | async-done | bytes 786448 | tf_op jit(solution)/shard_map/psum | solution.py:465
  246.8 3.3 choose.7
  251.0 3.5 combine.6
  254.8 1.6 collective-permute-start.22
  256.5 2.5 collective-permute-start.19
  259.0 16.9 %adjoint.5 = (f32[1024,2048]{1,0:T(8,128)}, f32[1024,1024]{1,0:T(8,128)}) custom-call(s32[3]{0:T(128)} %pad_add_fusion.place_ref.core_ref, s32[4]{0:T(128)} %all-reduce.counts_ref, f32[192,1024]{1,0:T(8,128)} %all-reduce.6.cloned.1.call-done.source.refs_0_, f32[192,1024]{1,0:T(8,128)} %collective-permute-done.21.refs_2_.refs_1_, ...), custom_call_target="tpu_custom_call" | custom-call | flops 1 | bytes 1 | tf_op jit(solution)/shard_map/adjoint/pallas_call | solution.py:180
  275.8 22.4 %all-reduce.10.cloned.1.call-done.refs_0_ = f32[192,1024]{1,0:T(8,128)} async-done(((f32[192,1024]{1,0:T(8,128)}), f32[192,1024]{1,0:T(8,128)}) %all-reduce.10.cloned.1.call-update) | async-done | bytes 786448 | tf_op jit(solution)/shard_map/psum | solution.py:465
  299.6 3.5 combine.7
  303.1 1.5 collective-permute-start.28
  305.9 2.4 collective-permute-start.24
  308.4 17.5 %adjoint.6 = (f32[1024,2048]{1,0:T(8,128)}, f32[1024,1024]{1,0:T(8,128)}) custom-call(s32[3]{0:T(128)} %pad_add_fusion.place_ref.core_ref, s32[4]{0:T(128)} %all-reduce.counts_ref, f32[192,1024]{1,0:T(8,128)} %all-reduce.8.cloned.1.call-done.source.refs_0_, f32[192,1024]{1,0:T(8,128)} %copy-done.11, ...), custom_call_target="tpu_custom_call", output_to_operand_aliasing={{0}: (14, {}), {1}: (15, {})} | custom-call | flops 1 | bytes 1 | tf_op jit(solution)/shard_map/adjoint/pallas_call | solution.py:180
  325.9 20.4 %all-reduce.12.cloned.1.call-done.refs_0_ = f32[192,1024]{1,0:T(8,128)} async-done(((f32[192,1024]{1,0:T(8,128)}), f32[192,1024]{1,0:T(8,128)}) %all-reduce.12.cloned.1.call-update) | async-done | bytes 786448 | tf_op jit(solution)/shard_map/psum | solution.py:465
  348.3 2.9 collective-permute-start.25
  351.2 17.5 %adjoint.7 = (f32[1024,2048]{1,0:T(8,128)}, f32[1024,1024]{1,0:T(8,128)}) custom-call(s32[3]{0:T(128)} %pad_add_fusion.place_ref.core_ref, s32[4]{0:T(128)} %all-reduce.counts_ref, f32[192,1024]{1,0:T(8,128)} %all-reduce.10.cloned.1.call-done.refs_0_, f32[192,1024]{1,0:T(8,128)} %collective-permute-done.24.refs_1_, ...), custom_call_target="tpu_custom_call", output_to_operand_aliasing={{0}: (14, {}), {1}: (15, {})} | custom-call | flops 1 | bytes 1 | tf_op jit(solution)/shard_map/adjoint/pallas_call | solution.py:180
  368.8 16.1 %collective-permute-done.27.refs_2_ = f32[192,1024]{1,0:T(8,128)S(1)} collective-permute-done((f32[192,1024]{1,0:T(8,128)}, f32[192,1024]{1,0:T(8,128)S(1)}, u32[]{:S(2)}, u32[]{:S(2)}) %collective-permute-start.27) | collective-permute-done | bytes 786464 | tf_op jit(solution)/shard_map/ppermute | solution.py:22
  386.0 9.9 %adjoint.8 = f32[1024,1024]{1,0:T(8,128)} custom-call(s32[3]{0:T(128)} %pad_add_fusion.place_ref.core_ref, s32[4]{0:T(128)} %all-reduce.counts_ref, f32[192,1024]{1,0:T(8,128)} %all-reduce.12.cloned.1.call-done.refs_0_, f32[192,1024]{1,0:T(8,128)} %copy-done.10, f32[192,1024]{1,0:T(8,128)} %copy-done.9, ...), custom_call_target="tpu_custom_call", output_to_operand_aliasing={{}: (10, {})} | custom-call | flops 1 | bytes 1 | tf_op jit(solution)/shard_map/adjoint/pallas_call | solution.py:180
  396.0 1.6 collective-permute-start.30
  397.6 10.2 %adjoint.9.before = f32[1024,2048]{1,0:T(8,128)} custom-call(s32[3]{0:T(128)} %pad_add_fusion.place_ref.core_ref, s32[4]{0:T(128)} %all-reduce.counts_ref, f32[192,1024]{1,0:T(8,128)} %all-reduce.12.cloned.1.call-done.refs_0_, f32[192,1024]{1,0:T(8,128)} %copy-done.10, f32[192,1024]{1,0:T(8,128)} %copy-done.9, ...), custom_call_target="tpu_custom_call", output_to_operand_aliasing={{}: (10, {})} | custom-call | flops 1 | bytes 1 | tf_op jit(solution)/shard_map/adjoint/pallas_call | solution.py:180
  407.8 4.2 %paste.1 = f32[1024,2048]{1,0:T(8,128)} custom-call(s32[3]{0:T(128)} %pad_add_fusion.place_ref.core_ref, f32[1024,1024]{1,0:T(8,128)} %collective-permute-done.30.arrived, f32[1024,2048]{1,0:T(8,128)} %adjoint.9.before), custom_call_target="tpu_custom_call", output_to_operand_aliasing={{}: (2, {})} | custom-call | flops 1 | bytes 1 | tf_op jit(solution)/shard_map/paste/pallas_call | solution.py:356
  (97 shorter events, 27.4 us)
Async XLA Ops:
  6.5 186.1 %all-reduce.6.cloned.1.call-start = ((), (), s32[]{:S(2)}) async-start(), calls=%async_computation | async-start | bytes 1572864 | tf_op jit(solution)/shard_map/psum | solution.py:465
  9.7 7.8 %copy-start.16 = (f32[192,1024]{1,0:T(8,128)S(1)}, f32[192,1024]{1,0:T(8,128)}, u32[]{:S(2)}) copy-start(f32[192,1024]{1,0:T(8,128)} %get-tuple-element.109) | copy-start | bytes 2359300
  9.7 9.7 %copy-start.17 = (u32[32]{0:T(128)S(1)}, u32[32]{0:T(128)}, u32[]{:S(2)}) copy-start(u32[32]{0:T(128)} %constant.19) | copy-start | bytes 388
  14.1 40.8 %collective-permute-start.3 = (f32[1024,1024]{1,0:T(8,128)}, f32[1024,1024]{1,0:T(8,128)}, u32[]{:S(2)}, u32[]{:S(2)}) collective-permute-start(f32[1024,1024]{1,0:T(8,128)} %side.1), channel_id=1, source_target_pairs={{0,1},{1,0},{2,3},{3,2},{4,5},{5,4},{6,7},{7,6},{8,9},{9,8},{10,11... | collective-permute-start | bytes 12582920 | tf_op jit(solution)/shard_map/ppermute | solution.py:31
  14.9 40.0 %collective-permute-start = (f32[192,1024]{1,0:T(8,128)}, f32[192,1024]{1,0:T(8,128)S(1)}, u32[]{:S(2)}, u32[]{:S(2)}) collective-permute-start(f32[192,1024]{1,0:T(8,128)} %get-tuple-element.106), channel_id=1, source_target_pairs={{8,0},{16,8},{24,16},{9,1},{17,9},{25,17},{10,2},{18,10},{26,18},{... | collective-permute-start | bytes 2359304 | tf_op jit(solution)/shard_map/ppermute | solution.py:22
  16.8 38.1 %collective-permute-start.4 = (f32[192,1024]{1,0:T(8,128)}, f32[192,1024]{1,0:T(8,128)S(1)}, u32[]{:S(2)}, u32[]{:S(2)}) collective-permute-start(f32[192,1024]{1,0:T(8,128)} %get-tuple-element.112), channel_id=1, source_target_pairs={{24,0},{25,1},{26,2},{27,3},{28,4},{29,5},{30,6},{31,7}} | collective-permute-start | bytes 2359304 | tf_op jit(solution)/shard_map/ppermute | solution.py:22
  17.5 37.3 %collective-permute-start.2 = (f32[192,1024]{1,0:T(8,128)S(1)}, f32[192,1024]{1,0:T(8,128)S(1)}, u32[]{:S(2)}, u32[]{:S(2)}) collective-permute-start(f32[192,1024]{1,0:T(8,128)S(1)} %copy-done.16), channel_id=1, source_target_pairs={{16,0},{24,8},{17,1},{25,9},{18,2},{26,10},{19,3},{27,11},{20,4},{... | collective-permute-start | bytes 2359304 | tf_op jit(solution)/shard_map/ppermute | solution.py:22
  54.8 1.2 copy-start.5
  54.9 1.4 copy-start.6
  58.9 20.7 %collective-permute-start.6 = (f32[576,1024]{1,0:T(8,128)}, f32[576,1024]{1,0:T(8,128)}, u32[]{:S(2)}, u32[]{:S(2)}) collective-permute-start(f32[576,1024]{1,0:T(8,128)} %stack.16), channel_id=1, source_target_pairs={{0,1},{1,0},{2,3},{3,2},{4,5},{5,4},{6,7},{7,6},{8,9},{9,8},{10,11... | collective-permute-start | bytes 7077896 | tf_op jit(solution)/shard_map/ppermute | solution.py:31
  59.4 36.3 %collective-permute-start.5 = (f32[192,1024]{1,0:T(8,128)}, f32[192,1024]{1,0:T(8,128)}, u32[]{:S(2)}, u32[]{:S(2)}) collective-permute-start(f32[192,1024]{1,0:T(8,128)} %get-tuple-element.114), channel_id=1, source_target_pairs={{24,0},{25,1},{26,2},{27,3},{28,4},{29,5},{30,6},{31,7}} | collective-permute-start | bytes 2359304 | tf_op jit(solution)/shard_map/ppermute | solution.py:22
  61.0 34.8 %collective-permute-start.8 = (f32[192,1024]{1,0:T(8,128)}, f32[192,1024]{1,0:T(8,128)}, u32[]{:S(2)}, u32[]{:S(2)}) collective-permute-start(f32[192,1024]{1,0:T(8,128)} %get-tuple-element.127), channel_id=1, source_target_pairs={{8,0},{16,8},{24,16},{9,1},{17,9},{25,17},{10,2},{18,10},{26,18},{... | collective-permute-start | bytes 2359304 | tf_op jit(solution)/shard_map/ppermute | solution.py:22
  65.1 35.3 %collective-permute-start.9 = (f32[192,1024]{1,0:T(8,128)}, f32[192,1024]{1,0:T(8,128)}, u32[]{:S(2)}, u32[]{:S(2)}) collective-permute-start(f32[192,1024]{1,0:T(8,128)} %get-tuple-element.130), channel_id=1, source_target_pairs={{16,0},{24,8},{17,1},{25,9},{18,2},{26,10},{19,3},{27,11},{20,4},{... | collective-permute-start | bytes 2359304 | tf_op jit(solution)/shard_map/ppermute | solution.py:22
  70.0 36.0 %collective-permute-start.1 = (f32[768,1024]{1,0:T(8,128)}, f32[768,1024]{1,0:T(8,128)S(1)}, u32[]{:S(2)}, u32[]{:S(2)}) collective-permute-start(f32[768,1024]{1,0:T(8,128)} %cut.4), channel_id=1, source_target_pairs={{0,1},{1,0},{2,3},{3,2},{4,5},{5,4},{6,7},{7,6},{8,9},{9,8},{10,11... | collective-permute-start | bytes 9437192 | tf_op jit(solution)/shard_map/ppermute | solution.py:31
  103.1 20.9 %collective-permute-start.10 = (f32[576,1024]{1,0:T(8,128)}, f32[576,1024]{1,0:T(8,128)}, u32[]{:S(2)}, u32[]{:S(2)}) collective-permute-start(f32[576,1024]{1,0:T(8,128)} %stack.17), channel_id=1, source_target_pairs={{0,1},{1,0},{2,3},{3,2},{4,5},{5,4},{6,7},{7,6},{8,9},{9,8},{10,11... | collective-permute-start | bytes 7077896 | tf_op jit(solution)/shard_map/ppermute | solution.py:31
  103.6 20.4 %collective-permute-start.12 = (f32[192,1024]{1,0:T(8,128)}, f32[192,1024]{1,0:T(8,128)}, u32[]{:S(2)}, u32[]{:S(2)}) collective-permute-start(f32[192,1024]{1,0:T(8,128)} %get-tuple-element.139), channel_id=1, source_target_pairs={{0,24},{8,0},{16,8},{24,16},{1,25},{9,1},{17,9},{25,17},{2,26},{10... | collective-permute-start | bytes 2359304 | tf_op jit(solution)/shard_map/ppermute | solution.py:27
  104.5 35.6 %collective-permute-start.7 = (f32[192,1024]{1,0:T(8,128)}, f32[192,1024]{1,0:T(8,128)}, u32[]{:S(2)}, u32[]{:S(2)}) collective-permute-start(f32[192,1024]{1,0:T(8,128)} %get-tuple-element.126), channel_id=1, source_target_pairs={{0,8},{8,16},{16,24},{24,0},{1,9},{9,17},{17,25},{25,1},{2,10},{10... | collective-permute-start | bytes 2359304 | tf_op jit(solution)/shard_map/ppermute | solution.py:27
  105.9 35.2 %collective-permute-start.13 = (f32[192,1024]{1,0:T(8,128)}, f32[192,1024]{1,0:T(8,128)}, u32[]{:S(2)}, u32[]{:S(2)}) collective-permute-start(f32[192,1024]{1,0:T(8,128)} %get-tuple-element.143), channel_id=1, source_target_pairs={{0,16},{8,24},{16,0},{24,8},{1,17},{9,25},{17,1},{25,9},{2,18},{10... | collective-permute-start | bytes 2359304 | tf_op jit(solution)/shard_map/ppermute | solution.py:27
  106.0 1.7 copy-start
  140.1 4.2 copy-start.15
  143.7 8.0 %collective-permute-start.14 = (f32[576,1024]{1,0:T(8,128)}, f32[576,1024]{1,0:T(8,128)S(1)}, u32[]{:S(2)}, u32[]{:S(2)}) collective-permute-start(f32[576,1024]{1,0:T(8,128)} %stack.18), channel_id=1, source_target_pairs={{0,1},{1,0},{2,3},{3,2},{4,5},{5,4},{6,7},{7,6},{8,9},{9,8},{10,11... | collective-permute-start | bytes 7077896 | tf_op jit(solution)/shard_map/ppermute | solution.py:31
  148.7 98.1 %all-reduce.8.cloned.1.call-start = ((), (), s32[]{:S(2)}) async-start(), calls=%async_computation.1 | async-start | bytes 1572864 | tf_op jit(solution)/shard_map/psum | solution.py:465
  148.8 47.1 %collective-permute-start.11 = (f32[192,1024]{1,0:T(8,128)}, f32[192,1024]{1,0:T(8,128)S(1)}, u32[]{:S(2)}, u32[]{:S(2)}) collective-permute-start(f32[192,1024]{1,0:T(8,128)} %get-tuple-element.138), channel_id=1, source_target_pairs={{0,8},{8,16},{16,24},{24,0},{1,9},{9,17},{17,25},{25,1},{2,10},{10... | collective-permute-start | bytes 2359304 | tf_op jit(solution)/shard_map/ppermute | solution.py:27
  150.4 45.5 %collective-permute-start.16 = (f32[192,1024]{1,0:T(8,128)}, f32[192,1024]{1,0:T(8,128)}, u32[]{:S(2)}, u32[]{:S(2)}) collective-permute-start(f32[192,1024]{1,0:T(8,128)} %get-tuple-element.156), channel_id=1, source_target_pairs={{0,16},{8,24},{16,0},{24,8},{1,17},{9,25},{17,1},{25,9},{2,18},{10... | collective-permute-start | bytes 2359304 | tf_op jit(solution)/shard_map/ppermute | solution.py:27
  151.5 44.4 %collective-permute-start.17 = (f32[192,1024]{1,0:T(8,128)}, f32[192,1024]{1,0:T(8,128)}, u32[]{:S(2)}, u32[]{:S(2)}) collective-permute-start(f32[192,1024]{1,0:T(8,128)} %get-tuple-element.159), channel_id=1, source_target_pairs={{0,24},{8,0},{16,8},{24,16},{1,25},{9,1},{17,9},{25,17},{2,26},{10... | collective-permute-start | bytes 2359304 | tf_op jit(solution)/shard_map/ppermute | solution.py:27
  151.8 1.5 copy-start.1
  199.4 7.6 %collective-permute-start.18 = (f32[576,1024]{1,0:T(8,128)}, f32[576,1024]{1,0:T(8,128)S(1)}, u32[]{:S(2)}, u32[]{:S(2)}) collective-permute-start(f32[576,1024]{1,0:T(8,128)} %stack.19), channel_id=1, source_target_pairs={{0,1},{1,0},{2,3},{3,2},{4,5},{5,4},{6,7},{7,6},{8,9},{9,8},{10,11... | collective-permute-start | bytes 7077896 | tf_op jit(solution)/shard_map/ppermute | solution.py:31
  203.7 94.5 %all-reduce.10.cloned.1.call-start = ((), (), s32[]{:S(2)}) async-start(), calls=%async_computation.2 | async-start | bytes 1572864 | tf_op jit(solution)/shard_map/psum | solution.py:465
  203.7 46.3 %collective-permute-start.15 = (f32[192,1024]{1,0:T(8,128)}, f32[192,1024]{1,0:T(8,128)S(1)}, u32[]{:S(2)}, u32[]{:S(2)}) collective-permute-start(f32[192,1024]{1,0:T(8,128)} %get-tuple-element.153), channel_id=1, source_target_pairs={{0,8},{8,16},{16,24},{24,0},{1,9},{9,17},{17,25},{25,1},{2,10},{10... | collective-permute-start | bytes 2359304 | tf_op jit(solution)/shard_map/ppermute | solution.py:27
  205.4 44.7 %collective-permute-start.20 = (f32[192,1024]{1,0:T(8,128)}, f32[192,1024]{1,0:T(8,128)}, u32[]{:S(2)}, u32[]{:S(2)}) collective-permute-start(f32[192,1024]{1,0:T(8,128)} %get-tuple-element.170), channel_id=1, source_target_pairs={{0,16},{8,24},{16,0},{24,8},{1,17},{9,25},{17,1},{25,9},{2,18},{10... | collective-permute-start | bytes 2359304 | tf_op jit(solution)/shard_map/ppermute | solution.py:27
  205.6 44.5 %collective-permute-start.21 = (f32[192,1024]{1,0:T(8,128)}, f32[192,1024]{1,0:T(8,128)}, u32[]{:S(2)}, u32[]{:S(2)}) collective-permute-start(f32[192,1024]{1,0:T(8,128)} %get-tuple-element.173), channel_id=1, source_target_pairs={{0,24},{8,0},{16,8},{24,16},{1,25},{9,1},{17,9},{25,17},{2,26},{10... | collective-permute-start | bytes 2359304 | tf_op jit(solution)/shard_map/ppermute | solution.py:27
  207.0 1.4 copy-start.2
  254.5 91.8 %all-reduce.12.cloned.1.call-start = ((), (), s32[]{:S(2)}) async-start(), calls=%async_computation.3 | async-start | bytes 1572864 | tf_op jit(solution)/shard_map/psum | solution.py:465
  254.5 43.7 %collective-permute-start.23 = (f32[192,1024]{1,0:T(8,128)}, f32[192,1024]{1,0:T(8,128)S(1)}, u32[]{:S(2)}, u32[]{:S(2)}) collective-permute-start(f32[192,1024]{1,0:T(8,128)} %get-tuple-element.183), channel_id=1, source_target_pairs={{0,24},{8,0},{16,8},{24,16},{1,25},{9,1},{17,9},{25,17},{2,26},{10... | collective-permute-start | bytes 2359304 | tf_op jit(solution)/shard_map/ppermute | solution.py:27
  254.8 43.4 %collective-permute-start.22 = (f32[192,1024]{1,0:T(8,128)}, f32[192,1024]{1,0:T(8,128)S(1)}, u32[]{:S(2)}, u32[]{:S(2)}) collective-permute-start(f32[192,1024]{1,0:T(8,128)} %get-tuple-element.181), channel_id=1, source_target_pairs={{0,16},{8,24},{16,0},{24,8},{1,17},{9,25},{17,1},{25,9},{2,18},{10... | collective-permute-start | bytes 2359304 | tf_op jit(solution)/shard_map/ppermute | solution.py:27
  256.5 41.8 %collective-permute-start.19 = (f32[192,1024]{1,0:T(8,128)}, f32[192,1024]{1,0:T(8,128)S(1)}, u32[]{:S(2)}, u32[]{:S(2)}) collective-permute-start(f32[192,1024]{1,0:T(8,128)} %get-tuple-element.167), channel_id=1, source_target_pairs={{0,8},{8,16},{16,24},{24,0},{1,9},{9,17},{17,25},{25,1},{2,10},{10... | collective-permute-start | bytes 2359304 | tf_op jit(solution)/shard_map/ppermute | solution.py:27
  298.2 4.9 %copy-start.14 = (f32[192,1024]{1,0:T(8,128)S(1)}, f32[192,1024]{1,0:T(8,128)}, u32[]{:S(2)}) copy-start(f32[192,1024]{1,0:T(8,128)} %all-reduce.10.cloned.1.call-done.refs_0_) | copy-start | bytes 2359300
  298.2 1.2 copy-start.12
  298.2 1.4 copy-start.13
  303.1 43.1 %collective-permute-start.28 = (f32[192,1024]{1,0:T(8,128)S(1)}, f32[192,1024]{1,0:T(8,128)}, u32[]{:S(2)}, u32[]{:S(2)}) collective-permute-start(f32[192,1024]{1,0:T(8,128)S(1)} %copy-done.14), channel_id=1, source_target_pairs={{24,0},{25,1},{26,2},{27,3},{28,4},{29,5},{30,6},{31,7}} | collective-permute-start | bytes 2359304 | tf_op jit(solution)/shard_map/ppermute | solution.py:22
  304.6 42.3 %collective-permute-start.26 = (f32[192,1024]{1,0:T(8,128)S(1)}, f32[192,1024]{1,0:T(8,128)}, u32[]{:S(2)}, u32[]{:S(2)}) collective-permute-start(f32[192,1024]{1,0:T(8,128)S(1)} %copy-done.14), channel_id=1, source_target_pairs={{16,0},{24,8},{17,1},{25,9},{18,2},{26,10},{19,3},{27,11},{20,4},{... | collective-permute-start | bytes 2359304 | tf_op jit(solution)/shard_map/ppermute | solution.py:22
  305.9 42.3 %collective-permute-start.24 = (f32[192,1024]{1,0:T(8,128)S(1)}, f32[192,1024]{1,0:T(8,128)}, u32[]{:S(2)}, u32[]{:S(2)}) collective-permute-start(f32[192,1024]{1,0:T(8,128)S(1)} %copy-done.14), channel_id=1, source_target_pairs={{8,0},{16,8},{24,16},{9,1},{17,9},{25,17},{10,2},{18,10},{26,18},{... | collective-permute-start | bytes 2359304 | tf_op jit(solution)/shard_map/ppermute | solution.py:22
  346.3 22.5 %collective-permute-start.29 = (f32[192,1024]{1,0:T(8,128)}, f32[192,1024]{1,0:T(8,128)S(1)}, u32[]{:S(2)}, u32[]{:S(2)}) collective-permute-start(f32[192,1024]{1,0:T(8,128)} %all-reduce.12.cloned.1.call-done.refs_0_), channel_id=1, source_target_pairs={{24,0},{25,1},{26,2},{27,3},{28,4},{29,5},{30,6},{31,7}} | collective-permute-start | bytes 2359304 | tf_op jit(solution)/shard_map/ppermute | solution.py:22
  347.0 37.9 %collective-permute-start.27 = (f32[192,1024]{1,0:T(8,128)}, f32[192,1024]{1,0:T(8,128)S(1)}, u32[]{:S(2)}, u32[]{:S(2)}) collective-permute-start(f32[192,1024]{1,0:T(8,128)} %all-reduce.12.cloned.1.call-done.refs_0_), channel_id=1, source_target_pairs={{16,0},{24,8},{17,1},{25,9},{18,2},{26,10},{19,3},{27,11},{20,4},{... | collective-permute-start | bytes 2359304 | tf_op jit(solution)/shard_map/ppermute | solution.py:22
  348.3 36.6 %collective-permute-start.25 = (f32[192,1024]{1,0:T(8,128)}, f32[192,1024]{1,0:T(8,128)S(1)}, u32[]{:S(2)}, u32[]{:S(2)}) collective-permute-start(f32[192,1024]{1,0:T(8,128)} %all-reduce.12.cloned.1.call-done.refs_0_), channel_id=1, source_target_pairs={{8,0},{16,8},{24,16},{9,1},{17,9},{25,17},{10,2},{18,10},{26,18},{... | collective-permute-start | bytes 2359304 | tf_op jit(solution)/shard_map/ppermute | solution.py:22
  368.8 16.1 %copy-start.8 = (f32[192,1024]{1,0:T(8,128)}, f32[192,1024]{1,0:T(8,128)S(1)}, u32[]{:S(2)}) copy-start(f32[192,1024]{1,0:T(8,128)S(1)} %collective-permute-done.29.refs_3_) | copy-start | bytes 2359300
  384.9 1.2 copy-start.10
  396.0 11.8 %collective-permute-start.30 = (f32[1024,1024]{1,0:T(8,128)}, f32[1024,1024]{1,0:T(8,128)}, u32[]{:S(2)}, u32[]{:S(2)}) collective-permute-start(f32[1024,1024]{1,0:T(8,128)} %adjoint.8), channel_id=1, source_target_pairs={{0,1},{1,0},{2,3},{3,2},{4,5},{5,4},{6,7},{7,6},{8,9},{9,8},{10,11... | collective-permute-start | bytes 12582920 | tf_op jit(solution)/shard_map/ppermute | solution.py:31
  (5 other events, 4.6 us)
Sparse Core Ops, SparseCore 0:
  148.9 43.6 all-reduce.5
  203.8 42.9 all-reduce.7
  254.6 43.5 all-reduce.9
  303.2 42.9 all-reduce.11

commit v3 on v1

--- a/solution.py
+++ b/solution.py
@@ -120,32 +120,34 @@
     weighted, refs = refs[:count], refs[count:]
     foot, refs = refs[:sides * count], refs[sides * count:]
     before, refs = (None, refs) if first else (refs[:sides], refs[sides:])
-    outs, parts_ref = refs[:sides], refs[sides]
+    outs, (high_ref, low_ref) = refs[:sides], refs[sides:]
     rows, tile = foot[0].shape[-2:]
-    depth = count * rows
 
     @pl.when(pl.program_id(0) == 0)
     def _():
         for i in range(count):
             value = jnp.where(place_ref[1] + i < place_ref[2], weighted[i][...], 0.0)
             high, low = halves(value)
-            for block, part in enumerate((high, high, low)):
-                parts_ref[pl.ds(block * depth + i * rows, rows), :] = part
-
+            high_ref[pl.ds(i * rows, rows), :] = high
+            low_ref[pl.ds(i * rows, rows), :] = low
+
+    dims = ((0,), (0,))
     for side in range(sides):
         mine = foot[side * count:(side + 1) * count]
         slab = jnp.concatenate([ref[...].reshape(rows, tile) for ref in mine], axis=0)
-        high, low = halves(slab.T)
-        total = times(jnp.concatenate([high, low, high], axis=1), parts_ref[...], ((1,), (0,)))
+        high, low = halves(slab)
+        total = times(high, high_ref[...], dims)
+        total = total + times(low, high_ref[...], dims)
+        total = total + times(high, low_ref[...], dims)
         if not first:
             total = total + before[side][...]
         outs[side][...] = total
 
 
-def adjoint(weighted, sides, core, cells):
+def adjoint(weighted, sides, place, cells):
     count = len(weighted)
     rows, half = weighted[0].shape
-    tile = min(WIDE, cells)
+    tile = min(TILE, cells)
     first = sides[0][2] is None
     out_specs = []
     for side in sides:
@@ -167,14 +169,14 @@
                 *([] if first else out_specs),
             ],
             out_specs=out_specs,
-            scratch_shapes=[pltpu.VMEM((3 * count * rows, half), jnp.bfloat16)],
+            scratch_shapes=[pltpu.VMEM((count * rows, half), jnp.bfloat16)] * 2,
         ),
         out_shape=[jax.ShapeDtypeStruct((cells, side[3]), jnp.float32) for side in sides],
         input_output_aliases={} if first else {at + i: i for i in range(len(sides))},
         compiler_params=pltpu.CompilerParams(vmem_limit_bytes=VMEM_LIMIT),
         name="adjoint",
         cost_estimate=LIGHT,
-    )(core, *weighted, *foot, *earlier)
+    )(place, *weighted, *foot, *earlier)
 
 
 def through(buffer, sems, moves):
@@ -253,33 +255,86 @@
     )(place, flux)
 
 
-def combine_kernel(place_ref, scale, same, *refs):
-    total = same[...]
-    for lag, ref in enumerate(refs[:-1], 1):
-        total = total + jnp.where(place_ref[1] >= lag, ref[...], 0.0)
-    refs[-1][...] = scale[...] * total
-
-
-def combine(scale, same, arrived, r, place):
+def meet_kernel(lows, highs, chosen, place_ref, scale, same, *refs):
+    count = len(highs)
+    refs = list(refs)
+    arrived = [refs.pop(0) for _ in range(max(lows + highs) + 1)]
+    source = refs.pop(0) if chosen else None
+    ups = [refs.pop(0) for _ in range(count)] if chosen else []
+    total = refs.pop(0)
+    stacked = refs.pop(0) if lows else None
+    outs = [refs.pop(0) for _ in range(count)] if chosen else []
+    held, base, sum_ref, picked, sems = refs
+    rows = same.shape[0]
+
+    loads = [pltpu.make_async_copy(a, held.at[i], sems.at[0, i]) for i, a in enumerate(arrived)]
+    base_load = pltpu.make_async_copy(same, base, sems.at[1, 0])
+    for load in [*loads, base_load]:
+        load.start()
+    picks = []
+    for i, up in enumerate(ups):
+        below = place_ref[1] > i
+        picks.append((below, pltpu.make_async_copy(source, picked.at[i], sems.at[2, i])))
+        picks.append((jnp.logical_not(below), pltpu.make_async_copy(up, picked.at[i], sems.at[2, i])))
+    for taken, pick in picks:
+        pl.when(taken)(pick.start)
+    for load in [*loads, base_load]:
+        load.wait()
+
+    value = base[...]
+    for lag, i in enumerate(highs, 1):
+        value = value + jnp.where(place_ref[1] >= lag, held[i], 0.0)
+    sum_ref[...] = scale[...] * value
+    stores = [pltpu.make_async_copy(sum_ref, total, sems.at[1, 1])]
+    stores[0].start()
+    for n, i in enumerate(lows):
+        stores.append(pltpu.make_async_copy(
+            held.at[i], stacked.at[pl.ds(n * rows, rows), :], sems.at[3, n]
+        ))
+        stores[-1].start()
+    for taken, pick in picks:
+        pl.when(taken)(pick.wait)
+    for i, out in enumerate(outs):
+        stores.append(pltpu.make_async_copy(picked.at[i], out, sems.at[4, i]))
+        stores[-1].start()
+    for store in stores:
+        store.wait()
+
+
+def meet(place, scale, same, arrived, lows, highs, source, ups):
     rows, half = same.shape
-    tile = min(WIDE, half)
-    block = pl.BlockSpec((rows, tile), lambda j, c: (0, j))
-    return pl.pallas_call(
-        combine_kernel,
-        grid_spec=pltpu.PrefetchScalarGridSpec(
-            num_scalar_prefetch=1,
-            grid=(half // tile,),
-            in_specs=[
-                pl.BlockSpec((rows, 1), lambda j, c: (r, 0)),
-                block,
-                *[block] * len(arrived),
-            ],
-            out_specs=block,
-        ),
-        out_shape=jax.ShapeDtypeStruct((rows, half), jnp.float32),
-        name="combine",
-        cost_estimate=LIGHT,
-    )(place, scale, same, *arrived)
+    count = len(highs)
+    chosen = source is not None
+    shape = jax.ShapeDtypeStruct((rows, half), jnp.float32)
+    outs = [shape]
+    if lows:
+        outs.append(jax.ShapeDtypeStruct((count * rows, arrived[lows[0]].shape[1]), jnp.float32))
+    if chosen:
+        outs += [shape] * count
+    extra = [source, *ups] if chosen else []
+    outs = list(pl.pallas_call(
+        functools.partial(meet_kernel, lows, highs, chosen),
+        in_specs=[
+            pl.BlockSpec(memory_space=pltpu.SMEM),
+            pl.BlockSpec(memory_space=pltpu.VMEM),
+            *[IN_PLACE] * (1 + len(arrived) + len(extra)),
+        ],
+        out_specs=[IN_PLACE] * len(outs),
+        scratch_shapes=[
+            pltpu.VMEM((len(arrived), rows, half), jnp.float32),
+            pltpu.VMEM((rows, half), jnp.float32),
+            pltpu.VMEM((rows, half), jnp.float32),
+            pltpu.VMEM((count, rows, half), jnp.float32),
+            pltpu.SemaphoreType.DMA((5, max(len(arrived), 2))),
+        ],
+        out_shape=outs,
+        compiler_params=pltpu.CompilerParams(vmem_limit_bytes=VMEM_LIMIT),
+        name="meet",
+        cost_estimate=LIGHT,
+    )(place, scale, same, *arrived, *extra))
+    total = outs.pop(0)
+    stacked = outs.pop(0) if lows else None
+    return total, stacked, outs
 
 
 def choose_kernel(r, place_ref, source, *refs):
@@ -406,36 +461,52 @@
     other, done = [], [None, None]
     kind, sent = payload(0)
     flux, sent[0] = together(flux, sent[0])
-    flux_parts = split(flux, swapped(side_of(flux, place)), place)
+    flux_other = swapped(side_of(flux, place))
     foot_other = swapped(cut(footprint, [0], slots, 0)[0])
-    same = forward(
-        [footprint] * CHUNKS,
-        [pl.BlockSpec((1, 1, rows, cells), lambda j, r=r: (0, 0, r, 0)) for r in chunks],
-        [foot_other] * CHUNKS,
-        [pl.BlockSpec((rows, cells), lambda j, r=r: (r, 0)) for r in chunks],
-        rows, flux_parts,
-    )
     for k in range(CHUNKS + 4):
         h, p, w = k, k - 2, k - 4
         arrived, sort = exchange(kind, sent), kind
         if k == 0:
-            arrived[0], flux_parts = together(arrived[0], flux_parts)
+            arrived[1], flux_other = together(arrived[1], flux_other)
+            flux_parts = split(flux, flux_other, place)
+            same = forward(
+                [footprint] * CHUNKS,
+                [pl.BlockSpec((1, 1, rows, cells), lambda j, r=r: (0, 0, r, 0)) for r in chunks],
+                [foot_other] * CHUNKS,
+                [pl.BlockSpec((rows, cells), lambda j, r=r: (r, 0)) for r in chunks],
+                rows, flux_parts,
+            )
         if k == 2:
             arrived[0], same[0] = together(arrived[0], same[0])
-        if k + 1 < CHUNKS + 4:
+        here_up = 0 <= p < CHUNKS
+        late = paired and CHUNKS <= k + 1 < CHUNKS + 2 and here_up
+        if k + 1 < CHUNKS + 4 and not late:
             kind, sent = payload(k + 1)
             for i in range(min(len(sent), len(arrived))):
                 arrived[i], sent[i] = together(arrived[i], sent[i])
         low, high = sorted_out(sort, arrived)
-        if h < CHUNKS:
-            own.append(low)
-            other.append(swapped(stack(low)))
-            terms.append(forward(low, specs, [other[h]] * len(later), other_specs, rows, flux_parts))
-        if 0 <= p < CHUNKS:
-            total = combine(row_scale, same[p], high, p, place)
+        stacked = None
+        if here_up:
+            count = len(later)
+            if not paired and low is not None and cells != half:
+                total, _, _ = meet(place, row_scale[p * rows:(p + 1) * rows], same[p], high, [], list(range(count)), None, [])
+            else:
+                lows = list(range(count)) if h < CHUNKS else []
+                highs = list(range(count))[::-1] if sort == "one" else list(range(len(arrived) - count, len(arrived)))
+                source = weighted[k - 3] if late else None
+                ups = terms[k - 1][::-1] if late else []
+                total, stacked, made = meet(
+                    place, row_scale[p * rows:(p + 1) * rows], same[p], arrived, lows, highs, source, ups
+                )
+                if late:
+                    kind, sent = "one", made
             if p > 0:
                 total, weighted[p - 1] = together(total, weighted[p - 1])
             weighted.append(lax.psum(total, "z"))
+        if h < CHUNKS:
+            own.append(low)
+            other.append(swapped(stack(low) if stacked is None else stacked))
+            terms.append(forward(low, specs, [other[h]] * len(later), other_specs, rows, flux_parts))
         if w >= 0:
             here = [weighted[w], *low]
             if w + 1 < CHUNKS:

time: 431 us -> 418 us (0.970)
  waiting for transfers between devices: 164 us -> 154 us
  Pallas kernels: 204 us -> 196 us
    psum x4, waiting for transfers between devices: 97.6 us -> 79.3 us  [on_device(): weighted.append(lax.psum(total, 'z'))]
    ppermute x12, waiting for transfers between devices: 1.3 us -> 19 us  [cycled(): lax.ppermute(value, 'tm', [(i, (i - by) % devices) for i in range(devices)])]
    ppermute x12, waiting for transfers between devices: 65.2 us -> 54.5 us  [shifted(): return lax.ppermute(value, 'tm', pairs)]
    pallas_call x4 -> x2, Pallas kernels: 13.1 us -> 6.56 us  [choose(): pl.pallas_call(functools.partial(choose_kernel, r), in_specs=[pl.BlockSpe...]
    pallas_call x4, Pallas kernels: 13.8 us -> 19.3 us  [meet(): pl.pallas_call(functools.partial(meet_kernel, lows, highs, chosen), in_sp...]
    pallas_call x4 -> x2, Pallas kernels: 10.4 us -> 5.28 us  [stack(): pl.pallas_call(stack_kernel, in_specs=[IN_PLACE] * len(pieces), out_specs...]
  transfers between devices with their start and end apart: 35 -> 35, of which waited for: 9 -> 12; matrix products, arithmetic and copies ran while one was open for 0% -> 1% of each run, Pallas kernels for 39% -> 37%
where the time goes in v3:
time: 418 us; the launch traced here: 414 us
  Pallas kernels  196 us (47%)
  waiting for transfers between devices  154 us (37%)
  starting transfers between devices  37.4 us (9%)
  between operations  14.2 us (3%)
  local copies, waits for them, and re-layouts  12.1 us (3%)
    psum x4, waiting for transfers between devices, on_device(): weighted.append(lax.psum(total, 'z'))  79.3 us
    pallas_call x5, Pallas kernels, adjoint(): pl.pallas_call(functools.partial(adjoint_kernel, count, len(sides), first...  70.4 us
    pallas_call x5, Pallas kernels, forward(): pl.pallas_call(functools.partial(forward_kernel, count), grid=(half // ti...  67.4 us
    ppermute x12, waiting for transfers between devices, shifted(): return lax.ppermute(value, 'tm', pairs)  54.5 us
    ppermute x12, starting transfers between devices, shifted(): return lax.ppermute(value, 'tm', pairs)  20.2 us
    pallas_call x4, Pallas kernels, meet(): pl.pallas_call(functools.partial(meet_kernel, lows, highs, chosen), in_sp...  19.3 us
    ppermute x12, waiting for transfers between devices, cycled(): lax.ppermute(value, 'tm', [(i, (i - by) % devices) for i in range(devices)])  19 us
    ppermute x12, starting transfers between devices, cycled(): lax.ppermute(value, 'tm', [(i, (i - by) % devices) for i in range(devices)])  12.6 us
  transfers between devices with their start and end apart: 35, of which 12 were waited for; matrix products, arithmetic and copies ran while one was open for 1% of the time, Pallas kernels for 37%

profile of v3, /device:TPU:3, one launch (start us, length us, event | category | flops | bytes accessed | tf_op | source)
XLA Modules:
  0.0 414.2 jit_solution(11938780644792512046)
XLA Ops:
  6.5 2.6 cut.4
  9.8 4.4 %side.1 = f32[1024,1024]{1,0:T(8,128)} custom-call(s32[3]{0:T(128)} %pad_add_fusion.place_ref.core_ref, f32[1,1024,2048]{2,1,0:T(8,128)} %own), custom_call_target="tpu_custom_call" | custom-call | flops 1 | bytes 1 | tf_op jit(solution)/shard_map/side/pallas_call | solution.py:247
  14.9 1.9 collective-permute-start.3
  18.9 2.6 cut.5
  21.5 15.6 %collective-permute-done.3.refs_0_.refs_5_ = f32[192,1024]{1,0:T(8,128)S(1)} collective-permute-done((f32[192,1024]{1,0:T(8,128)}, f32[192,1024]{1,0:T(8,128)S(1)}, u32[]{:S(2)}, u32[]{:S(2)}) %collective-permute-start.3) | collective-permute-done | bytes 786464 | tf_op jit(solution)/shard_map/ppermute | solution.py:22
  37.1 17.2 %collective-permute-done.1.refs_1_.refs_6_ = f32[192,1024]{1,0:T(8,128)S(1)} collective-permute-done((f32[192,1024]{1,0:T(8,128)S(1)}, f32[192,1024]{1,0:T(8,128)S(1)}, u32[]{:S(2)}, u32[]{:S(2)}) %collective-permute-start.1) | collective-permute-done | bytes 786464 | tf_op jit(solution)/shard_map/ppermute | solution.py:22
  55.2 2.6 stack.14
  58.4 4.0 collective-permute-start.4
  63.7 1.6 collective-permute-start.9
  65.2 3.6 cut.3
  69.2 9.2 %split.1.refs_8_.refs_6_ = bf16[6144,1024]{1,0:T(8,128)(2,1)} custom-call(s32[3]{0:T(128)} %pad_add_fusion.place_ref.core_ref, f32[1,1024,2048]{2,1,0:T(8,128)} %own, f32[1024,1024]{1,0:T(8,128)} %collective-permute-done.2.other), custom_call_target="tpu_custom_call" | custom-call | flops 1 | bytes 1 | tf_op jit(solution)/shard_map/split/pallas_call | solution.py:60
  78.4 12.9 %forward.6 = (f32[192,1024]{1,0:T(8,128)}, f32[192,1024]{1,0:T(8,128)}, f32[192,1024]{1,0:T(8,128)}) custom-call(f32[192,1024]{1,0:T(8,128)} %copy-done.3, f32[192,1024]{1,0:T(8,128)} %copy-done.5, f32[192,1024]{1,0:T(8,128)} %copy-done.4, f32[576,1024]{1,0:T(8,128)} %collective-permute-done.6.refs_3_.refs_4_.refs_5_.refs_9_.refs_10_.refs_11_, ...), custom_call_target="tpu_custom_call" | custom-call | flops 1 | bytes 1 | tf_op jit(solution)/shard_map/forward/pallas_call | solution.py:101
  91.3 3.3 choose.2
  94.6 3.2 collective-permute-done.8.refs_1_.refs_6_
  97.8 2.6 stack.15
  101.0 2.5 collective-permute-start.7
  106.2 1.7 copy-done
  107.9 16.0 %forward.5 = (f32[192,1024]{1,0:T(8,128)}, f32[192,1024]{1,0:T(8,128)}, f32[192,1024]{1,0:T(8,128)}, f32[192,1024]{1,0:T(8,128)}) custom-call(f32[1,4,768,1024]{3,2,1,0:T(8,128)} %refs_4_.7, f32[1,4,768,1024]{3,2,1,0:T(8,128)} %refs_4_.7, f32[1,4,768,1024]{3,2,1,0:T(8,128)} %refs_4_.7, f32[1,4,768,1024]{3,2,1,0:T(8,128)} %refs_4_.7, f32[768,1024]{1,0:T(8,128)} %copy-done, ...), custom_call_target="tpu_custom_call" | custom-call | flops 1 | bytes 1 | tf_op jit(solution)/shard_map/forward/pallas_call | solution.py:101
  123.9 12.8 %forward.7 = (f32[192,1024]{1,0:T(8,128)}, f32[192,1024]{1,0:T(8,128)}, f32[192,1024]{1,0:T(8,128)}) custom-call(f32[192,1024]{1,0:T(8,128)} %collective-permute-done.4.refs_0_.refs_5_, f32[192,1024]{1,0:T(8,128)} %collective-permute-done.8.refs_1_.refs_6_, f32[192,1024]{1,0:T(8,128)} %collective-permute-done.9.refs_2_.refs_7_, ...), custom_call_target="tpu_custom_call" | custom-call | flops 1 | bytes 1 | tf_op jit(solution)/shard_map/forward/pallas_call | solution.py:101
  136.8 3.3 choose.3
  140.1 4.7 %meet.4 = (f32[192,1024]{1,0:T(8,128)}, f32[576,1024]{1,0:T(8,128)}) custom-call(s32[3]{0:T(128)} %pad_add_fusion.place_ref.core_ref, f32[192,1]{1,0:T(8,128)} %copy.12.scale, f32[192,1024]{1,0:T(8,128)} %get-tuple-element.138.same, f32[192,1024]{1,0:T(8,128)} %collective-permute-done.7.refs_0_.refs_5_, f32[192,1024]{1,0:T(8,128)} %collective-permute-done.12.refs_1_.refs_6_, ...), custom_call_target="tpu_custom_call" | custom-call | flops 1 | bytes 1 | tf_op jit(solution)/shard_map/meet/pallas_call | solution.py:315
  145.6 1.7 collective-permute-start.15
  148.6 1.4 collective-permute-done.16.refs_3_.refs_4_.refs_5_.refs_9_.refs_10_.refs_11_
  150.0 1.5 copy-done.2
  151.5 12.8 %forward.8 = (f32[192,1024]{1,0:T(8,128)}, f32[192,1024]{1,0:T(8,128)}, f32[192,1024]{1,0:T(8,128)}) custom-call(f32[192,1024]{1,0:T(8,128)} %collective-permute-done.7.refs_0_.refs_5_, f32[192,1024]{1,0:T(8,128)} %collective-permute-done.12.refs_1_.refs_6_, f32[192,1024]{1,0:T(8,128)} %collective-permute-done.14.refs_2_.refs_7_, f32[576,1024]{1,0:T(8,128)} %copy-done.2, ...), custom_call_target="tpu_custom_call" | custom-call | flops 1 | bytes 1 | tf_op jit(solution)/shard_map/forward/pallas_call | solution.py:101
  165.1 18.2 %collective-permute-done.13.refs_1_.refs_6_ = f32[192,1024]{1,0:T(8,128)} collective-permute-done((f32[192,1024]{1,0:T(8,128)}, f32[192,1024]{1,0:T(8,128)}, u32[]{:S(2)}, u32[]{:S(2)}) %collective-permute-start.13) | collective-permute-done | bytes 786464 | tf_op jit(solution)/shard_map/ppermute | solution.py:27
  183.2 9.8 %all-reduce.5.cloned.1.call-done.refs_3_.refs_0_ = f32[192,1024]{1,0:T(8,128)} async-done(((f32[192,1024]{1,0:T(8,128)}), f32[192,1024]{1,0:T(8,128)}) %all-reduce.5.cloned.1.call-update) | async-done | bytes 786448 | tf_op jit(solution)/shard_map/psum | solution.py:505
  193.0 5.5 %meet.5 = (f32[192,1024]{1,0:T(8,128)}, f32[576,1024]{1,0:T(8,128)}, f32[192,1024]{1,0:T(8,128)}, f32[192,1024]{1,0:T(8,128)}, f32[192,1024]{1,0:T(8,128)}) custom-call(s32[3]{0:T(128)} %pad_add_fusion.place_ref.core_ref, f32[192,1]{1,0:T(8,128)} %copy.13.scale, f32[192,1024]{1,0:T(8,128)} %get-tuple-element.102.same, ...), custom_call_target="tpu_custom_call" | custom-call | flops 1 | bytes 1 | tf_op jit(solution)/shard_map/meet/pallas_call | solution.py:315
  199.8 1.6 collective-permute-start.18
  201.3 2.2 collective-permute-start.19
  204.3 1.5 copy-done.1
  205.7 12.8 %forward.9 = (f32[192,1024]{1,0:T(8,128)}, f32[192,1024]{1,0:T(8,128)}, f32[192,1024]{1,0:T(8,128)}) custom-call(f32[192,1024]{1,0:T(8,128)} %collective-permute-done.11.refs_0_.refs_5_, f32[192,1024]{1,0:T(8,128)} %collective-permute-done.13.refs_1_.refs_6_, f32[192,1024]{1,0:T(8,128)} %copy-done.6, f32[576,1024]{1,0:T(8,128)} %copy-done.1, ...), custom_call_target="tpu_custom_call" | custom-call | flops 1 | bytes 1 | tf_op jit(solution)/shard_map/forward/pallas_call | solution.py:101
  218.5 23.8 %all-reduce.7.cloned.1.call-done.refs_3_.refs_0_ = f32[192,1024]{1,0:T(8,128)} async-done(((f32[192,1024]{1,0:T(8,128)}), f32[192,1024]{1,0:T(8,128)}) %all-reduce.7.cloned.1.call-update) | async-done | bytes 786448 | tf_op jit(solution)/shard_map/psum | solution.py:505
  243.3 5.0 %meet.6 = (f32[192,1024]{1,0:T(8,128)}, f32[192,1024]{1,0:T(8,128)}, f32[192,1024]{1,0:T(8,128)}, f32[192,1024]{1,0:T(8,128)}) custom-call(s32[3]{0:T(128)} %pad_add_fusion.place_ref.core_ref, f32[192,1]{1,0:T(8,128)} %copy.14.scale, f32[192,1024]{1,0:T(8,128)} %get-tuple-element.101.same, f32[192,1024]{1,0:T(8,128)} %copy-done.10, ...), custom_call_target="tpu_custom_call" | custom-call | flops 1 | bytes 1 | tf_op jit(solution)/shard_map/meet/pallas_call | solution.py:315
  250.0 1.4 collective-permute-start.21
  252.1 15.7 %adjoint.5 = (f32[1024,2048]{1,0:T(8,128)}, f32[1024,1024]{1,0:T(8,128)}) custom-call(s32[3]{0:T(128)} %pad_add_fusion.place_ref.core_ref, f32[192,1024]{1,0:T(8,128)} %all-reduce.5.cloned.1.call-done.refs_3_.refs_0_, f32[192,1024]{1,0:T(8,128)} %copy-done.10, f32[192,1024]{1,0:T(8,128)} %collective-permute-done.18.refs_1_.refs_2_, ...), custom_call_target="tpu_custom_call" | custom-call | flops 1 | bytes 1 | tf_op jit(solution)/shard_map/adjoint/pallas_call | solution.py:161
  267.8 23.9 %all-reduce.9.cloned.1.call-done.refs_0_ = f32[192,1024]{1,0:T(8,128)} async-done(((f32[192,1024]{1,0:T(8,128)}), f32[192,1024]{1,0:T(8,128)}) %all-reduce.9.cloned.1.call-update) | async-done | bytes 786448 | tf_op jit(solution)/shard_map/psum | solution.py:505
  293.2 4.0 meet.7
  297.2 2.2 collective-permute-start.24
  300.7 1.5 collective-permute-start.28
  302.3 16.3 %adjoint.6 = (f32[1024,2048]{1,0:T(8,128)}, f32[1024,1024]{1,0:T(8,128)}) custom-call(s32[3]{0:T(128)} %pad_add_fusion.place_ref.core_ref, f32[192,1024]{1,0:T(8,128)} %all-reduce.7.cloned.1.call-done.refs_3_.refs_0_, f32[192,1024]{1,0:T(8,128)} %copy-done.13, f32[192,1024]{1,0:T(8,128)} %copy-done.12, ...), custom_call_target="tpu_custom_call", output_to_operand_aliasing={{0}: (13, {}), {1}: (14, {})} | custom-call | flops 1 | bytes 1 | tf_op jit(solution)/shard_map/adjoint/pallas_call | solution.py:161
  318.6 21.8 %all-reduce.11.cloned.1.call-done.refs_0_ = f32[192,1024]{1,0:T(8,128)} async-done(((f32[192,1024]{1,0:T(8,128)}), f32[192,1024]{1,0:T(8,128)}) %all-reduce.11.cloned.1.call-update) | async-done | bytes 786448 | tf_op jit(solution)/shard_map/psum | solution.py:505
  340.4 2.2 collective-permute-start.25
  344.8 16.3 %adjoint.7 = (f32[1024,2048]{1,0:T(8,128)}, f32[1024,1024]{1,0:T(8,128)}) custom-call(s32[3]{0:T(128)} %pad_add_fusion.place_ref.core_ref, f32[192,1024]{1,0:T(8,128)} %all-reduce.9.cloned.1.call-done.refs_0_, f32[192,1024]{1,0:T(8,128)} %collective-permute-done.24.refs_1_, ...), custom_call_target="tpu_custom_call", output_to_operand_aliasing={{0}: (13, {}), {1}: (14, {})} | custom-call | flops 1 | bytes 1 | tf_op jit(solution)/shard_map/adjoint/pallas_call | solution.py:161
  361.7 18.0 %collective-permute-done.27.refs_2_ = f32[192,1024]{1,0:T(8,128)S(1)} collective-permute-done((f32[192,1024]{1,0:T(8,128)}, f32[192,1024]{1,0:T(8,128)S(1)}, u32[]{:S(2)}, u32[]{:S(2)}) %collective-permute-start.27) | collective-permute-done | bytes 786464 | tf_op jit(solution)/shard_map/ppermute | solution.py:22
  380.8 11.1 %adjoint.8 = f32[1024,1024]{1,0:T(8,128)} custom-call(s32[3]{0:T(128)} %pad_add_fusion.place_ref.core_ref, f32[192,1024]{1,0:T(8,128)} %all-reduce.11.cloned.1.call-done.refs_0_, f32[192,1024]{1,0:T(8,128)} %copy-done.7, f32[192,1024]{1,0:T(8,128)} %copy-done.8, f32[192,1024]{1,0:T(8,128)} %copy-done.9, ...), custom_call_target="tpu_custom_call", output_to_operand_aliasing={{}: (9, {})} | custom-call | flops 1 | bytes 1 | tf_op jit(solution)/shard_map/adjoint/pallas_call | solution.py:161
  392.4 11.1 %adjoint.9.before = f32[1024,2048]{1,0:T(8,128)} custom-call(s32[3]{0:T(128)} %pad_add_fusion.place_ref.core_ref, f32[192,1024]{1,0:T(8,128)} %all-reduce.11.cloned.1.call-done.refs_0_, f32[192,1024]{1,0:T(8,128)} %copy-done.7, f32[192,1024]{1,0:T(8,128)} %copy-done.8, f32[192,1024]{1,0:T(8,128)} %copy-done.9, ...), custom_call_target="tpu_custom_call", output_to_operand_aliasing={{}: (9, {})} | custom-call | flops 1 | bytes 1 | tf_op jit(solution)/shard_map/adjoint/pallas_call | solution.py:161
  403.5 4.2 %paste.1 = f32[1024,2048]{1,0:T(8,128)} custom-call(s32[3]{0:T(128)} %pad_add_fusion.place_ref.core_ref, f32[1024,1024]{1,0:T(8,128)} %collective-permute-done.30.arrived, f32[1024,2048]{1,0:T(8,128)} %adjoint.9.before), custom_call_target="tpu_custom_call", output_to_operand_aliasing={{}: (2, {})} | custom-call | flops 1 | bytes 1 | tf_op jit(solution)/shard_map/paste/pallas_call | solution.py:387
  (92 shorter events, 24.4 us)
Async XLA Ops:
  6.5 186.5 %all-reduce.5.cloned.1.call-start = ((), (), s32[]{:S(2)}) async-start(), calls=%async_computation | async-start | bytes 1572864 | tf_op jit(solution)/shard_map/psum | solution.py:505
  9.8 7.8 %copy-start.16 = (f32[192,1024]{1,0:T(8,128)S(1)}, f32[192,1024]{1,0:T(8,128)}, u32[]{:S(2)}) copy-start(f32[192,1024]{1,0:T(8,128)} %get-tuple-element.98) | copy-start | bytes 2359300
  14.2 40.1 %collective-permute-start.2 = (f32[1024,1024]{1,0:T(8,128)}, f32[1024,1024]{1,0:T(8,128)}, u32[]{:S(2)}, u32[]{:S(2)}) collective-permute-start(f32[1024,1024]{1,0:T(8,128)} %side.1), channel_id=1, source_target_pairs={{0,1},{1,0},{2,3},{3,2},{4,5},{5,4},{6,7},{7,6},{8,9},{9,8},{10,11... | collective-permute-start | bytes 12582920 | tf_op jit(solution)/shard_map/ppermute | solution.py:31
  14.9 22.2 %collective-permute-start.3 = (f32[192,1024]{1,0:T(8,128)}, f32[192,1024]{1,0:T(8,128)S(1)}, u32[]{:S(2)}, u32[]{:S(2)}) collective-permute-start(f32[192,1024]{1,0:T(8,128)} %get-tuple-element.103), channel_id=1, source_target_pairs={{8,0},{16,8},{24,16},{9,1},{17,9},{25,17},{10,2},{18,10},{26,18},{... | collective-permute-start | bytes 2359304 | tf_op jit(solution)/shard_map/ppermute | solution.py:22
  16.9 20.3 %collective-permute-start.5 = (f32[192,1024]{1,0:T(8,128)}, f32[192,1024]{1,0:T(8,128)S(1)}, u32[]{:S(2)}, u32[]{:S(2)}) collective-permute-start(f32[192,1024]{1,0:T(8,128)} %get-tuple-element.110), channel_id=1, source_target_pairs={{24,0},{25,1},{26,2},{27,3},{28,4},{29,5},{30,6},{31,7}} | collective-permute-start | bytes 2359304 | tf_op jit(solution)/shard_map/ppermute | solution.py:22
  17.6 36.7 %collective-permute-start.1 = (f32[192,1024]{1,0:T(8,128)S(1)}, f32[192,1024]{1,0:T(8,128)S(1)}, u32[]{:S(2)}, u32[]{:S(2)}) collective-permute-start(f32[192,1024]{1,0:T(8,128)S(1)} %copy-done.16), channel_id=1, source_target_pairs={{16,0},{24,8},{17,1},{25,9},{18,2},{26,10},{19,3},{27,11},{20,4},{... | collective-permute-start | bytes 2359304 | tf_op jit(solution)/shard_map/ppermute | solution.py:22
  37.1 17.2 %copy-start.3 = (f32[192,1024]{1,0:T(8,128)}, f32[192,1024]{1,0:T(8,128)S(1)}, u32[]{:S(2)}) copy-start(f32[192,1024]{1,0:T(8,128)S(1)} %collective-permute-done.3.refs_0_.refs_5_) | copy-start | bytes 2359300
  37.1 17.2 %copy-start.4 = (f32[192,1024]{1,0:T(8,128)}, f32[192,1024]{1,0:T(8,128)S(1)}, u32[]{:S(2)}) copy-start(f32[192,1024]{1,0:T(8,128)S(1)} %collective-permute-done.5.refs_2_.refs_7_) | copy-start | bytes 2359300
  57.9 20.6 %collective-permute-start.6 = (f32[576,1024]{1,0:T(8,128)}, f32[576,1024]{1,0:T(8,128)}, u32[]{:S(2)}, u32[]{:S(2)}) collective-permute-start(f32[576,1024]{1,0:T(8,128)} %stack.14), channel_id=1, source_target_pairs={{0,1},{1,0},{2,3},{3,2},{4,5},{5,4},{6,7},{7,6},{8,9},{9,8},{10,11... | collective-permute-start | bytes 7077896 | tf_op jit(solution)/shard_map/ppermute | solution.py:31
  58.4 36.2 %collective-permute-start.4 = (f32[192,1024]{1,0:T(8,128)}, f32[192,1024]{1,0:T(8,128)}, u32[]{:S(2)}, u32[]{:S(2)}) collective-permute-start(f32[192,1024]{1,0:T(8,128)} %get-tuple-element.105), channel_id=1, source_target_pairs={{8,0},{16,8},{24,16},{9,1},{17,9},{25,17},{10,2},{18,10},{26,18},{... | collective-permute-start | bytes 2359304 | tf_op jit(solution)/shard_map/ppermute | solution.py:22
  62.4 35.4 %collective-permute-start.8 = (f32[192,1024]{1,0:T(8,128)}, f32[192,1024]{1,0:T(8,128)}, u32[]{:S(2)}, u32[]{:S(2)}) collective-permute-start(f32[192,1024]{1,0:T(8,128)} %get-tuple-element.121), channel_id=1, source_target_pairs={{16,0},{24,8},{17,1},{25,9},{18,2},{26,10},{19,3},{27,11},{20,4},{... | collective-permute-start | bytes 2359304 | tf_op jit(solution)/shard_map/ppermute | solution.py:22
  63.7 34.1 %collective-permute-start.9 = (f32[192,1024]{1,0:T(8,128)}, f32[192,1024]{1,0:T(8,128)}, u32[]{:S(2)}, u32[]{:S(2)}) collective-permute-start(f32[192,1024]{1,0:T(8,128)} %get-tuple-element.124), channel_id=1, source_target_pairs={{24,0},{25,1},{26,2},{27,3},{28,4},{29,5},{30,6},{31,7}} | collective-permute-start | bytes 2359304 | tf_op jit(solution)/shard_map/ppermute | solution.py:22
  68.8 37.4 %collective-permute-start = (f32[768,1024]{1,0:T(8,128)}, f32[768,1024]{1,0:T(8,128)S(1)}, u32[]{:S(2)}, u32[]{:S(2)}) collective-permute-start(f32[768,1024]{1,0:T(8,128)} %cut.3), channel_id=1, source_target_pairs={{0,1},{1,0},{2,3},{3,2},{4,5},{5,4},{6,7},{7,6},{8,9},{9,8},{10,11... | collective-permute-start | bytes 9437192 | tf_op jit(solution)/shard_map/ppermute | solution.py:31
  94.6 10.8 %copy-start.15 = (f32[1,768]{1,0:T(1,128)S(1)}, f32[1,768]{1,0:T(1,128)}, u32[]{:S(2)}) copy-start(f32[1,768]{1,0:T(1,128)} %param.6) | copy-start | bytes 9220
  100.5 23.5 %collective-permute-start.10 = (f32[576,1024]{1,0:T(8,128)}, f32[576,1024]{1,0:T(8,128)}, u32[]{:S(2)}, u32[]{:S(2)}) collective-permute-start(f32[576,1024]{1,0:T(8,128)} %stack.15), channel_id=1, source_target_pairs={{0,1},{1,0},{2,3},{3,2},{4,5},{5,4},{6,7},{7,6},{8,9},{9,8},{10,11... | collective-permute-start | bytes 7077896 | tf_op jit(solution)/shard_map/ppermute | solution.py:31
  101.0 22.9 %collective-permute-start.7 = (f32[192,1024]{1,0:T(8,128)}, f32[192,1024]{1,0:T(8,128)}, u32[]{:S(2)}, u32[]{:S(2)}) collective-permute-start(f32[192,1024]{1,0:T(8,128)} %get-tuple-element.117), channel_id=1, source_target_pairs={{0,24},{8,0},{16,8},{24,16},{1,25},{9,1},{17,9},{25,17},{2,26},{10... | collective-permute-start | bytes 2359304 | tf_op jit(solution)/shard_map/ppermute | solution.py:27
  103.5 36.6 %collective-permute-start.12 = (f32[192,1024]{1,0:T(8,128)}, f32[192,1024]{1,0:T(8,128)}, u32[]{:S(2)}, u32[]{:S(2)}) collective-permute-start(f32[192,1024]{1,0:T(8,128)} %get-tuple-element.132), channel_id=1, source_target_pairs={{0,16},{8,24},{16,0},{24,8},{1,17},{9,25},{17,1},{25,9},{2,18},{10... | collective-permute-start | bytes 2359304 | tf_op jit(solution)/shard_map/ppermute | solution.py:27
  103.5 36.6 %collective-permute-start.14 = (f32[192,1024]{1,0:T(8,128)}, f32[192,1024]{1,0:T(8,128)}, u32[]{:S(2)}, u32[]{:S(2)}) collective-permute-start(f32[192,1024]{1,0:T(8,128)} %get-tuple-element.135), channel_id=1, source_target_pairs={{0,8},{8,16},{16,24},{24,0},{1,9},{9,17},{17,25},{25,1},{2,10},{10... | collective-permute-start | bytes 2359304 | tf_op jit(solution)/shard_map/ppermute | solution.py:27
  106.2 1.7 copy-start
  144.9 5.2 %collective-permute-start.16 = (f32[576,1024]{1,0:T(8,128)}, f32[576,1024]{1,0:T(8,128)S(1)}, u32[]{:S(2)}, u32[]{:S(2)}) collective-permute-start(f32[576,1024]{1,0:T(8,128)} %get-tuple-element.143), channel_id=1, source_target_pairs={{0,1},{1,0},{2,3},{3,2},{4,5},{5,4},{6,7},{7,6},{8,9},{9,8},{10,11... | collective-permute-start | bytes 7077896 | tf_op jit(solution)/shard_map/ppermute | solution.py:31
  145.6 19.4 %collective-permute-start.15 = (f32[192,1024]{1,0:T(8,128)}, f32[192,1024]{1,0:T(8,128)S(1)}, u32[]{:S(2)}, u32[]{:S(2)}) collective-permute-start(f32[192,1024]{1,0:T(8,128)} %get-tuple-element.137), channel_id=1, source_target_pairs={{0,8},{8,16},{16,24},{24,0},{1,9},{9,17},{17,25},{25,1},{2,10},{10... | collective-permute-start | bytes 2359304 | tf_op jit(solution)/shard_map/ppermute | solution.py:27
  147.3 36.0 %collective-permute-start.13 = (f32[192,1024]{1,0:T(8,128)}, f32[192,1024]{1,0:T(8,128)}, u32[]{:S(2)}, u32[]{:S(2)}) collective-permute-start(f32[192,1024]{1,0:T(8,128)} %get-tuple-element.134), channel_id=1, source_target_pairs={{0,16},{8,24},{16,0},{24,8},{1,17},{9,25},{17,1},{25,9},{2,18},{10... | collective-permute-start | bytes 2359304 | tf_op jit(solution)/shard_map/ppermute | solution.py:27
  147.3 36.0 %collective-permute-start.11 = (f32[192,1024]{1,0:T(8,128)}, f32[192,1024]{1,0:T(8,128)}, u32[]{:S(2)}, u32[]{:S(2)}) collective-permute-start(f32[192,1024]{1,0:T(8,128)} %get-tuple-element.131), channel_id=1, source_target_pairs={{0,24},{8,0},{16,8},{24,16},{1,25},{9,1},{17,9},{25,17},{2,26},{10... | collective-permute-start | bytes 2359304 | tf_op jit(solution)/shard_map/ppermute | solution.py:27
  147.6 94.8 %all-reduce.7.cloned.1.call-start = ((), (), s32[]{:S(2)}) async-start(), calls=%async_computation.1 | async-start | bytes 1572864 | tf_op jit(solution)/shard_map/psum | solution.py:505
  150.0 1.5 copy-start.2
  165.1 28.0 %copy-start.6 = (f32[192,1024]{1,0:T(8,128)}, f32[192,1024]{1,0:T(8,128)S(1)}, u32[]{:S(2)}) copy-start(f32[192,1024]{1,0:T(8,128)S(1)} %collective-permute-done.15.refs_2_.refs_7_) | copy-start | bytes 2359300
  198.5 5.7 %collective-permute-start.20 = (f32[576,1024]{1,0:T(8,128)}, f32[576,1024]{1,0:T(8,128)S(1)}, u32[]{:S(2)}, u32[]{:S(2)}) collective-permute-start(f32[576,1024]{1,0:T(8,128)} %get-tuple-element.152), channel_id=1, source_target_pairs={{0,1},{1,0},{2,3},{3,2},{4,5},{5,4},{6,7},{7,6},{8,9},{9,8},{10,11... | collective-permute-start | bytes 7077896 | tf_op jit(solution)/shard_map/ppermute | solution.py:31
  199.4 92.3 %all-reduce.9.cloned.1.call-start = ((), (), s32[]{:S(2)}) async-start(), calls=%async_computation.2 | async-start | bytes 1572864 | tf_op jit(solution)/shard_map/psum | solution.py:505
  199.4 42.9 %collective-permute-start.17 = (f32[192,1024]{1,0:T(8,128)}, f32[192,1024]{1,0:T(8,128)S(1)}, u32[]{:S(2)}, u32[]{:S(2)}) collective-permute-start(f32[192,1024]{1,0:T(8,128)} %get-tuple-element.147), channel_id=1, source_target_pairs={{0,24},{8,0},{16,8},{24,16},{1,25},{9,1},{17,9},{25,17},{2,26},{10... | collective-permute-start | bytes 2359304 | tf_op jit(solution)/shard_map/ppermute | solution.py:27
  199.8 42.6 %collective-permute-start.18 = (f32[192,1024]{1,0:T(8,128)}, f32[192,1024]{1,0:T(8,128)}, u32[]{:S(2)}, u32[]{:S(2)}) collective-permute-start(f32[192,1024]{1,0:T(8,128)} %get-tuple-element.148), channel_id=1, source_target_pairs={{0,16},{8,24},{16,0},{24,8},{1,17},{9,25},{17,1},{25,9},{2,18},{10... | collective-permute-start | bytes 2359304 | tf_op jit(solution)/shard_map/ppermute | solution.py:27
  201.3 41.1 %collective-permute-start.19 = (f32[192,1024]{1,0:T(8,128)}, f32[192,1024]{1,0:T(8,128)}, u32[]{:S(2)}, u32[]{:S(2)}) collective-permute-start(f32[192,1024]{1,0:T(8,128)} %get-tuple-element.149), channel_id=1, source_target_pairs={{0,8},{8,16},{16,24},{24,0},{1,9},{9,17},{17,25},{25,1},{2,10},{10... | collective-permute-start | bytes 2359304 | tf_op jit(solution)/shard_map/ppermute | solution.py:27
  204.3 1.5 copy-start.1
  248.4 92.0 %all-reduce.11.cloned.1.call-start = ((), (), s32[]{:S(2)}) async-start(), calls=%async_computation.3 | async-start | bytes 1572864 | tf_op jit(solution)/shard_map/psum | solution.py:505
  248.4 43.3 %collective-permute-start.23 = (f32[192,1024]{1,0:T(8,128)}, f32[192,1024]{1,0:T(8,128)S(1)}, u32[]{:S(2)}, u32[]{:S(2)}) collective-permute-start(f32[192,1024]{1,0:T(8,128)} %get-tuple-element.165), channel_id=1, source_target_pairs={{0,8},{8,16},{16,24},{24,0},{1,9},{9,17},{17,25},{25,1},{2,10},{10... | collective-permute-start | bytes 2359304 | tf_op jit(solution)/shard_map/ppermute | solution.py:27
  249.8 42.0 %collective-permute-start.22 = (f32[192,1024]{1,0:T(8,128)}, f32[192,1024]{1,0:T(8,128)S(1)}, u32[]{:S(2)}, u32[]{:S(2)}) collective-permute-start(f32[192,1024]{1,0:T(8,128)} %get-tuple-element.163), channel_id=1, source_target_pairs={{0,16},{8,24},{16,0},{24,8},{1,17},{9,25},{17,1},{25,9},{2,18},{10... | collective-permute-start | bytes 2359304 | tf_op jit(solution)/shard_map/ppermute | solution.py:27
  250.0 41.8 %collective-permute-start.21 = (f32[192,1024]{1,0:T(8,128)}, f32[192,1024]{1,0:T(8,128)S(1)}, u32[]{:S(2)}, u32[]{:S(2)}) collective-permute-start(f32[192,1024]{1,0:T(8,128)} %get-tuple-element.156), channel_id=1, source_target_pairs={{0,24},{8,0},{16,8},{24,16},{1,25},{9,1},{17,9},{25,17},{2,26},{10... | collective-permute-start | bytes 2359304 | tf_op jit(solution)/shard_map/ppermute | solution.py:27
  291.7 5.5 %copy-start.14 = (f32[192,1024]{1,0:T(8,128)S(1)}, f32[192,1024]{1,0:T(8,128)}, u32[]{:S(2)}) copy-start(f32[192,1024]{1,0:T(8,128)} %all-reduce.9.cloned.1.call-done.refs_0_) | copy-start | bytes 2359300
  291.8 1.2 copy-start.12
  291.8 1.4 copy-start.13
  297.2 43.1 %collective-permute-start.24 = (f32[192,1024]{1,0:T(8,128)S(1)}, f32[192,1024]{1,0:T(8,128)}, u32[]{:S(2)}, u32[]{:S(2)}) collective-permute-start(f32[192,1024]{1,0:T(8,128)S(1)} %copy-done.14), channel_id=1, source_target_pairs={{8,0},{16,8},{24,16},{9,1},{17,9},{25,17},{10,2},{18,10},{26,18},{... | collective-permute-start | bytes 2359304 | tf_op jit(solution)/shard_map/ppermute | solution.py:22
  299.4 43.1 %collective-permute-start.26 = (f32[192,1024]{1,0:T(8,128)S(1)}, f32[192,1024]{1,0:T(8,128)}, u32[]{:S(2)}, u32[]{:S(2)}) collective-permute-start(f32[192,1024]{1,0:T(8,128)S(1)} %copy-done.14), channel_id=1, source_target_pairs={{16,0},{24,8},{17,1},{25,9},{18,2},{26,10},{19,3},{27,11},{20,4},{... | collective-permute-start | bytes 2359304 | tf_op jit(solution)/shard_map/ppermute | solution.py:22
  300.7 43.1 %collective-permute-start.28 = (f32[192,1024]{1,0:T(8,128)S(1)}, f32[192,1024]{1,0:T(8,128)}, u32[]{:S(2)}, u32[]{:S(2)}) collective-permute-start(f32[192,1024]{1,0:T(8,128)S(1)} %copy-done.14), channel_id=1, source_target_pairs={{24,0},{25,1},{26,2},{27,3},{28,4},{29,5},{30,6},{31,7}} | collective-permute-start | bytes 2359304 | tf_op jit(solution)/shard_map/ppermute | solution.py:22
  340.4 21.4 %collective-permute-start.25 = (f32[192,1024]{1,0:T(8,128)}, f32[192,1024]{1,0:T(8,128)S(1)}, u32[]{:S(2)}, u32[]{:S(2)}) collective-permute-start(f32[192,1024]{1,0:T(8,128)} %all-reduce.11.cloned.1.call-done.refs_0_), channel_id=1, source_target_pairs={{8,0},{16,8},{24,16},{9,1},{17,9},{25,17},{10,2},{18,10},{26,18},{... | collective-permute-start | bytes 2359304 | tf_op jit(solution)/shard_map/ppermute | solution.py:22
  342.6 37.1 %collective-permute-start.27 = (f32[192,1024]{1,0:T(8,128)}, f32[192,1024]{1,0:T(8,128)S(1)}, u32[]{:S(2)}, u32[]{:S(2)}) collective-permute-start(f32[192,1024]{1,0:T(8,128)} %all-reduce.11.cloned.1.call-done.refs_0_), channel_id=1, source_target_pairs={{16,0},{24,8},{17,1},{25,9},{18,2},{26,10},{19,3},{27,11},{20,4},{... | collective-permute-start | bytes 2359304 | tf_op jit(solution)/shard_map/ppermute | solution.py:22
  343.9 35.8 %collective-permute-start.29 = (f32[192,1024]{1,0:T(8,128)}, f32[192,1024]{1,0:T(8,128)S(1)}, u32[]{:S(2)}, u32[]{:S(2)}) collective-permute-start(f32[192,1024]{1,0:T(8,128)} %all-reduce.11.cloned.1.call-done.refs_0_), channel_id=1, source_target_pairs={{24,0},{25,1},{26,2},{27,3},{28,4},{29,5},{30,6},{31,7}} | collective-permute-start | bytes 2359304 | tf_op jit(solution)/shard_map/ppermute | solution.py:22
  361.7 18.0 %copy-start.7 = (f32[192,1024]{1,0:T(8,128)}, f32[192,1024]{1,0:T(8,128)S(1)}, u32[]{:S(2)}) copy-start(f32[192,1024]{1,0:T(8,128)S(1)} %collective-permute-done.25.refs_1_) | copy-start | bytes 2359300
  379.7 1.2 copy-start.9
  391.9 11.6 %collective-permute-start.30 = (f32[1024,1024]{1,0:T(8,128)}, f32[1024,1024]{1,0:T(8,128)}, u32[]{:S(2)}, u32[]{:S(2)}) collective-permute-start(f32[1024,1024]{1,0:T(8,128)} %adjoint.8), channel_id=1, source_target_pairs={{0,1},{1,0},{2,3},{3,2},{4,5},{5,4},{6,7},{7,6},{8,9},{9,8},{10,11... | collective-permute-start | bytes 12582920 | tf_op jit(solution)/shard_map/ppermute | solution.py:31
  (4 other events, 3.7 us)
Sparse Core Ops, SparseCore 0:
  147.7 45.2 all-reduce.4
  199.5 42.8 all-reduce.6
  248.5 43.2 all-reduce.8
  297.3 42.9 all-reduce.10

commit v4 on v3

--- a/solution.py
+++ b/solution.py
@@ -179,9 +179,12 @@
     )(place, *weighted, *foot, *earlier)
 
 
-def through(buffer, sems, moves):
-    loads = [pltpu.make_async_copy(a, buffer.at[i], sems.at[0, i]) for i, (a, _) in enumerate(moves)]
-    stores = [pltpu.make_async_copy(buffer.at[i], b, sems.at[1, i]) for i, (_, b) in enumerate(moves)]
+def through(*passages):
+    loads, stores = [], []
+    for buffer, sems, moves in passages:
+        for i, (source, target) in enumerate(moves):
+            loads.append(pltpu.make_async_copy(source, buffer.at[i], sems.at[0, i]))
+            stores.append(pltpu.make_async_copy(buffer.at[i], target, sems.at[1, i]))
     for load in loads:
         load.start()
     for load, store in zip(loads, stores):
@@ -198,9 +201,8 @@
 def cut_kernel(lags, r, footprint, *refs):
     outs, buffer, sems = refs[:-2], refs[-2], refs[-1]
     rows = outs[0].shape[0]
-    through(buffer, sems, [
-        (footprint.at[0, lag, pl.ds(r * rows, rows), :], out) for lag, out in zip(lags, outs)
-    ])
+    moves = [(footprint.at[0, lag, pl.ds(r * rows, rows), :], out) for lag, out in zip(lags, outs)]
+    through((buffer, sems, moves))
 
 
 def cut(footprint, lags, rows, r):
@@ -218,7 +220,8 @@
 def stack_kernel(*refs):
     pieces, out, buffer, sems = refs[:-3], refs[-3], refs[-2], refs[-1]
     rows = pieces[0].shape[0]
-    through(buffer, sems, [(piece, out.at[pl.ds(i * rows, rows), :]) for i, piece in enumerate(pieces)])
+    moves = [(piece, out.at[pl.ds(i * rows, rows), :]) for i, piece in enumerate(pieces)]
+    through((buffer, sems, moves))
 
 
 def stack(pieces):
@@ -234,25 +237,37 @@
     )(*pieces)
 
 
-def side_kernel(parts, place_ref, flux, out, buffer, sems):
-    cells, half = out.shape
-    rows = cells // parts
+def opening_kernel(lags, place_ref, footprint, flux, *refs):
+    pieces, (side, buffer, sems, side_buffer, side_sems) = refs[:len(lags)], refs[len(lags):]
+    rows = pieces[0].shape[0]
+    cells, half = side.shape
+    band = cells // PARTS
     left = pl.multiple_of((1 - place_ref[0]) * half, 128)
-    bands = [pl.ds(i * rows, rows) for i in range(parts)]
-    through(buffer, sems, [(flux.at[0, at, pl.ds(left, half)], out.at[at, :]) for at in bands])
-
-
-def side_of(flux, place):
+    bands = [pl.ds(i * band, band) for i in range(PARTS)]
+    through(
+        (buffer, sems, [(footprint.at[0, lag, pl.ds(0, rows), :], out) for lag, out in zip(lags, pieces)]),
+        (side_buffer, side_sems, [(flux.at[0, at, pl.ds(left, half)], side.at[at, :]) for at in bands]),
+    )
+
+
+def opening(footprint, flux, lags, rows, place):
     _, cells, width = flux.shape
-    return pl.pallas_call(
-        functools.partial(side_kernel, PARTS),
-        in_specs=[pl.BlockSpec(memory_space=pltpu.SMEM), IN_PLACE],
-        out_specs=IN_PLACE,
-        scratch_shapes=passage(PARTS, cells // PARTS, width // 2),
-        out_shape=jax.ShapeDtypeStruct((cells, width // 2), jnp.float32),
-        name="side",
-        cost_estimate=LIGHT,
-    )(place, flux)
+    outs = pl.pallas_call(
+        functools.partial(opening_kernel, lags),
+        in_specs=[pl.BlockSpec(memory_space=pltpu.SMEM), IN_PLACE, IN_PLACE],
+        out_specs=[IN_PLACE] * (len(lags) + 1),
+        scratch_shapes=[
+            *passage(len(lags), rows, footprint.shape[3]),
+            *passage(PARTS, cells // PARTS, width // 2),
+        ],
+        out_shape=[
+            *[jax.ShapeDtypeStruct((rows, footprint.shape[3]), jnp.float32)] * len(lags),
+            jax.ShapeDtypeStruct((cells, width // 2), jnp.float32),
+        ],
+        name="opening",
+        cost_estimate=LIGHT,
+    )(place, footprint, flux)
+    return list(outs[:-1]), outs[-1]
 
 
 def meet_kernel(lows, highs, chosen, place_ref, scale, same, *refs):
@@ -379,7 +394,7 @@
     rows = cells // parts
     left = pl.multiple_of((1 - place_ref[0]) * half, 128)
     bands = [pl.ds(i * rows, rows) for i in range(parts)]
-    through(buffer, sems, [(arrived.at[at, :], out.at[at, pl.ds(left, half)]) for at in bands])
+    through((buffer, sems, [(arrived.at[at, :], out.at[at, pl.ds(left, half)]) for at in bands]))
 
 
 def paste(arrived, whole, place):
@@ -459,9 +474,9 @@
         return foot, [column(r)] + [column(i) for i in range(len(later))], before, half, False
 
     other, done = [], [None, None]
-    kind, sent = payload(0)
-    flux, sent[0] = together(flux, sent[0])
-    flux_other = swapped(side_of(flux, place))
+    kind = "down"
+    sent, side = opening(footprint, flux, later, rows, place)
+    flux_other = swapped(side)
     foot_other = swapped(cut(footprint, [0], slots, 0)[0])
     for k in range(CHUNKS + 4):
         h, p, w = k, k - 2, k - 4

time: 418 us -> 417 us (level)
    pallas_call x3 -> x2, Pallas kernels: 8.8 us -> 6.18 us  [cut(): pl.pallas_call(functools.partial(cut_kernel, lags, r), in_specs=[IN_PLACE...]
    unnamed x34 -> x32, local copies, waits for them, and re-layouts: 8.94 us -> 9.01 us
where the time goes in v4:
time: 417 us; the launch traced here: 413 us
  Pallas kernels  195 us (47%)
  waiting for transfers between devices  154 us (37%)
  starting transfers between devices  37.9 us (9%)
  between operations  14.1 us (3%)
  local copies, waits for them, and re-layouts  12.2 us (3%)
    psum x4, waiting for transfers between devices, on_device(): weighted.append(lax.psum(total, 'z'))  79.3 us
    pallas_call x5, Pallas kernels, adjoint(): pl.pallas_call(functools.partial(adjoint_kernel, count, len(sides), first...  70.5 us
    pallas_call x5, Pallas kernels, forward(): pl.pallas_call(functools.partial(forward_kernel, count), grid=(half // ti...  67.5 us
    ppermute x12, waiting for transfers between devices, shifted(): return lax.ppermute(value, 'tm', pairs)  54.4 us
    ppermute x12, starting transfers between devices, shifted(): return lax.ppermute(value, 'tm', pairs)  20.4 us
    pallas_call x4, Pallas kernels, meet(): pl.pallas_call(functools.partial(meet_kernel, lows, highs, chosen), in_sp...  19.2 us
    ppermute x12, waiting for transfers between devices, cycled(): lax.ppermute(value, 'tm', [(i, (i - by) % devices) for i in range(devices)])  18.9 us
    ppermute x12, starting transfers between devices, cycled(): lax.ppermute(value, 'tm', [(i, (i - by) % devices) for i in range(devices)])  12.9 us
  transfers between devices with their start and end apart: 35, of which 12 were waited for; matrix products, arithmetic and copies ran while one was open for 1% of the time, Pallas kernels for 37%

profile of v4, /device:TPU:3, one launch (start us, length us, event | category | flops | bytes accessed | tf_op | source)
XLA Modules:
  0.0 413.5 jit_solution(6281331703715922196)
XLA Ops:
  7.2 5.8 %opening.1 = (f32[192,1024]{1,0:T(8,128)}, f32[192,1024]{1,0:T(8,128)}, f32[192,1024]{1,0:T(8,128)}, f32[1024,1024]{1,0:T(8,128)}) custom-call(s32[3]{0:T(128)} %pad_add_fusion.place_ref.core_ref, f32[1,4,768,1024]{3,2,1,0:T(8,128)} %refs_4_.7, f32[1,1024,2048]{2,1,0:T(8,128)} %own.1), custom_call_target="tpu_custom_call" | custom-call | flops 1 | bytes 1 | tf_op jit(solution)/shard_map/opening/pallas_call | solution.py:255
  13.7 1.9 collective-permute-start.3
  17.7 2.6 cut.3
  20.3 15.6 %collective-permute-done.3.refs_0_.refs_5_ = f32[192,1024]{1,0:T(8,128)S(1)} collective-permute-done((f32[192,1024]{1,0:T(8,128)}, f32[192,1024]{1,0:T(8,128)S(1)}, u32[]{:S(2)}, u32[]{:S(2)}) %collective-permute-start.3) | collective-permute-done | bytes 786464 | tf_op jit(solution)/shard_map/ppermute | solution.py:22
  35.9 17.2 %collective-permute-done.1.refs_1_.refs_6_ = f32[192,1024]{1,0:T(8,128)S(1)} collective-permute-done((f32[192,1024]{1,0:T(8,128)}, f32[192,1024]{1,0:T(8,128)S(1)}, u32[]{:S(2)}, u32[]{:S(2)}) %collective-permute-start.1) | collective-permute-done | bytes 786464 | tf_op jit(solution)/shard_map/ppermute | solution.py:22
  54.0 2.6 stack.14
  57.2 4.2 %collective-permute-start.4 = (f32[192,1024]{1,0:T(8,128)}, f32[192,1024]{1,0:T(8,128)}, u32[]{:S(2)}, u32[]{:S(2)}) collective-permute-start(f32[192,1024]{1,0:T(8,128)} %get-tuple-element.103), channel_id=1, source_target_pairs={{8,0},{16,8},{24,16},{9,1},{17,9},{25,17},{10,2},{18,10},{26,18},{... | collective-permute-start | bytes 2359304 | tf_op jit(solution)/shard_map/ppermute | solution.py:22
  62.7 1.6 collective-permute-start.9
  64.3 3.6 cut.2
  68.2 9.2 %split.1.refs_8_.refs_6_ = bf16[6144,1024]{1,0:T(8,128)(2,1)} custom-call(s32[3]{0:T(128)} %pad_add_fusion.place_ref.core_ref, f32[1,1024,2048]{2,1,0:T(8,128)} %own.1, f32[1024,1024]{1,0:T(8,128)} %collective-permute-done.2.other), custom_call_target="tpu_custom_call" | custom-call | flops 1 | bytes 1 | tf_op jit(solution)/shard_map/split/pallas_call | solution.py:60
  77.4 12.8 %forward.6 = (f32[192,1024]{1,0:T(8,128)}, f32[192,1024]{1,0:T(8,128)}, f32[192,1024]{1,0:T(8,128)}) custom-call(f32[192,1024]{1,0:T(8,128)} %copy-done.3, f32[192,1024]{1,0:T(8,128)} %copy-done.5, f32[192,1024]{1,0:T(8,128)} %copy-done.4, f32[576,1024]{1,0:T(8,128)} %collective-permute-done.6.refs_3_.refs_4_.refs_5_.refs_9_.refs_10_.refs_11_, ...), custom_call_target="tpu_custom_call" | custom-call | flops 1 | bytes 1 | tf_op jit(solution)/shard_map/forward/pallas_call | solution.py:101
  90.3 3.3 choose.2
  93.6 3.0 collective-permute-done.8.refs_1_.refs_6_
  96.6 2.6 stack.15
  99.8 2.7 collective-permute-start.7
  105.3 1.7 copy-done
  106.9 16.1 %forward.5 = (f32[192,1024]{1,0:T(8,128)}, f32[192,1024]{1,0:T(8,128)}, f32[192,1024]{1,0:T(8,128)}, f32[192,1024]{1,0:T(8,128)}) custom-call(f32[1,4,768,1024]{3,2,1,0:T(8,128)} %refs_4_.7, f32[1,4,768,1024]{3,2,1,0:T(8,128)} %refs_4_.7, f32[1,4,768,1024]{3,2,1,0:T(8,128)} %refs_4_.7, f32[1,4,768,1024]{3,2,1,0:T(8,128)} %refs_4_.7, f32[768,1024]{1,0:T(8,128)} %copy-done, ...), custom_call_target="tpu_custom_call" | custom-call | flops 1 | bytes 1 | tf_op jit(solution)/shard_map/forward/pallas_call | solution.py:101
  123.0 12.9 %forward.7 = (f32[192,1024]{1,0:T(8,128)}, f32[192,1024]{1,0:T(8,128)}, f32[192,1024]{1,0:T(8,128)}) custom-call(f32[192,1024]{1,0:T(8,128)} %collective-permute-done.4.refs_0_.refs_5_, f32[192,1024]{1,0:T(8,128)} %collective-permute-done.8.refs_1_.refs_6_, f32[192,1024]{1,0:T(8,128)} %collective-permute-done.9.refs_2_.refs_7_, ...), custom_call_target="tpu_custom_call" | custom-call | flops 1 | bytes 1 | tf_op jit(solution)/shard_map/forward/pallas_call | solution.py:101
  135.9 3.3 choose.3
  139.2 4.7 %meet.4 = (f32[192,1024]{1,0:T(8,128)}, f32[576,1024]{1,0:T(8,128)}) custom-call(s32[3]{0:T(128)} %pad_add_fusion.place_ref.core_ref, f32[192,1]{1,0:T(8,128)} %copy.12.scale, f32[192,1024]{1,0:T(8,128)} %get-tuple-element.136.same, f32[192,1024]{1,0:T(8,128)} %collective-permute-done.7.refs_0_.refs_5_, f32[192,1024]{1,0:T(8,128)} %collective-permute-done.12.refs_1_.refs_6_, ...), custom_call_target="tpu_custom_call" | custom-call | flops 1 | bytes 1 | tf_op jit(solution)/shard_map/meet/pallas_call | solution.py:330
  144.7 1.7 collective-permute-start.15
  147.7 1.4 collective-permute-done.16.refs_3_.refs_4_.refs_5_.refs_9_.refs_10_.refs_11_
  149.1 1.5 copy-done.2
  150.6 12.9 %forward.8 = (f32[192,1024]{1,0:T(8,128)}, f32[192,1024]{1,0:T(8,128)}, f32[192,1024]{1,0:T(8,128)}) custom-call(f32[192,1024]{1,0:T(8,128)} %collective-permute-done.7.refs_0_.refs_5_, f32[192,1024]{1,0:T(8,128)} %collective-permute-done.12.refs_1_.refs_6_, f32[192,1024]{1,0:T(8,128)} %collective-permute-done.14.refs_2_.refs_7_, f32[576,1024]{1,0:T(8,128)} %copy-done.2, ...), custom_call_target="tpu_custom_call" | custom-call | flops 1 | bytes 1 | tf_op jit(solution)/shard_map/forward/pallas_call | solution.py:101
  164.2 18.2 %collective-permute-done.13.refs_1_.refs_6_ = f32[192,1024]{1,0:T(8,128)} collective-permute-done((f32[192,1024]{1,0:T(8,128)}, f32[192,1024]{1,0:T(8,128)}, u32[]{:S(2)}, u32[]{:S(2)}) %collective-permute-start.13) | collective-permute-done | bytes 786464 | tf_op jit(solution)/shard_map/ppermute | solution.py:27
  182.3 9.8 %all-reduce.5.cloned.1.call-done.refs_3_.refs_0_ = f32[192,1024]{1,0:T(8,128)} async-done(((f32[192,1024]{1,0:T(8,128)}), f32[192,1024]{1,0:T(8,128)}) %all-reduce.5.cloned.1.call-update) | async-done | bytes 786448 | tf_op jit(solution)/shard_map/psum | solution.py:520
  192.1 5.6 %meet.5 = (f32[192,1024]{1,0:T(8,128)}, f32[576,1024]{1,0:T(8,128)}, f32[192,1024]{1,0:T(8,128)}, f32[192,1024]{1,0:T(8,128)}, f32[192,1024]{1,0:T(8,128)}) custom-call(s32[3]{0:T(128)} %pad_add_fusion.place_ref.core_ref, f32[192,1]{1,0:T(8,128)} %copy.13.scale, f32[192,1024]{1,0:T(8,128)} %get-tuple-element.100.same, ...), custom_call_target="tpu_custom_call" | custom-call | flops 1 | bytes 1 | tf_op jit(solution)/shard_map/meet/pallas_call | solution.py:330
  198.9 1.6 collective-permute-start.18
  200.5 2.2 collective-permute-start.19
  203.4 1.4 copy-done.1
  204.9 12.8 %forward.9 = (f32[192,1024]{1,0:T(8,128)}, f32[192,1024]{1,0:T(8,128)}, f32[192,1024]{1,0:T(8,128)}) custom-call(f32[192,1024]{1,0:T(8,128)} %collective-permute-done.11.refs_0_.refs_5_, f32[192,1024]{1,0:T(8,128)} %collective-permute-done.13.refs_1_.refs_6_, f32[192,1024]{1,0:T(8,128)} %copy-done.6, f32[576,1024]{1,0:T(8,128)} %copy-done.1, ...), custom_call_target="tpu_custom_call" | custom-call | flops 1 | bytes 1 | tf_op jit(solution)/shard_map/forward/pallas_call | solution.py:101
  217.7 23.8 %all-reduce.7.cloned.1.call-done.refs_3_.refs_0_ = f32[192,1024]{1,0:T(8,128)} async-done(((f32[192,1024]{1,0:T(8,128)}), f32[192,1024]{1,0:T(8,128)}) %all-reduce.7.cloned.1.call-update) | async-done | bytes 786448 | tf_op jit(solution)/shard_map/psum | solution.py:520
  242.5 5.0 %meet.6 = (f32[192,1024]{1,0:T(8,128)}, f32[192,1024]{1,0:T(8,128)}, f32[192,1024]{1,0:T(8,128)}, f32[192,1024]{1,0:T(8,128)}) custom-call(s32[3]{0:T(128)} %pad_add_fusion.place_ref.core_ref, f32[192,1]{1,0:T(8,128)} %copy.14.scale, f32[192,1024]{1,0:T(8,128)} %get-tuple-element.99.same, f32[192,1024]{1,0:T(8,128)} %copy-done.10, ...), custom_call_target="tpu_custom_call" | custom-call | flops 1 | bytes 1 | tf_op jit(solution)/shard_map/meet/pallas_call | solution.py:330
  247.6 1.3 collective-permute-start.23
  249.2 1.4 collective-permute-start.21
  251.3 15.7 %adjoint.5 = (f32[1024,2048]{1,0:T(8,128)}, f32[1024,1024]{1,0:T(8,128)}) custom-call(s32[3]{0:T(128)} %pad_add_fusion.place_ref.core_ref, f32[192,1024]{1,0:T(8,128)} %all-reduce.5.cloned.1.call-done.refs_3_.refs_0_, f32[192,1024]{1,0:T(8,128)} %copy-done.10, f32[192,1024]{1,0:T(8,128)} %collective-permute-done.18.refs_1_.refs_2_, ...), custom_call_target="tpu_custom_call" | custom-call | flops 1 | bytes 1 | tf_op jit(solution)/shard_map/adjoint/pallas_call | solution.py:161
  267.0 23.9 %all-reduce.9.cloned.1.call-done.refs_0_ = f32[192,1024]{1,0:T(8,128)} async-done(((f32[192,1024]{1,0:T(8,128)}), f32[192,1024]{1,0:T(8,128)}) %all-reduce.9.cloned.1.call-update) | async-done | bytes 786448 | tf_op jit(solution)/shard_map/psum | solution.py:520
  292.4 3.9 meet.7
  296.4 2.2 collective-permute-start.24
  299.9 1.6 collective-permute-start.28
  301.5 16.3 %adjoint.6 = (f32[1024,2048]{1,0:T(8,128)}, f32[1024,1024]{1,0:T(8,128)}) custom-call(s32[3]{0:T(128)} %pad_add_fusion.place_ref.core_ref, f32[192,1024]{1,0:T(8,128)} %all-reduce.7.cloned.1.call-done.refs_3_.refs_0_, f32[192,1024]{1,0:T(8,128)} %copy-done.13, f32[192,1024]{1,0:T(8,128)} %copy-done.12, ...), custom_call_target="tpu_custom_call", output_to_operand_aliasing={{0}: (13, {}), {1}: (14, {})} | custom-call | flops 1 | bytes 1 | tf_op jit(solution)/shard_map/adjoint/pallas_call | solution.py:161
  317.8 21.7 %all-reduce.11.cloned.1.call-done.refs_0_ = f32[192,1024]{1,0:T(8,128)} async-done(((f32[192,1024]{1,0:T(8,128)}), f32[192,1024]{1,0:T(8,128)}) %all-reduce.11.cloned.1.call-update) | async-done | bytes 786448 | tf_op jit(solution)/shard_map/psum | solution.py:520
  339.5 2.2 collective-permute-start.25
  344.0 16.3 %adjoint.7 = (f32[1024,2048]{1,0:T(8,128)}, f32[1024,1024]{1,0:T(8,128)}) custom-call(s32[3]{0:T(128)} %pad_add_fusion.place_ref.core_ref, f32[192,1024]{1,0:T(8,128)} %all-reduce.9.cloned.1.call-done.refs_0_, f32[192,1024]{1,0:T(8,128)} %collective-permute-done.24.refs_1_, ...), custom_call_target="tpu_custom_call", output_to_operand_aliasing={{0}: (13, {}), {1}: (14, {})} | custom-call | flops 1 | bytes 1 | tf_op jit(solution)/shard_map/adjoint/pallas_call | solution.py:161
  360.9 18.0 %collective-permute-done.27.refs_2_ = f32[192,1024]{1,0:T(8,128)S(1)} collective-permute-done((f32[192,1024]{1,0:T(8,128)}, f32[192,1024]{1,0:T(8,128)S(1)}, u32[]{:S(2)}, u32[]{:S(2)}) %collective-permute-start.27) | collective-permute-done | bytes 786464 | tf_op jit(solution)/shard_map/ppermute | solution.py:22
  380.0 11.1 %adjoint.8 = f32[1024,1024]{1,0:T(8,128)} custom-call(s32[3]{0:T(128)} %pad_add_fusion.place_ref.core_ref, f32[192,1024]{1,0:T(8,128)} %all-reduce.11.cloned.1.call-done.refs_0_, f32[192,1024]{1,0:T(8,128)} %copy-done.7, f32[192,1024]{1,0:T(8,128)} %copy-done.8, f32[192,1024]{1,0:T(8,128)} %copy-done.9, ...), custom_call_target="tpu_custom_call", output_to_operand_aliasing={{}: (9, {})} | custom-call | flops 1 | bytes 1 | tf_op jit(solution)/shard_map/adjoint/pallas_call | solution.py:161
  391.6 11.1 %adjoint.9.before = f32[1024,2048]{1,0:T(8,128)} custom-call(s32[3]{0:T(128)} %pad_add_fusion.place_ref.core_ref, f32[192,1024]{1,0:T(8,128)} %all-reduce.11.cloned.1.call-done.refs_0_, f32[192,1024]{1,0:T(8,128)} %copy-done.7, f32[192,1024]{1,0:T(8,128)} %copy-done.8, f32[192,1024]{1,0:T(8,128)} %copy-done.9, ...), custom_call_target="tpu_custom_call", output_to_operand_aliasing={{}: (9, {})} | custom-call | flops 1 | bytes 1 | tf_op jit(solution)/shard_map/adjoint/pallas_call | solution.py:161
  402.7 4.2 %paste.1 = f32[1024,2048]{1,0:T(8,128)} custom-call(s32[3]{0:T(128)} %pad_add_fusion.place_ref.core_ref, f32[1024,1024]{1,0:T(8,128)} %collective-permute-done.30.arrived, f32[1024,2048]{1,0:T(8,128)} %adjoint.9.before), custom_call_target="tpu_custom_call", output_to_operand_aliasing={{}: (2, {})} | custom-call | flops 1 | bytes 1 | tf_op jit(solution)/shard_map/paste/pallas_call | solution.py:402
  (89 shorter events, 23.1 us)
Async XLA Ops:
  6.5 185.6 %all-reduce.5.cloned.1.call-start = ((), (), s32[]{:S(2)}) async-start(), calls=%async_computation | async-start | bytes 1572864 | tf_op jit(solution)/shard_map/psum | solution.py:520
  13.0 40.1 %collective-permute-start.2 = (f32[1024,1024]{1,0:T(8,128)}, f32[1024,1024]{1,0:T(8,128)}, u32[]{:S(2)}, u32[]{:S(2)}) collective-permute-start(f32[1024,1024]{1,0:T(8,128)} %get-tuple-element.96), channel_id=1, source_target_pairs={{0,1},{1,0},{2,3},{3,2},{4,5},{5,4},{6,7},{7,6},{8,9},{9,8},{10,11... | collective-permute-start | bytes 12582920 | tf_op jit(solution)/shard_map/ppermute | solution.py:31
  13.7 22.2 %collective-permute-start.3 = (f32[192,1024]{1,0:T(8,128)}, f32[192,1024]{1,0:T(8,128)S(1)}, u32[]{:S(2)}, u32[]{:S(2)}) collective-permute-start(f32[192,1024]{1,0:T(8,128)} %get-tuple-element.101), channel_id=1, source_target_pairs={{8,0},{16,8},{24,16},{9,1},{17,9},{25,17},{10,2},{18,10},{26,18},{... | collective-permute-start | bytes 2359304 | tf_op jit(solution)/shard_map/ppermute | solution.py:22
  15.7 20.3 %collective-permute-start.5 = (f32[192,1024]{1,0:T(8,128)}, f32[192,1024]{1,0:T(8,128)S(1)}, u32[]{:S(2)}, u32[]{:S(2)}) collective-permute-start(f32[192,1024]{1,0:T(8,128)} %get-tuple-element.108), channel_id=1, source_target_pairs={{24,0},{25,1},{26,2},{27,3},{28,4},{29,5},{30,6},{31,7}} | collective-permute-start | bytes 2359304 | tf_op jit(solution)/shard_map/ppermute | solution.py:22
  16.4 36.7 %collective-permute-start.1 = (f32[192,1024]{1,0:T(8,128)}, f32[192,1024]{1,0:T(8,128)S(1)}, u32[]{:S(2)}, u32[]{:S(2)}) collective-permute-start(f32[192,1024]{1,0:T(8,128)} %get-tuple-element.95), channel_id=1, source_target_pairs={{16,0},{24,8},{17,1},{25,9},{18,2},{26,10},{19,3},{27,11},{20,4},{... | collective-permute-start | bytes 2359304 | tf_op jit(solution)/shard_map/ppermute | solution.py:22
  35.9 17.2 %copy-start.3 = (f32[192,1024]{1,0:T(8,128)}, f32[192,1024]{1,0:T(8,128)S(1)}, u32[]{:S(2)}) copy-start(f32[192,1024]{1,0:T(8,128)S(1)} %collective-permute-done.3.refs_0_.refs_5_) | copy-start | bytes 2359300
  35.9 17.2 %copy-start.4 = (f32[192,1024]{1,0:T(8,128)}, f32[192,1024]{1,0:T(8,128)S(1)}, u32[]{:S(2)}) copy-start(f32[192,1024]{1,0:T(8,128)S(1)} %collective-permute-done.5.refs_2_.refs_7_) | copy-start | bytes 2359300
  53.1 0.9 copy-start.5
  56.7 20.8 %collective-permute-start.6 = (f32[576,1024]{1,0:T(8,128)}, f32[576,1024]{1,0:T(8,128)}, u32[]{:S(2)}, u32[]{:S(2)}) collective-permute-start(f32[576,1024]{1,0:T(8,128)} %stack.14), channel_id=1, source_target_pairs={{0,1},{1,0},{2,3},{3,2},{4,5},{5,4},{6,7},{7,6},{8,9},{9,8},{10,11... | collective-permute-start | bytes 7077896 | tf_op jit(solution)/shard_map/ppermute | solution.py:31
  57.2 36.4 %collective-permute-start.4 = (f32[192,1024]{1,0:T(8,128)}, f32[192,1024]{1,0:T(8,128)}, u32[]{:S(2)}, u32[]{:S(2)}) collective-permute-start(f32[192,1024]{1,0:T(8,128)} %get-tuple-element.103), channel_id=1, source_target_pairs={{8,0},{16,8},{24,16},{9,1},{17,9},{25,17},{10,2},{18,10},{26,18},{... | collective-permute-start | bytes 2359304 | tf_op jit(solution)/shard_map/ppermute | solution.py:22
  61.4 35.2 %collective-permute-start.8 = (f32[192,1024]{1,0:T(8,128)}, f32[192,1024]{1,0:T(8,128)}, u32[]{:S(2)}, u32[]{:S(2)}) collective-permute-start(f32[192,1024]{1,0:T(8,128)} %get-tuple-element.119), channel_id=1, source_target_pairs={{16,0},{24,8},{17,1},{25,9},{18,2},{26,10},{19,3},{27,11},{20,4},{... | collective-permute-start | bytes 2359304 | tf_op jit(solution)/shard_map/ppermute | solution.py:22
  62.7 33.9 %collective-permute-start.9 = (f32[192,1024]{1,0:T(8,128)}, f32[192,1024]{1,0:T(8,128)}, u32[]{:S(2)}, u32[]{:S(2)}) collective-permute-start(f32[192,1024]{1,0:T(8,128)} %get-tuple-element.122), channel_id=1, source_target_pairs={{24,0},{25,1},{26,2},{27,3},{28,4},{29,5},{30,6},{31,7}} | collective-permute-start | bytes 2359304 | tf_op jit(solution)/shard_map/ppermute | solution.py:22
  67.8 37.4 %collective-permute-start = (f32[768,1024]{1,0:T(8,128)}, f32[768,1024]{1,0:T(8,128)S(1)}, u32[]{:S(2)}, u32[]{:S(2)}) collective-permute-start(f32[768,1024]{1,0:T(8,128)} %cut.2), channel_id=1, source_target_pairs={{0,1},{1,0},{2,3},{3,2},{4,5},{5,4},{6,7},{7,6},{8,9},{9,8},{10,11... | collective-permute-start | bytes 9437192 | tf_op jit(solution)/shard_map/ppermute | solution.py:31
  93.6 10.8 %copy-start.15 = (f32[1,768]{1,0:T(1,128)S(1)}, f32[1,768]{1,0:T(1,128)}, u32[]{:S(2)}) copy-start(f32[1,768]{1,0:T(1,128)} %param.6) | copy-start | bytes 9220
  99.3 23.7 %collective-permute-start.10 = (f32[576,1024]{1,0:T(8,128)}, f32[576,1024]{1,0:T(8,128)}, u32[]{:S(2)}, u32[]{:S(2)}) collective-permute-start(f32[576,1024]{1,0:T(8,128)} %stack.15), channel_id=1, source_target_pairs={{0,1},{1,0},{2,3},{3,2},{4,5},{5,4},{6,7},{7,6},{8,9},{9,8},{10,11... | collective-permute-start | bytes 7077896 | tf_op jit(solution)/shard_map/ppermute | solution.py:31
  99.8 23.2 %collective-permute-start.7 = (f32[192,1024]{1,0:T(8,128)}, f32[192,1024]{1,0:T(8,128)}, u32[]{:S(2)}, u32[]{:S(2)}) collective-permute-start(f32[192,1024]{1,0:T(8,128)} %get-tuple-element.115), channel_id=1, source_target_pairs={{0,24},{8,0},{16,8},{24,16},{1,25},{9,1},{17,9},{25,17},{2,26},{10... | collective-permute-start | bytes 2359304 | tf_op jit(solution)/shard_map/ppermute | solution.py:27
  102.5 36.7 %collective-permute-start.12 = (f32[192,1024]{1,0:T(8,128)}, f32[192,1024]{1,0:T(8,128)}, u32[]{:S(2)}, u32[]{:S(2)}) collective-permute-start(f32[192,1024]{1,0:T(8,128)} %get-tuple-element.130), channel_id=1, source_target_pairs={{0,16},{8,24},{16,0},{24,8},{1,17},{9,25},{17,1},{25,9},{2,18},{10... | collective-permute-start | bytes 2359304 | tf_op jit(solution)/shard_map/ppermute | solution.py:27
  102.5 36.7 %collective-permute-start.14 = (f32[192,1024]{1,0:T(8,128)}, f32[192,1024]{1,0:T(8,128)}, u32[]{:S(2)}, u32[]{:S(2)}) collective-permute-start(f32[192,1024]{1,0:T(8,128)} %get-tuple-element.133), channel_id=1, source_target_pairs={{0,8},{8,16},{16,24},{24,0},{1,9},{9,17},{17,25},{25,1},{2,10},{10... | collective-permute-start | bytes 2359304 | tf_op jit(solution)/shard_map/ppermute | solution.py:27
  105.3 1.7 copy-start
  144.0 5.2 %collective-permute-start.16 = (f32[576,1024]{1,0:T(8,128)}, f32[576,1024]{1,0:T(8,128)S(1)}, u32[]{:S(2)}, u32[]{:S(2)}) collective-permute-start(f32[576,1024]{1,0:T(8,128)} %get-tuple-element.141), channel_id=1, source_target_pairs={{0,1},{1,0},{2,3},{3,2},{4,5},{5,4},{6,7},{7,6},{8,9},{9,8},{10,11... | collective-permute-start | bytes 7077896 | tf_op jit(solution)/shard_map/ppermute | solution.py:31
  144.7 19.4 %collective-permute-start.15 = (f32[192,1024]{1,0:T(8,128)}, f32[192,1024]{1,0:T(8,128)S(1)}, u32[]{:S(2)}, u32[]{:S(2)}) collective-permute-start(f32[192,1024]{1,0:T(8,128)} %get-tuple-element.135), channel_id=1, source_target_pairs={{0,8},{8,16},{16,24},{24,0},{1,9},{9,17},{17,25},{25,1},{2,10},{10... | collective-permute-start | bytes 2359304 | tf_op jit(solution)/shard_map/ppermute | solution.py:27
  146.4 36.0 %collective-permute-start.13 = (f32[192,1024]{1,0:T(8,128)}, f32[192,1024]{1,0:T(8,128)}, u32[]{:S(2)}, u32[]{:S(2)}) collective-permute-start(f32[192,1024]{1,0:T(8,128)} %get-tuple-element.132), channel_id=1, source_target_pairs={{0,16},{8,24},{16,0},{24,8},{1,17},{9,25},{17,1},{25,9},{2,18},{10... | collective-permute-start | bytes 2359304 | tf_op jit(solution)/shard_map/ppermute | solution.py:27
  146.4 36.0 %collective-permute-start.11 = (f32[192,1024]{1,0:T(8,128)}, f32[192,1024]{1,0:T(8,128)}, u32[]{:S(2)}, u32[]{:S(2)}) collective-permute-start(f32[192,1024]{1,0:T(8,128)} %get-tuple-element.129), channel_id=1, source_target_pairs={{0,24},{8,0},{16,8},{24,16},{1,25},{9,1},{17,9},{25,17},{2,26},{10... | collective-permute-start | bytes 2359304 | tf_op jit(solution)/shard_map/ppermute | solution.py:27
  146.7 94.9 %all-reduce.7.cloned.1.call-start = ((), (), s32[]{:S(2)}) async-start(), calls=%async_computation.1 | async-start | bytes 1572864 | tf_op jit(solution)/shard_map/psum | solution.py:520
  149.1 1.5 copy-start.2
  164.2 28.0 %copy-start.6 = (f32[192,1024]{1,0:T(8,128)}, f32[192,1024]{1,0:T(8,128)S(1)}, u32[]{:S(2)}) copy-start(f32[192,1024]{1,0:T(8,128)S(1)} %collective-permute-done.15.refs_2_.refs_7_) | copy-start | bytes 2359300
  197.7 5.8 %collective-permute-start.20 = (f32[576,1024]{1,0:T(8,128)}, f32[576,1024]{1,0:T(8,128)S(1)}, u32[]{:S(2)}, u32[]{:S(2)}) collective-permute-start(f32[576,1024]{1,0:T(8,128)} %get-tuple-element.150), channel_id=1, source_target_pairs={{0,1},{1,0},{2,3},{3,2},{4,5},{5,4},{6,7},{7,6},{8,9},{9,8},{10,11... | collective-permute-start | bytes 7077896 | tf_op jit(solution)/shard_map/ppermute | solution.py:31
  198.5 92.4 %all-reduce.9.cloned.1.call-start = ((), (), s32[]{:S(2)}) async-start(), calls=%async_computation.2 | async-start | bytes 1572864 | tf_op jit(solution)/shard_map/psum | solution.py:520
  198.6 43.0 %collective-permute-start.17 = (f32[192,1024]{1,0:T(8,128)}, f32[192,1024]{1,0:T(8,128)S(1)}, u32[]{:S(2)}, u32[]{:S(2)}) collective-permute-start(f32[192,1024]{1,0:T(8,128)} %get-tuple-element.145), channel_id=1, source_target_pairs={{0,24},{8,0},{16,8},{24,16},{1,25},{9,1},{17,9},{25,17},{2,26},{10... | collective-permute-start | bytes 2359304 | tf_op jit(solution)/shard_map/ppermute | solution.py:27
  198.9 42.6 %collective-permute-start.18 = (f32[192,1024]{1,0:T(8,128)}, f32[192,1024]{1,0:T(8,128)}, u32[]{:S(2)}, u32[]{:S(2)}) collective-permute-start(f32[192,1024]{1,0:T(8,128)} %get-tuple-element.146), channel_id=1, source_target_pairs={{0,16},{8,24},{16,0},{24,8},{1,17},{9,25},{17,1},{25,9},{2,18},{10... | collective-permute-start | bytes 2359304 | tf_op jit(solution)/shard_map/ppermute | solution.py:27
  200.5 41.1 %collective-permute-start.19 = (f32[192,1024]{1,0:T(8,128)}, f32[192,1024]{1,0:T(8,128)}, u32[]{:S(2)}, u32[]{:S(2)}) collective-permute-start(f32[192,1024]{1,0:T(8,128)} %get-tuple-element.147), channel_id=1, source_target_pairs={{0,8},{8,16},{16,24},{24,0},{1,9},{9,17},{17,25},{25,1},{2,10},{10... | collective-permute-start | bytes 2359304 | tf_op jit(solution)/shard_map/ppermute | solution.py:27
  203.4 1.4 copy-start.1
  247.5 92.0 %all-reduce.11.cloned.1.call-start = ((), (), s32[]{:S(2)}) async-start(), calls=%async_computation.3 | async-start | bytes 1572864 | tf_op jit(solution)/shard_map/psum | solution.py:520
  247.6 43.4 %collective-permute-start.23 = (f32[192,1024]{1,0:T(8,128)}, f32[192,1024]{1,0:T(8,128)S(1)}, u32[]{:S(2)}, u32[]{:S(2)}) collective-permute-start(f32[192,1024]{1,0:T(8,128)} %get-tuple-element.163), channel_id=1, source_target_pairs={{0,8},{8,16},{16,24},{24,0},{1,9},{9,17},{17,25},{25,1},{2,10},{10... | collective-permute-start | bytes 2359304 | tf_op jit(solution)/shard_map/ppermute | solution.py:27
  248.9 42.0 %collective-permute-start.22 = (f32[192,1024]{1,0:T(8,128)}, f32[192,1024]{1,0:T(8,128)S(1)}, u32[]{:S(2)}, u32[]{:S(2)}) collective-permute-start(f32[192,1024]{1,0:T(8,128)} %get-tuple-element.161), channel_id=1, source_target_pairs={{0,16},{8,24},{16,0},{24,8},{1,17},{9,25},{17,1},{25,9},{2,18},{10... | collective-permute-start | bytes 2359304 | tf_op jit(solution)/shard_map/ppermute | solution.py:27
  249.2 41.8 %collective-permute-start.21 = (f32[192,1024]{1,0:T(8,128)}, f32[192,1024]{1,0:T(8,128)S(1)}, u32[]{:S(2)}, u32[]{:S(2)}) collective-permute-start(f32[192,1024]{1,0:T(8,128)} %get-tuple-element.154), channel_id=1, source_target_pairs={{0,24},{8,0},{16,8},{24,16},{1,25},{9,1},{17,9},{25,17},{2,26},{10... | collective-permute-start | bytes 2359304 | tf_op jit(solution)/shard_map/ppermute | solution.py:27
  290.9 5.4 %copy-start.14 = (f32[192,1024]{1,0:T(8,128)S(1)}, f32[192,1024]{1,0:T(8,128)}, u32[]{:S(2)}) copy-start(f32[192,1024]{1,0:T(8,128)} %all-reduce.9.cloned.1.call-done.refs_0_) | copy-start | bytes 2359300
  291.0 1.2 copy-start.12
  291.0 1.4 copy-start.13
  296.4 43.1 %collective-permute-start.24 = (f32[192,1024]{1,0:T(8,128)S(1)}, f32[192,1024]{1,0:T(8,128)}, u32[]{:S(2)}, u32[]{:S(2)}) collective-permute-start(f32[192,1024]{1,0:T(8,128)S(1)} %copy-done.14), channel_id=1, source_target_pairs={{8,0},{16,8},{24,16},{9,1},{17,9},{25,17},{10,2},{18,10},{26,18},{... | collective-permute-start | bytes 2359304 | tf_op jit(solution)/shard_map/ppermute | solution.py:22
  298.6 43.1 %collective-permute-start.26 = (f32[192,1024]{1,0:T(8,128)S(1)}, f32[192,1024]{1,0:T(8,128)}, u32[]{:S(2)}, u32[]{:S(2)}) collective-permute-start(f32[192,1024]{1,0:T(8,128)S(1)} %copy-done.14), channel_id=1, source_target_pairs={{16,0},{24,8},{17,1},{25,9},{18,2},{26,10},{19,3},{27,11},{20,4},{... | collective-permute-start | bytes 2359304 | tf_op jit(solution)/shard_map/ppermute | solution.py:22
  299.9 43.1 %collective-permute-start.28 = (f32[192,1024]{1,0:T(8,128)S(1)}, f32[192,1024]{1,0:T(8,128)}, u32[]{:S(2)}, u32[]{:S(2)}) collective-permute-start(f32[192,1024]{1,0:T(8,128)S(1)} %copy-done.14), channel_id=1, source_target_pairs={{24,0},{25,1},{26,2},{27,3},{28,4},{29,5},{30,6},{31,7}} | collective-permute-start | bytes 2359304 | tf_op jit(solution)/shard_map/ppermute | solution.py:22
  339.5 21.4 %collective-permute-start.25 = (f32[192,1024]{1,0:T(8,128)}, f32[192,1024]{1,0:T(8,128)S(1)}, u32[]{:S(2)}, u32[]{:S(2)}) collective-permute-start(f32[192,1024]{1,0:T(8,128)} %all-reduce.11.cloned.1.call-done.refs_0_), channel_id=1, source_target_pairs={{8,0},{16,8},{24,16},{9,1},{17,9},{25,17},{10,2},{18,10},{26,18},{... | collective-permute-start | bytes 2359304 | tf_op jit(solution)/shard_map/ppermute | solution.py:22
  341.7 37.1 %collective-permute-start.27 = (f32[192,1024]{1,0:T(8,128)}, f32[192,1024]{1,0:T(8,128)S(1)}, u32[]{:S(2)}, u32[]{:S(2)}) collective-permute-start(f32[192,1024]{1,0:T(8,128)} %all-reduce.11.cloned.1.call-done.refs_0_), channel_id=1, source_target_pairs={{16,0},{24,8},{17,1},{25,9},{18,2},{26,10},{19,3},{27,11},{20,4},{... | collective-permute-start | bytes 2359304 | tf_op jit(solution)/shard_map/ppermute | solution.py:22
  343.1 35.8 %collective-permute-start.29 = (f32[192,1024]{1,0:T(8,128)}, f32[192,1024]{1,0:T(8,128)S(1)}, u32[]{:S(2)}, u32[]{:S(2)}) collective-permute-start(f32[192,1024]{1,0:T(8,128)} %all-reduce.11.cloned.1.call-done.refs_0_), channel_id=1, source_target_pairs={{24,0},{25,1},{26,2},{27,3},{28,4},{29,5},{30,6},{31,7}} | collective-permute-start | bytes 2359304 | tf_op jit(solution)/shard_map/ppermute | solution.py:22
  360.9 18.0 %copy-start.7 = (f32[192,1024]{1,0:T(8,128)}, f32[192,1024]{1,0:T(8,128)S(1)}, u32[]{:S(2)}) copy-start(f32[192,1024]{1,0:T(8,128)S(1)} %collective-permute-done.25.refs_1_) | copy-start | bytes 2359300
  378.9 1.2 copy-start.9
  391.1 11.6 %collective-permute-start.30 = (f32[1024,1024]{1,0:T(8,128)}, f32[1024,1024]{1,0:T(8,128)}, u32[]{:S(2)}, u32[]{:S(2)}) collective-permute-start(f32[1024,1024]{1,0:T(8,128)} %adjoint.8), channel_id=1, source_target_pairs={{0,1},{1,0},{2,3},{3,2},{4,5},{5,4},{6,7},{7,6},{8,9},{9,8},{10,11... | collective-permute-start | bytes 12582920 | tf_op jit(solution)/shard_map/ppermute | solution.py:31
  (3 other events, 2.8 us)
Sparse Core Ops, SparseCore 0:
  146.8 45.2 all-reduce.4
  198.7 42.8 all-reduce.6
  247.7 43.2 all-reduce.8
  296.5 42.9 all-reduce.10
